TPU v7x, 32 devices: a whole 2x2x4 slice. The times are simulated.
32 devices in a mesh: grp: 2 (over x), run: 8 (over z, y), sub: 2 (over core).
Axes of the slice: x: 2, y: 2, z: 4, core: 2. Of those that a mesh axis runs over, the one named last changes fastest.
Arguments:
- load_field: float32 [3, 128, 64, 128], P(None, ('grp', 'run'), 'sub'), parts along dimension 1, may hold values from -6 to 6
- initial_guess: float32 [3, 128, 64, 128], P(None, ('grp', 'run'), 'sub'), parts along dimension 1, may hold values from -4 to 4
- occupancy: int32 [128, 64, 128], P(('grp', 'run'), 'sub'), parts along dimension 0, may hold values from 0 to 1, as said below
- density: float32 [128, 64, 128], P(('grp', 'run'), 'sub'), parts along dimension 0, may hold values from 0.3 to 1
Outputs:
- displacement: float32 [3, 128, 64, 128], P(None, ('grp', 'run'), 'sub'), parts along dimension 1
- new_density: float32 [128, 64, 128], P(('grp', 'run'), 'sub'), parts along dimension 0
There are 2 independent parts, one for each index of `grp`. A program takes and returns all parts, laid end to end along the dimension named above; each array names one. Nothing has to cross between parts.
Inputs may be any that keep to these rules, and one draw needn't show every extreme that they name: `occupancy`: 1 marks a bone voxel, 0 marrow; every part has bone voxels.
All inputs are finite; a program needn't handle non-finite values.
Results may differ from a plain program's by a relative error of at most 0.0018.
Values sent between devices are 32-bit elements; how exact they have to be, the bound alone decides.
No kernel may reach another device: no remote copies, remote signals or barrier semaphores. Data moves between devices by JAX's collectives and lax.ppermute only.
A program may use at most 64 MiB of HBM per device.

v0:
```python
import functools
import math

import jax
import jax.numpy as jnp
from jax import lax
from jax.experimental import pallas as pl
from jax.experimental.pallas import tpu as pltpu
from jax.sharding import PartitionSpec as P

REACH = 32
POISSON = 0.3
MARROW = 0.05
RATE = 0.5
SLOPE = 4.0
DECAY = REACH / 4.0

LAME = POISSON / ((1.0 + POISSON) * (1.0 - 2.0 * POISSON)) / 16.0
SHEAR = 0.5 / (1.0 + POISSON) / 16.0
ENTRY = 16.0 * (LAME + 4.0 * SHEAR) / 9.0
NORM = 1.0 / sum(math.exp(-abs(k) / DECAY) for k in range(-REACH, REACH + 1))

DEEP = 3
WIN = 13
ROWS = 40
SLOT_LO = 17
SLOT_HI = 11
SIDE = 39 + 33 + 12
PAIR = ("run", "sub")

VMEM = pl.BlockSpec(memory_space=pltpu.VMEM)


def weight(distance):
    return NORM * math.exp(-distance / DECAY)


def call(kernel, outs, ins, scratch=()):
    return pl.pallas_call(
        kernel,
        out_shape=[jax.ShapeDtypeStruct(s, jnp.float32) for s in outs],
        in_specs=[VMEM] * len(ins),
        out_specs=[VMEM] * len(outs),
        scratch_shapes=[pltpu.VMEM(s, jnp.float32) for s in scratch],
        compiler_params=pltpu.CompilerParams(vmem_limit_bytes=40 * 1024 * 1024),
    )(*ins)


def lane_right(block):
    lane = lax.broadcasted_iota(jnp.int32, block.shape, 1)
    return jnp.where(lane == 0, 0.0, pltpu.roll(block, 1, 1))


def lane_left(block):
    lane = lax.broadcasted_iota(jnp.int32, block.shape, 1)
    return jnp.where(lane == block.shape[1] - 1, 0.0, pltpu.roll(block, block.shape[1] - 1, 1))


def row_up(block):
    row = lax.broadcasted_iota(jnp.int32, block.shape, 0)
    return jnp.where(row == 0, 0.0, pltpu.roll(block, 1, 0))


def row_down(block):
    row = lax.broadcasted_iota(jnp.int32, block.shape, 0)
    return jnp.where(row == block.shape[0] - 1, 0.0, pltpu.roll(block, block.shape[0] - 1, 0))


def faces(block):
    other = lane_right(block)
    total, change = block + other, block - other
    a, b = row_up(total), row_up(change)
    return total + a, change + b, total - a, change - b


def unfaces(modes):
    columns = []
    for x in range(2):
        total, change = modes[x], modes[2 + x]
        columns.append(total + change + row_down(total - change))
    return columns[0] + columns[1] + lane_left(columns[0] - columns[1])


def modes_of(low, high):
    out = []
    for c in range(3):
        modes = [None] * 8
        for m in range(4):
            if m:
                modes[m] = high[4 * c + m] + low[4 * c + m]
            modes[4 + m] = high[4 * c + m] - low[4 * c + m]
        out.append(modes)
    return out


X, Y, Z = 1, 2, 4


def stress(u, mod):
    g = [[None] * 8 for _ in range(3)]
    bulk, rigid = mod * LAME, mod * SHEAR
    twice = rigid + rigid
    bulk3, rigid3 = mod * (LAME / 3.0), mod * (SHEAR / 3.0)
    last = mod * ((LAME + 4.0 * SHEAR) / 9.0)
    t = (u[0][X] + u[1][Y] + u[2][Z]) * bulk
    g[0][X] = t + u[0][X] * twice
    g[1][Y] = t + u[1][Y] * twice
    g[2][Z] = t + u[2][Z] * twice
    g[0][Y] = g[1][X] = (u[0][Y] + u[1][X]) * rigid
    g[0][Z] = g[2][X] = (u[0][Z] + u[2][X]) * rigid
    g[1][Z] = g[2][Y] = (u[1][Z] + u[2][Y]) * rigid
    for (c, m), (d, n) in (
        ((1, X | Y), (2, X | Z)),
        ((0, X | Y), (2, Y | Z)),
        ((0, X | Z), (1, Y | Z)),
    ):
        s = (u[c][m] + u[d][n]) * bulk3
        g[c][m] = s + u[c][m] * rigid
        g[d][n] = s + u[d][n] * rigid
    s = u[0][Y | Z] + u[1][X | Z] + u[2][X | Y]
    g[0][Y | Z] = (s + u[0][Y | Z]) * rigid3
    g[1][X | Z] = (s + u[1][X | Z]) * rigid3
    g[2][X | Y] = (s + u[2][X | Y]) * rigid3
    for c in range(3):
        g[c][7] = u[c][7] * last
    return g


def quadratic(u):
    def sq(v):
        return v * v

    t = sq(u[0][X] + u[1][Y] + u[2][Z])
    r2 = sq(u[0][X]) + sq(u[1][Y]) + sq(u[2][Z])
    r = sq(u[0][Y] + u[1][X]) + sq(u[0][Z] + u[2][X]) + sq(u[1][Z] + u[2][Y])
    t3 = 0.0
    for (c, m), (d, n) in (
        ((1, X | Y), (2, X | Z)),
        ((0, X | Y), (2, Y | Z)),
        ((0, X | Z), (1, Y | Z)),
    ):
        t3 = t3 + sq(u[c][m] + u[d][n])
        r = r + (sq(u[c][m]) + sq(u[d][n]))
    p, q, s = u[0][Y | Z], u[1][X | Z], u[2][X | Y]
    r3 = sq(p + q) + sq(p + s) + sq(q + s)
    last = sq(u[0][7]) + sq(u[1][7]) + sq(u[2][7])
    return (
        LAME * (t + t3 * (1.0 / 3.0))
        + SHEAR * (r + r2 + r2 + r3 * (1.0 / 3.0))
        + ((LAME + 4.0 * SHEAR) / 9.0) * last
    )


def pack_planes(load, guess, occupancy, density, modulus, up, down):
    modulus[...] = jnp.where(occupancy[...] == 1, density[...] * density[...], MARROW)
    for c in range(3):
        for k in range(3):
            up[3 * c + k] = guess[c, 5 + k]
        for k in range(2):
            up[9 + 2 * c + k] = load[c, 6 + k]
            down[2 * c + k] = guess[c, k]
        down[6 + c] = load[c, 0]
    for k in range(2):
        up[15 + k] = modulus[6 + k]
        down[9 + k] = modulus[k]


def pack_rows(load, guess, modulus, low, high, side):
    sub = lax.axis_index("sub")
    rows = pl.ds(pl.multiple_of(24 * (1 - sub), 8), 8)
    for c in range(3):
        for k in range(3):
            side[13 * c + k] = low[3 * c + k, rows]
        for k in range(8):
            side[13 * c + 3 + k] = guess[c, k, rows]
        for k in range(2):
            side[13 * c + 11 + k] = high[2 * c + k, rows]
        for k in range(2):
            side[39 + 11 * c + k] = low[9 + 2 * c + k, rows]
        for k in range(8):
            side[39 + 11 * c + 2 + k] = load[c, k, rows]
        side[39 + 11 * c + 10] = high[6 + c, rows]
    for k in range(2):
        side[72 + k] = low[15 + k, rows]
        side[72 + 10 + k] = high[9 + k, rows]
    for k in range(8):
        side[72 + 2 + k] = modulus[k, rows]


def krylov(
    load, guess, modulus, low, high, side, row_out, guess_w, first, second,
    load_w, mod_w, inverse, plane, total, carry, sums,
):
    sub = lax.axis_index("sub")
    run = lax.axis_index("run")
    own = pl.ds(pl.multiple_of(8 * sub, 8), 32)
    rest = pl.ds(pl.multiple_of(32 * (1 - sub), 8), 8)
    for c in range(3):
        for k in range(3):
            guess_w[c, k, own] = low[3 * c + k]
        for k in range(8):
            guess_w[c, 3 + k, own] = guess[c, k]
        for k in range(2):
            guess_w[c, 11 + k, own] = high[2 * c + k]
        for k in range(13):
            guess_w[c, k, rest] = side[13 * c + k]
        for k in range(2):
            load_w[c, k, own] = low[9 + 2 * c + k]
        for k in range(8):
            load_w[c, 2 + k, own] = load[c, k]
        load_w[c, 10, own] = high[6 + c]
        for k in range(11):
            load_w[c, k, rest] = side[39 + 11 * c + k]
    for k in range(2):
        mod_w[k, own] = low[15 + k]
        mod_w[10 + k, own] = high[9 + k]
    for k in range(8):
        mod_w[2 + k, own] = modulus[k]
    for k in range(12):
        mod_w[k, rest] = side[72 + k]

    def invert(k, _):
        t = mod_w[k] + mod_w[k + 1]
        t = t + row_down(t)
        t = (t + lane_left(t)) * ENTRY
        fine = (t > 0.0) & (run * 8 + k - 2 >= 0)
        inverse[k] = jnp.where(fine, 1.0 / jnp.where(fine, t, 1.0), 0.0)
        return 0

    lax.fori_loop(0, 11, invert, 0)

    sums[...] = jnp.zeros_like(sums)

    def enter(field, k, slot):
        for c in range(3):
            for m, value in enumerate(faces(field[c, k])):
                plane[slot, 4 * c + m] = value

    def voxels(k, mod_at):
        now, before = lax.rem(k, 2), lax.rem(k + 1, 2)
        for tile in range(ROWS // 8):
            rows = slice(8 * tile, 8 * tile + 8)
            high_m = [plane[now, m, rows] for m in range(12)]
            low_m = [plane[before, m, rows] for m in range(12)]
            g = stress(modes_of(low_m, high_m), mod_w[mod_at, rows])
            for c in range(3):
                for m in range(4):
                    d = g[c][4 + m]
                    at = 4 * c + m
                    if m:
                        s = g[c][m]
                        total[at, rows] = carry[at, rows] + (s - d)
                        carry[at, rows] = s + d
                    else:
                        total[at, rows] = carry[at, rows] - d
                        carry[at, rows] = d

    def image(c):
        return unfaces([total[4 * c + m] for m in range(4)])

    enter(guess_w, 0, 0)
    carry[...] = jnp.zeros_like(carry)

    def pass_one(k, _):
        enter(guess_w, k, lax.rem(k, 2))
        voxels(k, k - 1)

        @pl.when(k >= 2)
        def _():
            dot = 0.0
            for c in range(3):
                residual = load_w[c, k - 2] - image(c)
                z = residual * inverse[k - 2]
                first[c, k - 2] = z
                dot = dot + residual * z

            @pl.when((k >= 4) & (k < 12))
            def _():
                sums[0] += dot

        return 0

    lax.fori_loop(1, 13, pass_one, 0)

    enter(first, 0, 0)
    carry[...] = jnp.zeros_like(carry)

    def pass_two(k, _):
        enter(first, k, lax.rem(k, 2))
        voxels(k, k)

        @pl.when(k >= 2)
        def _():
            dot, cross = 0.0, 0.0
            for c in range(3):
                w = image(c)
                s = w * inverse[k - 1]
                second[c, k - 2] = s
                dot = dot + w * first[c, k - 1]
                cross = cross + w * s

            @pl.when(k >= 3)
            def _():
                sums[1] += dot
                sums[2] += cross

        return 0

    lax.fori_loop(1, 11, pass_two, 0)

    enter(second, 0, 0)

    def pass_three(k, _):
        enter(second, k, lax.rem(k, 2))
        now, before = lax.rem(k, 2), lax.rem(k + 1, 2)
        for tile in range(ROWS // 8):
            rows = slice(8 * tile, 8 * tile + 8)
            u = modes_of(
                [plane[before, m, rows] for m in range(12)],
                [plane[now, m, rows] for m in range(12)],
            )
            sums[3, rows] += quadratic(u) * mod_w[k + 1, rows]
        return 0

    lax.fori_loop(1, 9, pass_three, 0)

    lane = lax.broadcasted_iota(jnp.int32, (1, 128), 1)
    line = jnp.zeros((1, 128), jnp.float32)
    for k in range(4):
        value = jnp.sum(jnp.sum(sums[k, own], axis=0, keepdims=True), axis=1, keepdims=True)
        line = jnp.where(lane == k, value, line)
    row_out[...] = jnp.broadcast_to(line, row_out.shape)


def pick(line, k):
    lane = lax.broadcasted_iota(jnp.int32, line.shape, 1)
    return jnp.sum(jnp.where(lane == k, line, 0.0), axis=1, keepdims=True)


def energies(lines, guess_w, first, second, occupancy, density, out, smooth, plane, field, specific):
    sub = lax.axis_index("sub")
    own = pl.ds(pl.multiple_of(8 * sub, 8), 32)
    line = jnp.sum(lines[...], axis=0, keepdims=True)
    a, b, c, e = (pick(line, k) for k in range(4))
    alpha = a / b
    fresh = alpha * alpha * c - a
    beta = fresh / a
    square = alpha * alpha * e - (1.0 + beta) * (1.0 + beta) * b
    after = fresh / square
    p = jnp.broadcast_to(alpha + after * (1.0 + beta), (ROWS, 128))
    q = jnp.broadcast_to(-after * alpha, (ROWS, 128))

    def enter(k, slot):
        for c in range(3):
            value = guess_w[c, k + 2] + p * first[c, k + 1] + q * second[c, k]
            field[c] = value
            for m, mode in enumerate(faces(value)):
                plane[slot, 4 * c + m] = mode

    enter(0, 0)

    def body(k, _):
        now, before = lax.rem(k, 2), lax.rem(k + 1, 2)
        enter(k, now)
        for c in range(3):
            out[c, k - 1] = field[c, own]
        for tile in range(4):
            rows = pl.ds(pl.multiple_of(8 * sub + 8 * tile, 8), 8)
            here = slice(8 * tile, 8 * tile + 8)
            u = modes_of(
                [plane[before, m, rows] for m in range(12)],
                [plane[now, m, rows] for m in range(12)],
            )
            rho = density[k - 1, here]
            bone = occupancy[k - 1, here] == 1
            share = jnp.where(bone, rho * rho / rho, 0.0)
            specific[pl.ds(pl.multiple_of(32 * (k - 1) + 8 * tile, 8), 8), :] = (
                0.5 * share * quadratic(u)
            )
        return 0

    lax.fori_loop(1, 9, body, 0)
    row = lax.broadcasted_iota(jnp.int32, (128, 128), 0)
    col = lax.broadcasted_iota(jnp.int32, (128, 128), 1)
    gap = jnp.abs(row - col).astype(jnp.float32)
    band = jnp.where(gap <= REACH, NORM * jnp.exp(gap * (-1.0 / DECAY)), 0.0)
    smooth[...] = jnp.dot(
        specific[...], band, precision=lax.Precision.HIGHEST, preferred_element_type=jnp.float32
    ).reshape(smooth.shape)


def along_y(mine, other, out, planes):
    sub = lax.axis_index("sub")
    run = lax.axis_index("run")
    row = lax.broadcasted_iota(jnp.int32, (32, 32), 0)
    col = lax.broadcasted_iota(jnp.int32, (32, 32), 1)

    def band(offset):
        gap = jnp.abs(col + offset - row).astype(jnp.float32)
        return jnp.where(gap <= REACH, NORM * jnp.exp(gap * (-1.0 / DECAY)), 0.0)

    near = band(0)
    far = band(32 - 64 * sub)
    upward, downward = 0.0, 0.0
    for k in range(8):
        value = jnp.dot(
            near, mine[k], precision=lax.Precision.HIGHEST, preferred_element_type=jnp.float32
        ) + jnp.dot(
            far, other[k], precision=lax.Precision.HIGHEST, preferred_element_type=jnp.float32
        )
        out[k] = value
        upward = upward + math.exp(-(7 - k) / DECAY) * value
        downward = downward + math.exp(-k / DECAY) * value
    for k in range(planes.shape[0]):
        planes[k] = jnp.where(k > run, upward, downward)


def along_z(count, mine, planes, below, above, occupancy, stimulus, row_out):
    run = lax.axis_index("run")
    span = REACH // 8
    lower, upper = 0.0, 0.0
    for o in range(1, span):
        scale = math.exp(-8.0 * (o - 1) / DECAY)
        at = jnp.maximum(run - o, 0)
        lower = lower + jnp.where(run - o >= 0, scale * planes[at], 0.0)
        at = jnp.minimum(run + o, count - 1)
        upper = upper + jnp.where(run + o < count, scale * planes[at], 0.0)
    has_below = run - span >= 0
    has_above = run + span < count
    total, bone = 0.0, 0.0
    for i in range(8):
        value = weight(i + 1) * lower + weight(8 - i) * upper
        far_below, far_above = 0.0, 0.0
        for j in range(8):
            value = value + weight(abs(i - j)) * mine[j]
            if j >= i:
                far_below = far_below + weight(i - j + REACH) * below[j]
            if j <= i:
                far_above = far_above + weight(j - i + REACH) * above[j]
        value = value + jnp.where(has_below, far_below, 0.0) + jnp.where(has_above, far_above, 0.0)
        stimulus[i] = value
        share = occupancy[i].astype(jnp.float32)
        total = total + share * value
        bone = bone + share
    lane = lax.broadcasted_iota(jnp.int32, (1, 128), 1)

    def whole(block):
        return jnp.sum(jnp.sum(block, axis=0, keepdims=True), axis=1, keepdims=True)

    line = jnp.where(lane == 0, whole(total), jnp.where(lane == 1, whole(bone), 0.0))
    row_out[...] = jnp.broadcast_to(line, row_out.shape)


def remodel(lines, stimulus, occupancy, density, out):
    line = jnp.sum(lines[...], axis=0, keepdims=True)
    mean = jnp.broadcast_to(pick(line, 0) / pick(line, 1), stimulus.shape[1:])
    for k in range(8):
        rho = density[k]
        updated = jnp.minimum(rho * (1.0 + RATE * jnp.tanh(SLOPE * (stimulus[k] / mean - 1.0))), 1.0)
        out[k] = jnp.where(occupancy[k] == 1, updated, rho)


def everyone(lines):
    return lax.all_to_all(lines, PAIR, 0, 0, tiled=True)


def local(load, guess, occupancy, density):
    count = lax.axis_size("run")
    members = count * lax.axis_size("sub")
    block = density.shape
    modulus, up, down = call(
        pack_planes,
        [block, (SLOT_LO, 32, 128), (SLOT_HI, 32, 128)],
        [load, guess, occupancy, density],
    )
    low = lax.ppermute(up, "run", [(i, i + 1) for i in range(count - 1)])
    high = lax.ppermute(down, "run", [(i + 1, i) for i in range(count - 1)])
    (side,) = call(pack_rows, [(SIDE, 8, 128)], [load, guess, modulus, low, high])
    swap = [(0, 1), (1, 0)]
    side = lax.ppermute(side, "sub", swap)
    lines, guess_w, first, second = call(
        krylov,
        [(members, 128), (3, 13, ROWS, 128), (3, 11, ROWS, 128), (3, 9, ROWS, 128)],
        [load, guess, modulus, low, high, side],
        [
            (3, 11, ROWS, 128), (12, ROWS, 128), (11, ROWS, 128),
            (2, 12, ROWS, 128), (12, ROWS, 128), (12, ROWS, 128), (4, ROWS, 128),
        ],
    )
    lines = everyone(lines)
    displacement, smooth = call(
        energies,
        [guess.shape, block],
        [lines, guess_w, first, second, occupancy, density],
        [(2, 12, ROWS, 128), (3, ROWS, 128), (256, 128)],
    )
    other = lax.ppermute(smooth, "sub", swap)
    smooth, planes = call(along_y, [block, (count, 32, 128)], [smooth, other])
    span = REACH // 8
    rise = [(i, i + span) for i in range(count - span)]
    fall = [(i + span, i) for i in range(count - span)]
    if count <= 2 * span:
        below = above = lax.ppermute(smooth, "run", rise + fall)
    else:
        below = lax.ppermute(smooth, "run", rise)
        above = lax.ppermute(smooth, "run", fall)
    planes = lax.all_to_all(planes, "run", 0, 0, tiled=True)
    stimulus, lines = call(
        functools.partial(along_z, count),
        [block, (members, 128)],
        [smooth, planes, below, above, occupancy],
    )
    lines = everyone(lines)
    (new_density,) = call(remodel, [block], [lines, stimulus, occupancy, density])
    return displacement, new_density


def solution(mesh):
    field = P(None, ("grp", "run"), "sub", None)
    cells = P(("grp", "run"), "sub", None)
    return jax.shard_map(
        local,
        mesh=mesh,
        in_specs=(field, field, cells, cells),
        out_specs=(field, cells),
        check_vma=False,
    )
```

profile of v0, /device:TPU:0, one launch (start us, length us, event | category | flops | bytes accessed | tf_op | source)
XLA Modules:
  0.0 74.4 jit_solution(16709504268693324866)
XLA Ops:
  0.6 0.0 copy-start
  0.6 1.0 %copy-done = f32[3,8,32,128]{3,2,1,0:T(8,128)S(1)} copy-done((f32[3,8,32,128]{3,2,1,0:T(8,128)S(1)}, f32[3,8,32,128]{3,2,1,0:T(8,128)}, u32[]{:S(2)}) %copy-start) | copy-done | bytes 393240
  1.6 0.0 copy-start.1
  1.6 1.0 %copy-done.1 = f32[3,8,32,128]{3,2,1,0:T(8,128)S(1)} copy-done((f32[3,8,32,128]{3,2,1,0:T(8,128)S(1)}, f32[3,8,32,128]{3,2,1,0:T(8,128)}, u32[]{:S(2)}) %copy-start.1) | copy-done | bytes 393240
  2.6 0.0 copy-start.2
  2.6 0.9 %copy-done.2 = s32[8,32,128]{2,1,0:T(8,128)S(1)} copy-done((s32[8,32,128]{2,1,0:T(8,128)S(1)}, s32[8,32,128]{2,1,0:T(8,128)}, u32[]{:S(2)}) %copy-start.2) | copy-done | bytes 131096
  3.5 0.0 copy-start.4
  3.5 0.9 %copy-done.4 = f32[8,32,128]{2,1,0:T(8,128)S(1)} copy-done((f32[8,32,128]{2,1,0:T(8,128)S(1)}, f32[8,32,128]{2,1,0:T(8,128)}, u32[]{:S(2)}) %copy-start.4) | copy-done | bytes 131096
  4.5 4.9 %collective-permute-start = (f32[17,32,128]{2,1,0:T(8,128)S(1)}, f32[17,32,128]{2,1,0:T(8,128)S(1)}, u32[]{:S(2)}, u32[]{:S(2)}) collective-permute-start(f32[17,32,128]{2,1,0:T(8,128)S(1)} %get-tuple-element.16), channel_id=1, source_target_pairs={{0,2},{2,4},{4,6},{6,8},{8,10},{10,12},{12,14},{1,3},{3,5},{5,7},{... | collective-permute-start | bytes 835592 | tf_op jit(solution)/shard_map/ppermute | solution.py:476
  9.4 1.3 %collective-permute-start.1 = (f32[11,32,128]{2,1,0:T(8,128)S(1)}, f32[11,32,128]{2,1,0:T(8,128)S(1)}, u32[]{:S(2)}, u32[]{:S(2)}) collective-permute-start(f32[11,32,128]{2,1,0:T(8,128)S(1)} %get-tuple-element.17), channel_id=1, source_target_pairs={{2,0},{4,2},{6,4},{8,6},{10,8},{12,10},{14,12},{3,1},{5,3},{7,5},{... | collective-permute-start | bytes 540680 | tf_op jit(solution)/shard_map/ppermute | solution.py:477
  10.7 6.6 %collective-permute-done.1.high = f32[11,32,128]{2,1,0:T(8,128)S(1)} collective-permute-done((f32[11,32,128]{2,1,0:T(8,128)S(1)}, f32[11,32,128]{2,1,0:T(8,128)S(1)}, u32[]{:S(2)}, u32[]{:S(2)}) %collective-permute-start.1) | collective-permute-done | bytes 180256 | tf_op jit(solution)/shard_map/ppermute | solution.py:477
  17.3 1.8 %collective-permute-done.low = f32[17,32,128]{2,1,0:T(8,128)S(1)} collective-permute-done((f32[17,32,128]{2,1,0:T(8,128)S(1)}, f32[17,32,128]{2,1,0:T(8,128)S(1)}, u32[]{:S(2)}, u32[]{:S(2)}) %collective-permute-start) | collective-permute-done | bytes 278560 | tf_op jit(solution)/shard_map/ppermute | solution.py:476
  19.2 0.0 copy-start.3
  19.2 0.0 copy-start.5
  19.2 0.1 collective-permute-start.2
  19.3 1.6 %collective-permute-done.2.side = f32[84,8,128]{2,1,0:T(8,128)S(1)} collective-permute-done((f32[84,8,128]{2,1,0:T(8,128)S(1)}, f32[84,8,128]{2,1,0:T(8,128)S(1)}, u32[]{:S(2)}, u32[]{:S(2)}) %collective-permute-start.2) | collective-permute-done | bytes 344096 | tf_op jit(solution)/shard_map/ppermute | solution.py:480
  20.9 9.3 %shard_map.61 = (f32[16,128]{1,0:T(8,128)S(1)}, f32[3,13,40,128]{3,2,1,0:T(8,128)S(1)}, f32[3,11,40,128]{3,2,1,0:T(8,128)S(1)}, f32[3,9,40,128]{3,2,1,0:T(8,128)S(1)}) custom-call(f32[3,8,32,128]{3,2,1,0:T(8,128)S(1)} %copy-done, f32[3,8,32,128]{3,2,1,0:T(8,128)S(1)} %copy-done.1, f32[8,32,128]{2,1,0:T(8,128)S(1)} %get-tuple-element.15.modulus, ...), custom_call_target="tpu_custom_call" | custom-call | tf_op jit(solution)/shard_map/pallas_call | solution.py:39
  30.2 13.0 %all_to_all.27 = f32[16,1,128]{2,1,0:T(1,128)S(1)} all-to-all(f32[16,1,128]{2,1,0:T(1,128)S(1)} %bitcast.10), channel_id=1, replica_groups=mesh['grp'=2,'run'=8,'sub'=2] {'run','sub'}, dimensions={0} | all-to-all | bytes 16384 | tf_op jit(solution)/shard_map/all_to_all | solution.py:464
  43.3 0.0 copy-done.3
  43.3 0.0 copy-done.5
  43.3 2.1 %shard_map.62 = (f32[3,8,32,128]{3,2,1,0:T(8,128)}, f32[8,32,128]{2,1,0:T(8,128)S(1)}) custom-call(f32[16,128]{1,0:T(8,128)S(1)} %bitcast.8, f32[3,13,40,128]{3,2,1,0:T(8,128)S(1)} %get-tuple-element.19.guess_w, f32[3,11,40,128]{3,2,1,0:T(8,128)S(1)} %get-tuple-element.20.first, f32[3,9,40,128]{3,2,1,0:T(8,128)S(1)} %get-tuple-element.21.second, ...), custom_call_target="tpu_custom_call" | custom-call | tf_op jit(solution)/shard_map/pallas_call | solution.py:39
  45.4 0.0 collective-permute-start.3
  45.4 1.3 %collective-permute-done.3.other = f32[8,32,128]{2,1,0:T(8,128)S(1)} collective-permute-done((f32[8,32,128]{2,1,0:T(8,128)S(1)}, f32[8,32,128]{2,1,0:T(8,128)S(1)}, u32[]{:S(2)}, u32[]{:S(2)}) %collective-permute-start.3) | collective-permute-done | bytes 131104 | tf_op jit(solution)/shard_map/ppermute | solution.py:497
  46.7 1.1 %shard_map.63 = (f32[8,32,128]{2,1,0:T(8,128)S(1)}, f32[8,32,128]{2,1,0:T(8,128)}) custom-call(f32[8,32,128]{2,1,0:T(8,128)S(1)} %get-tuple-element.23.mine, f32[8,32,128]{2,1,0:T(8,128)S(1)} %collective-permute-done.3.other), custom_call_target="tpu_custom_call" | custom-call | tf_op jit(solution)/shard_map/pallas_call | solution.py:39
  47.8 3.4 %all-to-all-start.1 = ((f32[8,32,128]{2,1,0:T(8,128)}), f32[8,32,128]{2,1,0:T(8,128)S(1)}, u32[]{:S(2)}, u32[]{:S(2)}) async-start(f32[8,32,128]{2,1,0:T(8,128)} %get-tuple-element.25), calls=%async_computation.1 | async-start | bytes 262144 | tf_op jit(solution)/shard_map/all_to_all | solution.py:507
  51.2 2.8 %collective-permute-start.4 = (f32[8,32,128]{2,1,0:T(8,128)S(1)}, f32[8,32,128]{2,1,0:T(8,128)S(1)}, u32[]{:S(2)}, u32[]{:S(2)}) collective-permute-start(f32[8,32,128]{2,1,0:T(8,128)S(1)} %get-tuple-element.24.mine), channel_id=1, source_target_pairs={{0,8},{2,10},{4,12},{6,14},{8,0},{10,2},{12,4},{14,6},{1,9},{3,11}... | collective-permute-start | bytes 393224 | tf_op jit(solution)/shard_map/ppermute | solution.py:503
  54.0 9.3 %collective-permute-done.4.below.above = f32[8,32,128]{2,1,0:T(8,128)S(1)} collective-permute-done((f32[8,32,128]{2,1,0:T(8,128)S(1)}, f32[8,32,128]{2,1,0:T(8,128)S(1)}, u32[]{:S(2)}, u32[]{:S(2)}) %collective-permute-start.4) | collective-permute-done | bytes 131104 | tf_op jit(solution)/shard_map/ppermute | solution.py:503
  63.4 0.0 all-to-all-done.1.planes
  63.4 0.3 shard_map.64
  63.7 9.9 %all_to_all.28 = f32[16,1,128]{2,1,0:T(1,128)S(1)} all-to-all(f32[16,1,128]{2,1,0:T(1,128)S(1)} %bitcast.11), channel_id=1, replica_groups=mesh['grp'=2,'run'=8,'sub'=2] {'run','sub'}, dimensions={0} | all-to-all | bytes 16384 | tf_op jit(solution)/shard_map/all_to_all | solution.py:464
  73.6 0.8 %shard_map.65 = f32[8,32,128]{2,1,0:T(8,128)} custom-call(f32[16,128]{1,0:T(8,128)S(1)} %bitcast.9, f32[8,32,128]{2,1,0:T(8,128)S(1)} %get-tuple-element.27.stimulus, s32[8,32,128]{2,1,0:T(8,128)S(1)} %copy-done.3, f32[8,32,128]{2,1,0:T(8,128)S(1)} %copy-done.5), custom_call_target="tpu_custom_call" | custom-call | tf_op jit(solution)/shard_map/pallas_call | solution.py:39
  (2 shorter events, 0.1 us)
Async XLA Ops:
  0.6 1.0 %copy-start = (f32[3,8,32,128]{3,2,1,0:T(8,128)S(1)}, f32[3,8,32,128]{3,2,1,0:T(8,128)}, u32[]{:S(2)}) copy-start(f32[3,8,32,128]{3,2,1,0:T(8,128)} %load.5) | copy-start | bytes 1179652
  1.6 1.0 %copy-start.1 = (f32[3,8,32,128]{3,2,1,0:T(8,128)S(1)}, f32[3,8,32,128]{3,2,1,0:T(8,128)}, u32[]{:S(2)}) copy-start(f32[3,8,32,128]{3,2,1,0:T(8,128)} %guess.5) | copy-start | bytes 1179652
  2.6 0.9 %copy-start.2 = (s32[8,32,128]{2,1,0:T(8,128)S(1)}, s32[8,32,128]{2,1,0:T(8,128)}, u32[]{:S(2)}) copy-start(s32[8,32,128]{2,1,0:T(8,128)} %occupancy.7) | copy-start | bytes 393220
  3.5 0.9 %copy-start.4 = (f32[8,32,128]{2,1,0:T(8,128)S(1)}, f32[8,32,128]{2,1,0:T(8,128)}, u32[]{:S(2)}) copy-start(f32[8,32,128]{2,1,0:T(8,128)} %density.5) | copy-start | bytes 393220
  4.5 14.6 %collective-permute-start = (f32[17,32,128]{2,1,0:T(8,128)S(1)}, f32[17,32,128]{2,1,0:T(8,128)S(1)}, u32[]{:S(2)}, u32[]{:S(2)}) collective-permute-start(f32[17,32,128]{2,1,0:T(8,128)S(1)} %get-tuple-element.16), channel_id=1, source_target_pairs={{0,2},{2,4},{4,6},{6,8},{8,10},{10,12},{12,14},{1,3},{3,5},{5,7},{... | collective-permute-start | bytes 835592 | tf_op jit(solution)/shard_map/ppermute | solution.py:476
  9.4 7.9 %collective-permute-start.1 = (f32[11,32,128]{2,1,0:T(8,128)S(1)}, f32[11,32,128]{2,1,0:T(8,128)S(1)}, u32[]{:S(2)}, u32[]{:S(2)}) collective-permute-start(f32[11,32,128]{2,1,0:T(8,128)S(1)} %get-tuple-element.17), channel_id=1, source_target_pairs={{2,0},{4,2},{6,4},{8,6},{10,8},{12,10},{14,12},{3,1},{5,3},{7,5},{... | collective-permute-start | bytes 540680 | tf_op jit(solution)/shard_map/ppermute | solution.py:477
  19.2 24.1 %copy-start.3 = (s32[8,32,128]{2,1,0:T(8,128)S(1)}, s32[8,32,128]{2,1,0:T(8,128)}, u32[]{:S(2)}) copy-start(s32[8,32,128]{2,1,0:T(8,128)} %occupancy.7) | copy-start | bytes 393220
  19.2 24.1 %copy-start.5 = (f32[8,32,128]{2,1,0:T(8,128)S(1)}, f32[8,32,128]{2,1,0:T(8,128)}, u32[]{:S(2)}) copy-start(f32[8,32,128]{2,1,0:T(8,128)} %density.5) | copy-start | bytes 393220
  19.2 1.7 %collective-permute-start.2 = (f32[84,8,128]{2,1,0:T(8,128)S(1)}, f32[84,8,128]{2,1,0:T(8,128)S(1)}, u32[]{:S(2)}, u32[]{:S(2)}) collective-permute-start(f32[84,8,128]{2,1,0:T(8,128)S(1)} %shard_map.60), channel_id=1, source_target_pairs={{0,1},{1,0},{2,3},{3,2},{4,5},{5,4},{6,7},{7,6},{8,9},{9,8},{10,11... | collective-permute-start | bytes 1032200 | tf_op jit(solution)/shard_map/ppermute | solution.py:480
  45.4 1.3 %collective-permute-start.3 = (f32[8,32,128]{2,1,0:T(8,128)S(1)}, f32[8,32,128]{2,1,0:T(8,128)S(1)}, u32[]{:S(2)}, u32[]{:S(2)}) collective-permute-start(f32[8,32,128]{2,1,0:T(8,128)S(1)} %get-tuple-element.23.mine), channel_id=1, source_target_pairs={{0,1},{1,0},{2,3},{3,2},{4,5},{5,4},{6,7},{7,6},{8,9},{9,8},{10,11... | collective-permute-start | bytes 393224 | tf_op jit(solution)/shard_map/ppermute | solution.py:497
  47.8 15.6 %all-to-all-start.1 = ((f32[8,32,128]{2,1,0:T(8,128)}), f32[8,32,128]{2,1,0:T(8,128)S(1)}, u32[]{:S(2)}, u32[]{:S(2)}) async-start(f32[8,32,128]{2,1,0:T(8,128)} %get-tuple-element.25), calls=%async_computation.1 | async-start | bytes 262144 | tf_op jit(solution)/shard_map/all_to_all | solution.py:507
  51.2 12.2 %collective-permute-start.4 = (f32[8,32,128]{2,1,0:T(8,128)S(1)}, f32[8,32,128]{2,1,0:T(8,128)S(1)}, u32[]{:S(2)}, u32[]{:S(2)}) collective-permute-start(f32[8,32,128]{2,1,0:T(8,128)S(1)} %get-tuple-element.24.mine), channel_id=1, source_target_pairs={{0,8},{2,10},{4,12},{6,14},{8,0},{10,2},{12,4},{14,6},{1,9},{3,11}... | collective-permute-start | bytes 393224 | tf_op jit(solution)/shard_map/ppermute | solution.py:503
where the time goes:
time: 74.9 us; the launch traced here: 74.4 us
  blocking collectives  23 us (31%)
  waiting for transfers between devices  20.8 us (28%)
  Pallas kernels  13.7 us (18%)
  starting transfers between devices  12.5 us (17%)
  local copies, waits for them, and re-layouts  3.8 us (5%)
    all_to_all x2, blocking collectives, everyone(): return lax.all_to_all(lines, PAIR, 0, 0, tiled=True)  23 us
    pallas_call x7, Pallas kernels, call(): pl.pallas_call(kernel, out_shape=[jax.ShapeDtypeStruct(s, jnp.float32) fo...  13.7 us
    ppermute x1, waiting for transfers between devices, local(): below = above = lax.ppermute(smooth, 'run', rise + fall)  9.35 us
    ppermute x1, waiting for transfers between devices, local(): high = lax.ppermute(down, 'run', [(i + 1, i) for i in range(count - 1)])  6.6 us
    ppermute x1, starting transfers between devices, local(): low = lax.ppermute(up, 'run', [(i, i + 1) for i in range(count - 1)])  4.89 us
    unnamed x12, local copies, waits for them, and re-layouts  3.8 us
    all_to_all x1, starting transfers between devices, local(): planes = lax.all_to_all(planes, 'run', 0, 0, tiled=True)  3.37 us
    ppermute x1, starting transfers between devices, local(): below = above = lax.ppermute(smooth, 'run', rise + fall)  2.84 us
  transfers between devices with their start and end apart: 6, of which 5 were waited for; matrix products, arithmetic and copies ran while one was open for 0% of the time, Pallas kernels for 0%

commit v1 on v0

v1 whole, which is shorter than its diff:
```python
import functools
import math

import jax
import jax.numpy as jnp
from jax import lax
from jax.experimental import pallas as pl
from jax.experimental.pallas import tpu as pltpu
from jax.sharding import PartitionSpec as P

REACH = 32
POISSON = 0.3
MARROW = 0.05
RATE = 0.5
SLOPE = 4.0
DECAY = REACH / 4.0

LAME = POISSON / ((1.0 + POISSON) * (1.0 - 2.0 * POISSON)) / 16.0
SHEAR = 0.5 / (1.0 + POISSON) / 16.0
ENTRY = 16.0 * (LAME + 4.0 * SHEAR) / 9.0
NORM = 1.0 / sum(math.exp(-abs(k) / DECAY) for k in range(-REACH, REACH + 1))

ROWS = 40
PAIR = ("run", "sub")

VMEM = pl.BlockSpec(memory_space=pltpu.VMEM)


def weight(distance):
    return NORM * math.exp(-distance / DECAY)


def call(kernel, outs, ins, scratch=()):
    return pl.pallas_call(
        kernel,
        out_shape=[jax.ShapeDtypeStruct(s, jnp.float32) for s in outs],
        in_specs=[VMEM] * len(ins),
        out_specs=[VMEM] * len(outs),
        scratch_shapes=[pltpu.VMEM(s, jnp.float32) for s in scratch],
        compiler_params=pltpu.CompilerParams(vmem_limit_bytes=40 * 1024 * 1024),
    )(*ins)


def lane_right(block):
    lane = lax.broadcasted_iota(jnp.int32, block.shape, 1)
    return jnp.where(lane == 0, 0.0, pltpu.roll(block, 1, 1))


def lane_left(block):
    lane = lax.broadcasted_iota(jnp.int32, block.shape, 1)
    return jnp.where(lane == block.shape[1] - 1, 0.0, pltpu.roll(block, block.shape[1] - 1, 1))


def row_down(block):
    row = lax.broadcasted_iota(jnp.int32, block.shape, 0)
    return jnp.where(row == block.shape[0] - 1, 0.0, pltpu.roll(block, block.shape[0] - 1, 0))


def stiff(occupancy, density):
    return jnp.where(occupancy == 1, density * density, MARROW)


def enter(pair, k, c, field):
    other = lane_right(field)
    pair[2 * c, k, 8:48] = field + other
    pair[2 * c + 1, k, 8:48] = field - other


def clear(pair):
    for m in range(6):
        for k in range(pair.shape[1]):
            pair[m, k, 0:8] = jnp.zeros((8, 128), jnp.float32)


def plane_modes(pair, k, tile):
    out = [None] * 12
    for c in range(3):
        for x in range(2):
            here = pair[2 * c + x, k, 8 + 8 * tile : 16 + 8 * tile]
            above = pair[2 * c + x, k, 7 + 8 * tile : 15 + 8 * tile]
            out[4 * c + x] = here + above
            out[4 * c + 2 + x] = here - above
    return out


def steps(count, body, carry):
    def turn(k, carry):
        return body(2 * k + 1, body(2 * k, carry))

    carry = lax.fori_loop(0, count // 2, turn, carry)
    return body(count - 1, carry) if count % 2 else carry


def march(pair, start, count, mod, near, far, to):
    for tile in range(ROWS // 8):
        rows = slice(8 * tile, 8 * tile + 8)

        def leave(k, totals):
            for c in range(3):
                for x in range(2):
                    s, d = totals[4 * c + x], totals[4 * c + 2 + x]
                    near[2 * c + x, k, rows] = s + d
                    far[2 * c + x, k, rows] = s - d

        def body(k, carry):
            low, kept = carry
            high = plane_modes(pair, start + k + 1, tile)
            g = stress(modes_of(low, high), mod(k, rows))
            totals, after = [None] * 12, [None] * 12
            for c in range(3):
                for m in range(4):
                    d = g[c][4 + m]
                    at = 4 * c + m
                    if m:
                        s = g[c][m]
                        totals[at] = kept[at] + (s - d)
                        after[at] = s + d
                    else:
                        totals[at] = kept[at] - d
                        after[at] = d
            leave(to + k, totals)
            return high, after

        zeros = [jnp.zeros((8, 128), jnp.float32)] * 12
        _, kept = steps(count, body, (plane_modes(pair, start, tile), zeros))
        leave(to + count, kept)


def image(near, far, k, c):
    columns = [
        near[2 * c + x, k, 0:ROWS] + far[2 * c + x, k, 1 : ROWS + 1] for x in range(2)
    ]
    return columns[0] + columns[1] + lane_left(columns[0] - columns[1])


def energy_march(pair, count, use):
    for tile in range(ROWS // 8):

        def body(k, low):
            high = plane_modes(pair, k + 1, tile)
            use(k, tile, quadratic(modes_of(low, high)))
            return high

        steps(count, body, plane_modes(pair, 0, tile))


def inverted(low, high):
    t = low + high
    t = t + row_down(t)
    t = (t + lane_left(t)) * ENTRY
    return jnp.where(t > 0.0, 1.0 / jnp.where(t > 0.0, t, 1.0), 0.0)


def whole(block):
    return jnp.sum(jnp.sum(block, axis=0, keepdims=True), axis=1, keepdims=True)


def modes_of(low, high):
    out = []
    for c in range(3):
        modes = [None] * 8
        for m in range(4):
            if m:
                modes[m] = high[4 * c + m] + low[4 * c + m]
            modes[4 + m] = high[4 * c + m] - low[4 * c + m]
        out.append(modes)
    return out


X, Y, Z = 1, 2, 4


def stress(u, mod):
    g = [[None] * 8 for _ in range(3)]
    bulk, rigid = mod * LAME, mod * SHEAR
    twice = rigid + rigid
    bulk3, rigid3 = mod * (LAME / 3.0), mod * (SHEAR / 3.0)
    last = mod * ((LAME + 4.0 * SHEAR) / 9.0)
    t = (u[0][X] + u[1][Y] + u[2][Z]) * bulk
    g[0][X] = t + u[0][X] * twice
    g[1][Y] = t + u[1][Y] * twice
    g[2][Z] = t + u[2][Z] * twice
    g[0][Y] = g[1][X] = (u[0][Y] + u[1][X]) * rigid
    g[0][Z] = g[2][X] = (u[0][Z] + u[2][X]) * rigid
    g[1][Z] = g[2][Y] = (u[1][Z] + u[2][Y]) * rigid
    for (c, m), (d, n) in (
        ((1, X | Y), (2, X | Z)),
        ((0, X | Y), (2, Y | Z)),
        ((0, X | Z), (1, Y | Z)),
    ):
        s = (u[c][m] + u[d][n]) * bulk3
        g[c][m] = s + u[c][m] * rigid
        g[d][n] = s + u[d][n] * rigid
    s = u[0][Y | Z] + u[1][X | Z] + u[2][X | Y]
    g[0][Y | Z] = (s + u[0][Y | Z]) * rigid3
    g[1][X | Z] = (s + u[1][X | Z]) * rigid3
    g[2][X | Y] = (s + u[2][X | Y]) * rigid3
    for c in range(3):
        g[c][7] = u[c][7] * last
    return g


def quadratic(u):
    def sq(v):
        return v * v

    t = sq(u[0][X] + u[1][Y] + u[2][Z])
    r2 = sq(u[0][X]) + sq(u[1][Y]) + sq(u[2][Z])
    r = sq(u[0][Y] + u[1][X]) + sq(u[0][Z] + u[2][X]) + sq(u[1][Z] + u[2][Y])
    t3 = 0.0
    for (c, m), (d, n) in (
        ((1, X | Y), (2, X | Z)),
        ((0, X | Y), (2, Y | Z)),
        ((0, X | Z), (1, Y | Z)),
    ):
        t3 = t3 + sq(u[c][m] + u[d][n])
        r = r + (sq(u[c][m]) + sq(u[d][n]))
    p, q, s = u[0][Y | Z], u[1][X | Z], u[2][X | Y]
    r3 = sq(p + q) + sq(p + s) + sq(q + s)
    last = sq(u[0][7]) + sq(u[1][7]) + sq(u[2][7])
    return (
        LAME * (t + t3 * (1.0 / 3.0))
        + SHEAR * (r + r2 + r2 + r3 * (1.0 / 3.0))
        + ((LAME + 4.0 * SHEAR) / 9.0) * last
    )


def side_rows(load, guess, occupancy, density):
    sub = lax.axis_index("sub")
    flat = lambda part: part.reshape((-1,) + part.shape[-2:])
    near = lambda part: jnp.where(sub == 0, part[..., 24:32, :], part[..., 0:8, :])
    return jnp.concatenate(
        [flat(near(guess)), flat(near(load)), stiff(near(occupancy), near(density))], axis=0
    )


def inner(
    load, guess, bone, density, side, up, down, guess_w, first_w, mod_w, inverse, square,
    pair, near, far,
):
    sub = lax.axis_index("sub")
    own = pl.ds(pl.multiple_of(8 * sub, 8), 32)
    rest = pl.ds(pl.multiple_of(32 * (1 - sub), 8), 8)
    clear(pair)
    far[:, :, ROWS : ROWS + 8] = jnp.zeros((6, 8, 8, 128), jnp.float32)
    for k in range(8):
        mod_w[k, own] = stiff(bone[k], density[k])
        mod_w[k, rest] = side[48 + k]
        for c in range(3):
            guess_w[c, k, own] = guess[c, k]
            guess_w[c, k, rest] = side[8 * c + k]
            first_w[c, k, own] = load[c, k]
            first_w[c, k, rest] = side[24 + 8 * c + k]

    def prepare(k, _):
        for c in range(3):
            enter(pair, k, c, guess_w[c, k])
        return 0

    lax.fori_loop(0, 8, prepare, 0)
    for k in range(7):
        inverse[k] = inverted(mod_w[k], mod_w[k + 1])
    march(pair, 0, 7, lambda k, rows: mod_w[k + 1, rows], near, far, 0)
    square[...] = jnp.zeros_like(square)

    def settle(k, _):
        for c in range(3):
            residual = first_w[c, k] - image(near, far, k, c)
            z = residual * inverse[k]
            first_w[c, k] = z
            square[...] += residual * z
        return 0

    for c in range(3):
        down[3 + c] = first_w[c, 0] - image(near, far, 0, c)
        up[3 + c] = first_w[c, 7] - image(near, far, 7, c)
    lax.fori_loop(1, 7, settle, 0)
    for c in range(3):
        down[c] = guess_w[c, 0]
        up[c] = guess_w[c, 7]
        up[6 + c] = first_w[c, 6]
    up[9] = mod_w[7]
    down[6] = mod_w[0]
    down[7] = inverse[0]


def krylov(
    up, down, guess_w, first_w, mod_w, inverse, square, low, high, row_out, first, second,
    pair, near, far, mods, inverses, sums,
):
    sub = lax.axis_index("sub")
    run = lax.axis_index("run")
    own = pl.ds(pl.multiple_of(8 * sub, 8), 32)
    clear(pair)
    far[:, :, ROWS : ROWS + 8] = jnp.zeros((6, 11, 8, 128), jnp.float32)
    mods[0] = low[9]
    mods[9] = high[6]
    for k in range(8):
        mods[1 + k] = mod_w[k]
    inverses[0] = jnp.where(run > 0, inverted(low[9], mod_w[0]), 0.0)
    for k in range(7):
        inverses[1 + k] = inverse[k]
    inverses[8] = inverted(mod_w[7], high[6])

    for c in range(3):
        enter(pair, 0, c, low[c])
        enter(pair, 1, c, guess_w[c, 0])
        enter(pair, 2, c, guess_w[c, 7])
        enter(pair, 3, c, high[c])
    march(pair, 0, 1, lambda k, rows: mods[1, rows], near, far, 0)
    march(pair, 2, 1, lambda k, rows: mods[9, rows], near, far, 2)
    begun = (low, down, up, high)
    invert = (inverses[0], inverses[1], inverses[8], high[7])
    sums[...] = jnp.zeros_like(sums)
    dot = square[...]
    for c in range(3):
        values = []
        for k in range(4):
            residual = begun[k][3 + c] - image(near, far, k, c)
            z = residual * invert[k]
            values.append(z)
            if k in (1, 2):
                dot = dot + residual * z
        first[c, 0] = low[6 + c]
        first[c, 1] = values[0]
        first[c, 2] = values[1]
        for k in range(1, 7):
            first[c, 2 + k] = first_w[c, k]
        first[c, 9] = values[2]
        first[c, 10] = values[3]
    sums[0] = dot

    def prepare(k, _):
        for c in range(3):
            enter(pair, k, c, first[c, k])
        return 0

    lax.fori_loop(0, 11, prepare, 0)
    march(pair, 0, 10, lambda k, rows: mods[k, rows], near, far, 0)

    def settle(k, _):
        dot, cross = 0.0, 0.0
        for c in range(3):
            w = image(near, far, k + 1, c)
            s = w * inverses[k]
            second[c, k] = s
            enter(pair, k, c, s)
            dot = dot + w * first[c, k + 1]
            cross = cross + w * s

        @pl.when(k >= 1)
        def _():
            sums[1] += dot
            sums[2] += cross

        return 0

    lax.fori_loop(0, 9, settle, 0)

    def use(k, tile, value):
        rows = slice(8 * tile, 8 * tile + 8)
        sums[3, rows] += value * mods[k + 1, rows]

    energy_march(pair, 8, use)
    lane = lax.broadcasted_iota(jnp.int32, (1, 128), 1)
    line = jnp.zeros((1, 128), jnp.float32)
    for k in range(4):
        line = jnp.where(lane == k, whole(sums[k, own]), line)
    row_out[...] = jnp.broadcast_to(line, row_out.shape)


def pick(line, k):
    lane = lax.broadcasted_iota(jnp.int32, line.shape, 1)
    return jnp.sum(jnp.where(lane == k, line, 0.0), axis=1, keepdims=True)


def energies(
    lines, guess_w, low, first, second, occupancy, density, out, smooth, pair, field, specific
):
    sub = lax.axis_index("sub")
    own = pl.ds(pl.multiple_of(8 * sub, 8), 32)
    line = jnp.sum(lines[...], axis=0, keepdims=True)
    a, b, c, e = (pick(line, k) for k in range(4))
    alpha = a / b
    fresh = alpha * alpha * c - a
    beta = fresh / a
    square = alpha * alpha * e - (1.0 + beta) * (1.0 + beta) * b
    after = fresh / square
    p = jnp.broadcast_to(alpha + after * (1.0 + beta), (ROWS, 128))
    q = jnp.broadcast_to(-after * alpha, (ROWS, 128))
    clear(pair)
    for c in range(3):
        enter(pair, 0, c, low[c] + p * first[c, 1] + q * second[c, 0])

    def advance(k, _):
        for c in range(3):
            value = guess_w[c, k] + p * first[c, k + 2] + q * second[c, k + 1]
            field[c] = value
            enter(pair, k + 1, c, value)
        for c in range(3):
            out[c, k] = field[c, own]
        return 0

    lax.fori_loop(0, 8, advance, 0)

    def use(k, tile, value):
        specific[k, 8 * tile : 8 * tile + 8] = value

    energy_march(pair, 8, use)
    parts = []
    for k in range(8):
        rho = density[k]
        share = jnp.where(occupancy[k] == 1, rho * rho / rho, 0.0)
        parts.append(0.5 * share * specific[k, own])
    row = lax.broadcasted_iota(jnp.int32, (128, 128), 0)
    col = lax.broadcasted_iota(jnp.int32, (128, 128), 1)
    gap = jnp.abs(row - col).astype(jnp.float32)
    band = jnp.where(gap <= REACH, NORM * jnp.exp(gap * (-1.0 / DECAY)), 0.0)
    smooth[...] = jnp.dot(
        jnp.concatenate(parts, axis=0), band,
        precision=lax.Precision.HIGHEST, preferred_element_type=jnp.float32,
    ).reshape(smooth.shape)


def along_y(mine, other, out, planes):
    sub = lax.axis_index("sub")
    run = lax.axis_index("run")
    row = lax.broadcasted_iota(jnp.int32, (32, 32), 0)
    col = lax.broadcasted_iota(jnp.int32, (32, 32), 1)

    def band(offset):
        gap = jnp.abs(col + offset - row).astype(jnp.float32)
        return jnp.where(gap <= REACH, NORM * jnp.exp(gap * (-1.0 / DECAY)), 0.0)

    near = band(0)
    far = band(32 - 64 * sub)
    upward, downward = 0.0, 0.0
    for k in range(8):
        value = jnp.dot(
            near, mine[k], precision=lax.Precision.HIGHEST, preferred_element_type=jnp.float32
        ) + jnp.dot(
            far, other[k], precision=lax.Precision.HIGHEST, preferred_element_type=jnp.float32
        )
        out[k] = value
        upward = upward + math.exp(-(7 - k) / DECAY) * value
        downward = downward + math.exp(-k / DECAY) * value
    for k in range(planes.shape[0]):
        planes[k] = jnp.where(k > run, upward, downward)


def along_z(count, mine, planes, below, above, occupancy, stimulus, row_out):
    run = lax.axis_index("run")
    span = REACH // 8
    lower, upper = 0.0, 0.0
    for o in range(1, span):
        scale = math.exp(-8.0 * (o - 1) / DECAY)
        at = jnp.maximum(run - o, 0)
        lower = lower + jnp.where(run - o >= 0, scale * planes[at], 0.0)
        at = jnp.minimum(run + o, count - 1)
        upper = upper + jnp.where(run + o < count, scale * planes[at], 0.0)
    has_below = run - span >= 0
    has_above = run + span < count
    total, bone = 0.0, 0.0
    for i in range(8):
        value = weight(i + 1) * lower + weight(8 - i) * upper
        far_below, far_above = 0.0, 0.0
        for j in range(8):
            value = value + weight(abs(i - j)) * mine[j]
            if j >= i:
                far_below = far_below + weight(i - j + REACH) * below[j]
            if j <= i:
                far_above = far_above + weight(j - i + REACH) * above[j]
        value = value + jnp.where(has_below, far_below, 0.0) + jnp.where(has_above, far_above, 0.0)
        stimulus[i] = value
        share = occupancy[i].astype(jnp.float32)
        total = total + share * value
        bone = bone + share
    lane = lax.broadcasted_iota(jnp.int32, (1, 128), 1)
    line = jnp.where(lane == 0, whole(total), jnp.where(lane == 1, whole(bone), 0.0))
    row_out[...] = jnp.broadcast_to(line, row_out.shape)


def remodel(lines, stimulus, occupancy, density, out):
    line = jnp.sum(lines[...], axis=0, keepdims=True)
    mean = jnp.broadcast_to(pick(line, 0) / pick(line, 1), stimulus.shape[1:])
    for k in range(8):
        rho = density[k]
        updated = jnp.minimum(rho * (1.0 + RATE * jnp.tanh(SLOPE * (stimulus[k] / mean - 1.0))), 1.0)
        out[k] = jnp.where(occupancy[k] == 1, updated, rho)


def everyone(lines):
    return lax.all_to_all(lines, PAIR, 0, 0, tiled=True)


def local(load, guess, occupancy, density):
    count = lax.axis_size("run")
    members = count * lax.axis_size("sub")
    block = density.shape
    swap = [(0, 1), (1, 0)]
    side = lax.ppermute(side_rows(load, guess, occupancy, density), "sub", swap)
    wide = (3, 8, ROWS, 128)
    kept = call(
        inner,
        [
            (10, ROWS, 128), (8, ROWS, 128), wide, wide,
            (8, ROWS, 128), (7, ROWS, 128), (ROWS, 128),
        ],
        [load, guess, occupancy, density, side],
        [(6, 8, 48, 128), (6, 8, 48, 128), (6, 8, 48, 128)],
    )
    up, down, guess_w = kept[:3]
    low = lax.ppermute(up, "run", [(i, i + 1) for i in range(count - 1)])
    high = lax.ppermute(down, "run", [(i + 1, i) for i in range(count - 1)])
    lines, first, second = call(
        krylov,
        [(members, 128), (3, 11, ROWS, 128), (3, 9, ROWS, 128)],
        [*kept, low, high],
        [
            (6, 11, 48, 128), (6, 11, 48, 128), (6, 11, 48, 128),
            (10, ROWS, 128), (9, ROWS, 128), (4, ROWS, 128),
        ],
    )
    lines = everyone(lines)
    displacement, smooth = call(
        energies,
        [guess.shape, block],
        [lines, guess_w, low, first, second, occupancy, density],
        [(6, 9, 48, 128), (3, ROWS, 128), (8, ROWS, 128)],
    )
    other = lax.ppermute(smooth, "sub", swap)
    smooth, planes = call(along_y, [block, (count, 32, 128)], [smooth, other])
    span = REACH // 8
    rise = [(i, i + span) for i in range(count - span)]
    fall = [(i + span, i) for i in range(count - span)]
    if count <= 2 * span:
        below = above = lax.ppermute(smooth, "run", rise + fall)
    else:
        below = lax.ppermute(smooth, "run", rise)
        above = lax.ppermute(smooth, "run", fall)
    planes = lax.all_to_all(planes, "run", 0, 0, tiled=True)
    stimulus, lines = call(
        functools.partial(along_z, count),
        [block, (members, 128)],
        [smooth, planes, below, above, occupancy],
    )
    lines = everyone(lines)
    (new_density,) = call(remodel, [block], [lines, stimulus, occupancy, density])
    return displacement, new_density


def solution(mesh):
    field = P(None, ("grp", "run"), "sub", None)
    cells = P(("grp", "run"), "sub", None)
    return jax.shard_map(
        local,
        mesh=mesh,
        in_specs=(field, field, cells, cells),
        out_specs=(field, cells),
        check_vma=False,
    )
```

time: 74.9 us -> 69.5 us (0.928)
  local copies, waits for them, and re-layouts: 3.8 us -> 0.03 us
  waiting for transfers between devices: 20.8 us -> 18.7 us
  other arithmetic: 0 us -> 1.97 us
  Pallas kernels: 13.7 us -> 11.9 us
    unnamed x12 -> x8, local copies, waits for them, and re-layouts: 3.8 us -> 0.03 us
    select_n x0 -> x2, other arithmetic: none -> 1.96 us  [the longest x1 1.14 us: side_rows(): jnp.where(sub == 0, part[..., 24:32, :], part[..., 0:8, :])]
    pallas_call x7 -> x6, Pallas kernels: 13.7 us -> 11.9 us  [call(): pl.pallas_call(kernel, out_shape=[jax.ShapeDtypeStruct(s, jnp.float32) fo...]
    ppermute x1, waiting for transfers between devices: 1.84 us -> 0.3 us  [local(): low = lax.ppermute(up, 'run', [(i, i + 1) for i in range(count - 1)])]
where the time goes in v1:
time: 69.5 us; the launch traced here: 69.1 us
  blocking collectives  22.9 us (33%)
  waiting for transfers between devices  18.7 us (27%)
  starting transfers between devices  12.8 us (18%)
  Pallas kernels  11.9 us (17%)
  other arithmetic  1.97 us (3%)
  between operations  0.72 us (1%)
    all_to_all x2, blocking collectives, everyone(): return lax.all_to_all(lines, PAIR, 0, 0, tiled=True)  22.9 us
    pallas_call x6, Pallas kernels, call(): pl.pallas_call(kernel, out_shape=[jax.ShapeDtypeStruct(s, jnp.float32) fo...  11.9 us
    ppermute x1, waiting for transfers between devices, local(): below = above = lax.ppermute(smooth, 'run', rise + fall)  9.35 us
    ppermute x1, waiting for transfers between devices, local(): high = lax.ppermute(down, 'run', [(i + 1, i) for i in range(count - 1)])  6.55 us
    ppermute x1, starting transfers between devices, local(): low = lax.ppermute(up, 'run', [(i, i + 1) for i in range(count - 1)])  4.81 us
    all_to_all x1, starting transfers between devices, local(): planes = lax.all_to_all(planes, 'run', 0, 0, tiled=True)  3.37 us
    ppermute x1, starting transfers between devices, local(): below = above = lax.ppermute(smooth, 'run', rise + fall)  2.84 us
  transfers between devices with their start and end apart: 6, of which 5 were waited for; matrix products, arithmetic and copies ran while one was open for 0% of the time, Pallas kernels for 0%

profile of v1, /device:TPU:0, one launch (start us, length us, event | category | flops | bytes accessed | tf_op | source)
XLA Modules:
  0.0 69.1 jit_solution(17325712211218509232)
XLA Ops:
  0.6 0.8 %multiply_select_fusion = f32[8,8,128]{2,1,0:T(8,128)S(1)} fusion(f32[8,32,128]{2,1,0:T(8,128)} %density.5, s32[8,32,128]{2,1,0:T(8,128)} %occupancy.5, pred[]{:T(512)S(6)} %eq.12), kind=kLoop, calls=%fused_computation.3 | loop fusion | flops 40960 | bytes 163841 | tf_op jit(solution)/shard_map/jit(_where)/select_n | solution.py:60
  1.5 0.0 copy-start.2
  1.5 0.0 copy-start.3
  1.5 1.1 %slice_select_fusion = (f32[3,8,8,128]{3,2,1,0:T(8,128)S(1)}, f32[3,8,8,128]{3,2,1,0:T(8,128)S(1)}) fusion(f32[3,8,32,128]{3,2,1,0:T(8,128)} %load.1, pred[]{:T(512)S(6)} %eq.12, f32[3,8,32,128]{3,2,1,0:T(8,128)} %guess.1), kind=kLoop, calls=%fused_computation.1 | loop fusion | flops 49152 | bytes 589825 | tf_op jit(solution)/shard_map/jit(_where)/select_n | solution.py:231
  2.6 0.0 copy-start
  2.6 0.0 copy-start.1
  2.7 0.5 collective-permute-start
  3.2 1.1 %collective-permute-done.side = f32[56,8,128]{2,1,0:T(8,128)S(1)} collective-permute-done((f32[56,8,128]{2,1,0:T(8,128)S(1)}, f32[56,8,128]{2,1,0:T(8,128)S(1)}, u32[]{:S(2)}, u32[]{:S(2)}) %collective-permute-start) | collective-permute-done | bytes 229408 | tf_op jit(solution)/shard_map/ppermute | solution.py:501
  4.3 0.0 copy-done.2
  4.3 0.0 copy-done.3
  4.3 0.0 copy-done
  4.3 0.0 copy-done.1
  4.3 2.4 %shard_map.59 = (f32[10,40,128]{2,1,0:T(8,128)S(1)}, f32[8,40,128]{2,1,0:T(8,128)S(1)}, f32[3,8,40,128]{3,2,1,0:T(8,128)S(1)}, f32[3,8,40,128]{3,2,1,0:T(8,128)S...) custom-call(f32[3,8,32,128]{3,2,1,0:T(8,128)S(1)} %copy-done.2, ...), custom_call_target="tpu_custom_call" | custom-call | tf_op jit(solution)/shard_map/pallas_call | solution.py:34
  6.7 4.8 %collective-permute-start.1 = (f32[10,40,128]{2,1,0:T(8,128)S(1)}, f32[10,40,128]{2,1,0:T(8,128)S(1)}, u32[]{:S(2)}, u32[]{:S(2)}) collective-permute-start(f32[10,40,128]{2,1,0:T(8,128)S(1)} %get-tuple-element.18.up), channel_id=1, source_target_pairs={{0,2},{2,4},{4,6},{6,8},{8,10},{10,12},{12,14},{1,3},{3,5},{5,7},{... | collective-permute-start | bytes 614408 | tf_op jit(solution)/shard_map/ppermute | solution.py:513
  11.5 1.3 %collective-permute-start.2 = (f32[8,40,128]{2,1,0:T(8,128)S(1)}, f32[8,40,128]{2,1,0:T(8,128)S(1)}, u32[]{:S(2)}, u32[]{:S(2)}) collective-permute-start(f32[8,40,128]{2,1,0:T(8,128)S(1)} %get-tuple-element.19.down), channel_id=1, source_target_pairs={{2,0},{4,2},{6,4},{8,6},{10,8},{12,10},{14,12},{3,1},{5,3},{7,5},{... | collective-permute-start | bytes 491528 | tf_op jit(solution)/shard_map/ppermute | solution.py:514
  12.8 6.5 %collective-permute-done.2.high = f32[8,40,128]{2,1,0:T(8,128)S(1)} collective-permute-done((f32[8,40,128]{2,1,0:T(8,128)S(1)}, f32[8,40,128]{2,1,0:T(8,128)S(1)}, u32[]{:S(2)}, u32[]{:S(2)}) %collective-permute-start.2) | collective-permute-done | bytes 163872 | tf_op jit(solution)/shard_map/ppermute | solution.py:514
  19.4 0.3 collective-permute-done.1.low
  19.7 4.9 %shard_map.60 = (f32[16,128]{1,0:T(8,128)S(1)}, f32[3,11,40,128]{3,2,1,0:T(8,128)S(1)}, f32[3,9,40,128]{3,2,1,0:T(8,128)S(1)}) custom-call(f32[10,40,128]{2,1,0:T(8,128)S(1)} %get-tuple-element.18.up, f32[8,40,128]{2,1,0:T(8,128)S(1)} %get-tuple-element.19.down, f32[3,8,40,128]{3,2,1,0:T(8,128)S(1)} %get-tuple-element.20.guess_w, ...), custom_call_target="tpu_custom_call" | custom-call | tf_op jit(solution)/shard_map/pallas_call | solution.py:34
  24.6 13.0 %all_to_all.27 = f32[16,1,128]{2,1,0:T(1,128)S(1)} all-to-all(f32[16,1,128]{2,1,0:T(1,128)S(1)} %bitcast.12), channel_id=1, replica_groups=mesh['grp'=2,'run'=8,'sub'=2] {'run','sub'}, dimensions={0} | all-to-all | bytes 16384 | tf_op jit(solution)/shard_map/all_to_all | solution.py:493
  37.6 2.5 %shard_map.61 = (f32[3,8,32,128]{3,2,1,0:T(8,128)}, f32[8,32,128]{2,1,0:T(8,128)S(1)}) custom-call(f32[16,128]{1,0:T(8,128)S(1)} %bitcast.10, f32[3,8,40,128]{3,2,1,0:T(8,128)S(1)} %get-tuple-element.20.guess_w, f32[10,40,128]{2,1,0:T(8,128)S(1)} %collective-permute-done.1.low, f32[3,11,40,128]{3,2,1,0:T(8,128)S(1)} %get-tuple-element.26.first, ...), custom_call_target="tpu_custom_call" | custom-call | tf_op jit(solution)/shard_map/pallas_call | solution.py:34
  40.0 0.0 collective-permute-start.3
  40.0 1.3 %collective-permute-done.3.other = f32[8,32,128]{2,1,0:T(8,128)S(1)} collective-permute-done((f32[8,32,128]{2,1,0:T(8,128)S(1)}, f32[8,32,128]{2,1,0:T(8,128)S(1)}, u32[]{:S(2)}, u32[]{:S(2)}) %collective-permute-start.3) | collective-permute-done | bytes 131104 | tf_op jit(solution)/shard_map/ppermute | solution.py:531
  41.4 1.1 %shard_map.62 = (f32[8,32,128]{2,1,0:T(8,128)S(1)}, f32[8,32,128]{2,1,0:T(8,128)}) custom-call(f32[8,32,128]{2,1,0:T(8,128)S(1)} %get-tuple-element.29.mine, f32[8,32,128]{2,1,0:T(8,128)S(1)} %collective-permute-done.3.other), custom_call_target="tpu_custom_call" | custom-call | tf_op jit(solution)/shard_map/pallas_call | solution.py:34
  42.5 3.4 %all-to-all-start.1 = ((f32[8,32,128]{2,1,0:T(8,128)}), f32[8,32,128]{2,1,0:T(8,128)S(1)}, u32[]{:S(2)}, u32[]{:S(2)}) async-start(f32[8,32,128]{2,1,0:T(8,128)} %get-tuple-element.31), calls=%async_computation.1 | async-start | bytes 262144 | tf_op jit(solution)/shard_map/all_to_all | solution.py:541
  45.9 2.8 %collective-permute-start.4 = (f32[8,32,128]{2,1,0:T(8,128)S(1)}, f32[8,32,128]{2,1,0:T(8,128)S(1)}, u32[]{:S(2)}, u32[]{:S(2)}) collective-permute-start(f32[8,32,128]{2,1,0:T(8,128)S(1)} %get-tuple-element.30.mine), channel_id=1, source_target_pairs={{0,8},{2,10},{4,12},{6,14},{8,0},{10,2},{12,4},{14,6},{1,9},{3,11}... | collective-permute-start | bytes 393224 | tf_op jit(solution)/shard_map/ppermute | solution.py:537
  48.7 9.3 %collective-permute-done.4.below.above = f32[8,32,128]{2,1,0:T(8,128)S(1)} collective-permute-done((f32[8,32,128]{2,1,0:T(8,128)S(1)}, f32[8,32,128]{2,1,0:T(8,128)S(1)}, u32[]{:S(2)}, u32[]{:S(2)}) %collective-permute-start.4) | collective-permute-done | bytes 131104 | tf_op jit(solution)/shard_map/ppermute | solution.py:537
  58.1 0.0 all-to-all-done.1.planes
  58.1 0.3 shard_map.63
  58.4 9.9 %all_to_all.28 = f32[16,1,128]{2,1,0:T(1,128)S(1)} all-to-all(f32[16,1,128]{2,1,0:T(1,128)S(1)} %bitcast.13), channel_id=1, replica_groups=mesh['grp'=2,'run'=8,'sub'=2] {'run','sub'}, dimensions={0} | all-to-all | bytes 16384 | tf_op jit(solution)/shard_map/all_to_all | solution.py:493
  68.3 0.8 %shard_map.64 = f32[8,32,128]{2,1,0:T(8,128)} custom-call(f32[16,128]{1,0:T(8,128)S(1)} %bitcast.11, f32[8,32,128]{2,1,0:T(8,128)S(1)} %get-tuple-element.33.stimulus, s32[8,32,128]{2,1,0:T(8,128)S(1)} %copy-done, f32[8,32,128]{2,1,0:T(8,128)S(1)} %copy-done.1), custom_call_target="tpu_custom_call" | custom-call | tf_op jit(solution)/shard_map/pallas_call | solution.py:34
  (1 shorter events, 0.0 us)
Async XLA Ops:
  1.5 2.8 %copy-start.2 = (f32[3,8,32,128]{3,2,1,0:T(8,128)S(1)}, f32[3,8,32,128]{3,2,1,0:T(8,128)}, u32[]{:S(2)}) copy-start(f32[3,8,32,128]{3,2,1,0:T(8,128)} %load.1) | copy-start | bytes 1179652
  1.5 2.8 %copy-start.3 = (f32[3,8,32,128]{3,2,1,0:T(8,128)S(1)}, f32[3,8,32,128]{3,2,1,0:T(8,128)}, u32[]{:S(2)}) copy-start(f32[3,8,32,128]{3,2,1,0:T(8,128)} %guess.1) | copy-start | bytes 1179652
  2.6 1.7 %copy-start = (s32[8,32,128]{2,1,0:T(8,128)S(1)}, s32[8,32,128]{2,1,0:T(8,128)}, u32[]{:S(2)}) copy-start(s32[8,32,128]{2,1,0:T(8,128)} %occupancy.5) | copy-start | bytes 393220
  2.6 1.7 %copy-start.1 = (f32[8,32,128]{2,1,0:T(8,128)S(1)}, f32[8,32,128]{2,1,0:T(8,128)}, u32[]{:S(2)}) copy-start(f32[8,32,128]{2,1,0:T(8,128)} %density.5) | copy-start | bytes 393220
  2.7 1.6 %collective-permute-start = (f32[56,8,128]{2,1,0:T(8,128)S(1)}, f32[56,8,128]{2,1,0:T(8,128)S(1)}, u32[]{:S(2)}, u32[]{:S(2)}) collective-permute-start(f32[56,8,128]{2,1,0:T(8,128)S(1)} %pad_maximum_fusion), channel_id=1, source_target_pairs={{0,1},{1,0},{2,3},{3,2},{4,5},{5,4},{6,7},{7,6},{8,9},{9,8},{10,11... | collective-permute-start | bytes 688136 | tf_op jit(solution)/shard_map/ppermute | solution.py:501
  6.7 13.0 %collective-permute-start.1 = (f32[10,40,128]{2,1,0:T(8,128)S(1)}, f32[10,40,128]{2,1,0:T(8,128)S(1)}, u32[]{:S(2)}, u32[]{:S(2)}) collective-permute-start(f32[10,40,128]{2,1,0:T(8,128)S(1)} %get-tuple-element.18.up), channel_id=1, source_target_pairs={{0,2},{2,4},{4,6},{6,8},{8,10},{10,12},{12,14},{1,3},{3,5},{5,7},{... | collective-permute-start | bytes 614408 | tf_op jit(solution)/shard_map/ppermute | solution.py:513
  11.5 7.8 %collective-permute-start.2 = (f32[8,40,128]{2,1,0:T(8,128)S(1)}, f32[8,40,128]{2,1,0:T(8,128)S(1)}, u32[]{:S(2)}, u32[]{:S(2)}) collective-permute-start(f32[8,40,128]{2,1,0:T(8,128)S(1)} %get-tuple-element.19.down), channel_id=1, source_target_pairs={{2,0},{4,2},{6,4},{8,6},{10,8},{12,10},{14,12},{3,1},{5,3},{7,5},{... | collective-permute-start | bytes 491528 | tf_op jit(solution)/shard_map/ppermute | solution.py:514
  40.0 1.3 %collective-permute-start.3 = (f32[8,32,128]{2,1,0:T(8,128)S(1)}, f32[8,32,128]{2,1,0:T(8,128)S(1)}, u32[]{:S(2)}, u32[]{:S(2)}) collective-permute-start(f32[8,32,128]{2,1,0:T(8,128)S(1)} %get-tuple-element.29.mine), channel_id=1, source_target_pairs={{0,1},{1,0},{2,3},{3,2},{4,5},{5,4},{6,7},{7,6},{8,9},{9,8},{10,11... | collective-permute-start | bytes 393224 | tf_op jit(solution)/shard_map/ppermute | solution.py:531
  42.5 15.6 %all-to-all-start.1 = ((f32[8,32,128]{2,1,0:T(8,128)}), f32[8,32,128]{2,1,0:T(8,128)S(1)}, u32[]{:S(2)}, u32[]{:S(2)}) async-start(f32[8,32,128]{2,1,0:T(8,128)} %get-tuple-element.31), calls=%async_computation.1 | async-start | bytes 262144 | tf_op jit(solution)/shard_map/all_to_all | solution.py:541
  45.9 12.2 %collective-permute-start.4 = (f32[8,32,128]{2,1,0:T(8,128)S(1)}, f32[8,32,128]{2,1,0:T(8,128)S(1)}, u32[]{:S(2)}, u32[]{:S(2)}) collective-permute-start(f32[8,32,128]{2,1,0:T(8,128)S(1)} %get-tuple-element.30.mine), channel_id=1, source_target_pairs={{0,8},{2,10},{4,12},{6,14},{8,0},{10,2},{12,4},{14,6},{1,9},{3,11}... | collective-permute-start | bytes 393224 | tf_op jit(solution)/shard_map/ppermute | solution.py:537

commit v2 on v1

--- a/solution.py
+++ b/solution.py
@@ -30,7 +30,10 @@
     return NORM * math.exp(-distance / DECAY)
 
 
-def call(kernel, outs, ins, scratch=()):
+def call(kernel, outs, ins, scratch=(), flops=None):
+    cost = None
+    if flops is not None:
+        cost = pl.CostEstimate(flops=flops, bytes_accessed=2**20, transcendentals=0)
     return pl.pallas_call(
         kernel,
         out_shape=[jax.ShapeDtypeStruct(s, jnp.float32) for s in outs],
@@ -38,6 +41,7 @@
         out_specs=[VMEM] * len(outs),
         scratch_shapes=[pltpu.VMEM(s, jnp.float32) for s in scratch],
         compiler_params=pltpu.CompilerParams(vmem_limit_bytes=40 * 1024 * 1024),
+        cost_estimate=cost,
     )(*ins)
 
 
@@ -448,29 +452,43 @@
         planes[k] = jnp.where(k > run, upward, downward)
 
 
-def along_z(count, mine, planes, below, above, occupancy, stimulus, row_out):
+def near_z(count, planes, i):
     run = lax.axis_index("run")
-    span = REACH // 8
     lower, upper = 0.0, 0.0
-    for o in range(1, span):
+    for o in range(1, REACH // 8):
         scale = math.exp(-8.0 * (o - 1) / DECAY)
         at = jnp.maximum(run - o, 0)
-        lower = lower + jnp.where(run - o >= 0, scale * planes[at], 0.0)
+        lower = lower + jnp.where(run - o >= 0, scale * planes[at, 0:32], 0.0)
         at = jnp.minimum(run + o, count - 1)
-        upper = upper + jnp.where(run + o < count, scale * planes[at], 0.0)
-    has_below = run - span >= 0
-    has_above = run + span < count
+        upper = upper + jnp.where(run + o < count, scale * planes[at, 0:32], 0.0)
+    return weight(i + 1) * lower + weight(8 - i) * upper
+
+
+def far_z(count, mine, below, above):
+    run = lax.axis_index("run")
+    has_below = run - REACH // 8 >= 0
+    has_above = run + REACH // 8 < count
+    for i in range(8):
+        value, far_below, far_above = 0.0, 0.0, 0.0
+        for j in range(8):
+            value = value + weight(abs(i - j)) * mine(j)
+            if j >= i:
+                far_below = far_below + weight(i - j + REACH) * below(j)
+            if j <= i:
+                far_above = far_above + weight(j - i + REACH) * above(j)
+        yield value + jnp.where(has_below, far_below, 0.0) + jnp.where(has_above, far_above, 0.0)
+
+
+def partial_z(count, mine, below, above, out):
+    blocks = [lambda j, ref=ref: ref[j] for ref in (mine, below, above)]
+    for i, value in enumerate(far_z(count, *blocks)):
+        out[i] = value
+
+
+def along_z(count, part, planes, occupancy, stimulus, row_out):
     total, bone = 0.0, 0.0
     for i in range(8):
-        value = weight(i + 1) * lower + weight(8 - i) * upper
-        far_below, far_above = 0.0, 0.0
-        for j in range(8):
-            value = value + weight(abs(i - j)) * mine[j]
-            if j >= i:
-                far_below = far_below + weight(i - j + REACH) * below[j]
-            if j <= i:
-                far_above = far_above + weight(j - i + REACH) * above[j]
-        value = value + jnp.where(has_below, far_below, 0.0) + jnp.where(has_above, far_above, 0.0)
+        value = part[i] + near_z(count, planes, i)
         stimulus[i] = value
         share = occupancy[i].astype(jnp.float32)
         total = total + share * value
@@ -530,23 +548,28 @@
     )
     other = lax.ppermute(smooth, "sub", swap)
     smooth, planes = call(along_y, [block, (count, 32, 128)], [smooth, other])
-    span = REACH // 8
+    below, above = far_slabs(smooth)
+    planes = lax.all_to_all(planes, "run", 0, 0, tiled=True)
+    (part,) = call(
+        functools.partial(partial_z, count), [block], [smooth, below, above], flops=10**10
+    )
+    stimulus, lines = call(
+        functools.partial(along_z, count), [block, (members, 128)], [part, planes, occupancy]
+    )
+    lines = everyone(lines)
+    (new_density,) = call(remodel, [block], [lines, stimulus, occupancy, density])
+    return displacement, new_density
+
+
+def far_slabs(block):
+    count = lax.axis_size("run")
+    span = REACH // block.shape[0]
     rise = [(i, i + span) for i in range(count - span)]
     fall = [(i + span, i) for i in range(count - span)]
     if count <= 2 * span:
-        below = above = lax.ppermute(smooth, "run", rise + fall)
-    else:
-        below = lax.ppermute(smooth, "run", rise)
-        above = lax.ppermute(smooth, "run", fall)
-    planes = lax.all_to_all(planes, "run", 0, 0, tiled=True)
-    stimulus, lines = call(
-        functools.partial(along_z, count),
-        [block, (members, 128)],
-        [smooth, planes, below, above, occupancy],
-    )
-    lines = everyone(lines)
-    (new_density,) = call(remodel, [block], [lines, stimulus, occupancy, density])
-    return displacement, new_density
+        both = lax.ppermute(block, "run", rise + fall)
+        return both, both
+    return lax.ppermute(block, "run", rise), lax.ppermute(block, "run", fall)
 
 
 def solution(mesh):

time: 69.5 us -> 64.9 us (0.934)
  starting transfers between devices: 12.8 us -> 10.8 us
  waiting for transfers between devices: 18.7 us -> 17 us
  blocking collectives: 22.9 us -> 22 us
    ppermute x1, waiting for transfers between devices: 9.35 us -> 5.83 us  [far_slabs(): both = lax.ppermute(block, 'run', rise + fall)]
    ppermute x1, starting transfers between devices: 2.84 us -> 0.52 us  [far_slabs(): both = lax.ppermute(block, 'run', rise + fall)]
    all_to_all x1, waiting for transfers between devices: 0.01 us -> 1.85 us  [local(): planes = lax.all_to_all(planes, 'run', 0, 0, tiled=True)]
    all_to_all x2, blocking collectives: 22.9 us -> 22 us  [everyone(): return lax.all_to_all(lines, PAIR, 0, 0, tiled=True)]
    pallas_call x6 -> x7, Pallas kernels: 11.9 us -> 12 us  [call(): pl.pallas_call(kernel, out_shape=[jax.ShapeDtypeStruct(s, jnp.float32) fo...]
  transfers between devices with their start and end apart: 6 -> 6, of which waited for: 5 -> 6; matrix products, arithmetic and copies ran while one was open for 0% -> 0% of each run, Pallas kernels for 0% -> 0%
where the time goes in v2:
time: 64.9 us; the launch traced here: 64.5 us
  blocking collectives  22 us (34%)
  waiting for transfers between devices  17 us (26%)
  Pallas kernels  12 us (18%)
  starting transfers between devices  10.8 us (17%)
  other arithmetic  1.97 us (3%)
  between operations  0.72 us (1%)
    all_to_all x2, blocking collectives, everyone(): return lax.all_to_all(lines, PAIR, 0, 0, tiled=True)  22 us
    pallas_call x7, Pallas kernels, call(): pl.pallas_call(kernel, out_shape=[jax.ShapeDtypeStruct(s, jnp.float32) fo...  12 us
    ppermute x1, waiting for transfers between devices, local(): high = lax.ppermute(down, 'run', [(i + 1, i) for i in range(count - 1)])  6.55 us
    ppermute x1, waiting for transfers between devices, far_slabs(): both = lax.ppermute(block, 'run', rise + fall)  5.83 us
    ppermute x1, starting transfers between devices, local(): low = lax.ppermute(up, 'run', [(i, i + 1) for i in range(count - 1)])  4.81 us
    all_to_all x1, starting transfers between devices, local(): planes = lax.all_to_all(planes, 'run', 0, 0, tiled=True)  3.68 us
    all_to_all x1, waiting for transfers between devices, local(): planes = lax.all_to_all(planes, 'run', 0, 0, tiled=True)  1.85 us
    ppermute x1, waiting for transfers between devices, local(): other = lax.ppermute(smooth, 'sub', swap)  1.35 us
  transfers between devices with their start and end apart: 6, of which 6 were waited for; matrix products, arithmetic and copies ran while one was open for 0% of the time, Pallas kernels for 0%

profile of v2, /device:TPU:0, one launch (start us, length us, event | category | flops | bytes accessed | tf_op | source)
XLA Modules:
  0.0 64.5 jit_solution(16812294208530728730)
XLA Ops:
  0.6 0.8 %multiply_select_fusion = f32[8,8,128]{2,1,0:T(8,128)S(1)} fusion(f32[8,32,128]{2,1,0:T(8,128)} %density.5, s32[8,32,128]{2,1,0:T(8,128)} %occupancy.5, pred[]{:T(512)S(6)} %eq.12), kind=kLoop, calls=%fused_computation.3 | loop fusion | flops 40960 | bytes 163841 | tf_op jit(solution)/shard_map/jit(_where)/select_n | solution.py:64
  1.5 0.0 copy-start.2
  1.5 0.0 copy-start.3
  1.5 1.1 %slice_select_fusion = (f32[3,8,8,128]{3,2,1,0:T(8,128)S(1)}, f32[3,8,8,128]{3,2,1,0:T(8,128)S(1)}) fusion(f32[3,8,32,128]{3,2,1,0:T(8,128)} %load.1, pred[]{:T(512)S(6)} %eq.12, f32[3,8,32,128]{3,2,1,0:T(8,128)} %guess.1), kind=kLoop, calls=%fused_computation.1 | loop fusion | flops 49152 | bytes 589825 | tf_op jit(solution)/shard_map/jit(_where)/select_n | solution.py:235
  2.6 0.0 copy-start
  2.6 0.0 copy-start.1
  2.7 0.5 collective-permute-start
  3.2 1.1 %collective-permute-done.side = f32[56,8,128]{2,1,0:T(8,128)S(1)} collective-permute-done((f32[56,8,128]{2,1,0:T(8,128)S(1)}, f32[56,8,128]{2,1,0:T(8,128)S(1)}, u32[]{:S(2)}, u32[]{:S(2)}) %collective-permute-start) | collective-permute-done | bytes 229408 | tf_op jit(solution)/shard_map/ppermute | solution.py:519
  4.3 0.0 copy-done.2
  4.3 0.0 copy-done.3
  4.3 0.0 copy-done
  4.3 0.0 copy-done.1
  4.3 2.4 %shard_map.59 = (f32[10,40,128]{2,1,0:T(8,128)S(1)}, f32[8,40,128]{2,1,0:T(8,128)S(1)}, f32[3,8,40,128]{3,2,1,0:T(8,128)S(1)}, f32[3,8,40,128]{3,2,1,0:T(8,128)S...) custom-call(f32[3,8,32,128]{3,2,1,0:T(8,128)S(1)} %copy-done.2, ...), custom_call_target="tpu_custom_call" | custom-call | tf_op jit(solution)/shard_map/pallas_call | solution.py:37
  6.7 4.8 %collective-permute-start.1 = (f32[10,40,128]{2,1,0:T(8,128)S(1)}, f32[10,40,128]{2,1,0:T(8,128)S(1)}, u32[]{:S(2)}, u32[]{:S(2)}) collective-permute-start(f32[10,40,128]{2,1,0:T(8,128)S(1)} %get-tuple-element.18.up), channel_id=1, source_target_pairs={{0,2},{2,4},{4,6},{6,8},{8,10},{10,12},{12,14},{1,3},{3,5},{5,7},{... | collective-permute-start | bytes 614408 | tf_op jit(solution)/shard_map/ppermute | solution.py:531
  11.5 1.3 %collective-permute-start.2 = (f32[8,40,128]{2,1,0:T(8,128)S(1)}, f32[8,40,128]{2,1,0:T(8,128)S(1)}, u32[]{:S(2)}, u32[]{:S(2)}) collective-permute-start(f32[8,40,128]{2,1,0:T(8,128)S(1)} %get-tuple-element.19.down), channel_id=1, source_target_pairs={{2,0},{4,2},{6,4},{8,6},{10,8},{12,10},{14,12},{3,1},{5,3},{7,5},{... | collective-permute-start | bytes 491528 | tf_op jit(solution)/shard_map/ppermute | solution.py:532
  12.8 6.5 %collective-permute-done.2.high = f32[8,40,128]{2,1,0:T(8,128)S(1)} collective-permute-done((f32[8,40,128]{2,1,0:T(8,128)S(1)}, f32[8,40,128]{2,1,0:T(8,128)S(1)}, u32[]{:S(2)}, u32[]{:S(2)}) %collective-permute-start.2) | collective-permute-done | bytes 163872 | tf_op jit(solution)/shard_map/ppermute | solution.py:532
  19.4 0.3 collective-permute-done.1.low
  19.7 4.9 %shard_map.60 = (f32[16,128]{1,0:T(8,128)S(1)}, f32[3,11,40,128]{3,2,1,0:T(8,128)S(1)}, f32[3,9,40,128]{3,2,1,0:T(8,128)S(1)}) custom-call(f32[10,40,128]{2,1,0:T(8,128)S(1)} %get-tuple-element.18.up, f32[8,40,128]{2,1,0:T(8,128)S(1)} %get-tuple-element.19.down, f32[3,8,40,128]{3,2,1,0:T(8,128)S(1)} %get-tuple-element.20.guess_w, ...), custom_call_target="tpu_custom_call" | custom-call | tf_op jit(solution)/shard_map/pallas_call | solution.py:37
  24.6 13.0 %all_to_all.27 = f32[16,1,128]{2,1,0:T(1,128)S(1)} all-to-all(f32[16,1,128]{2,1,0:T(1,128)S(1)} %bitcast.12), channel_id=1, replica_groups=mesh['grp'=2,'run'=8,'sub'=2] {'run','sub'}, dimensions={0} | all-to-all | bytes 16384 | tf_op jit(solution)/shard_map/all_to_all | solution.py:511
  37.6 2.5 %shard_map.61 = (f32[3,8,32,128]{3,2,1,0:T(8,128)}, f32[8,32,128]{2,1,0:T(8,128)S(1)}) custom-call(f32[16,128]{1,0:T(8,128)S(1)} %bitcast.10, f32[3,8,40,128]{3,2,1,0:T(8,128)S(1)} %get-tuple-element.20.guess_w, f32[10,40,128]{2,1,0:T(8,128)S(1)} %collective-permute-done.1.low, f32[3,11,40,128]{3,2,1,0:T(8,128)S(1)} %get-tuple-element.26.first, ...), custom_call_target="tpu_custom_call" | custom-call | tf_op jit(solution)/shard_map/pallas_call | solution.py:37
  40.0 0.0 collective-permute-start.3
  40.0 1.3 %collective-permute-done.3.other = f32[8,32,128]{2,1,0:T(8,128)S(1)} collective-permute-done((f32[8,32,128]{2,1,0:T(8,128)S(1)}, f32[8,32,128]{2,1,0:T(8,128)S(1)}, u32[]{:S(2)}, u32[]{:S(2)}) %collective-permute-start.3) | collective-permute-done | bytes 131104 | tf_op jit(solution)/shard_map/ppermute | solution.py:549
  41.4 1.1 %shard_map.62 = (f32[8,32,128]{2,1,0:T(8,128)S(1)}, f32[8,32,128]{2,1,0:T(8,128)}) custom-call(f32[8,32,128]{2,1,0:T(8,128)S(1)} %get-tuple-element.29.mine, f32[8,32,128]{2,1,0:T(8,128)S(1)} %collective-permute-done.3.other), custom_call_target="tpu_custom_call" | custom-call | tf_op jit(solution)/shard_map/pallas_call | solution.py:37
  42.5 0.5 collective-permute-start.4
  43.0 3.7 %all-to-all-start.1 = ((f32[8,32,128]{2,1,0:T(8,128)}), f32[8,32,128]{2,1,0:T(8,128)S(1)}, u32[]{:S(2)}, u32[]{:S(2)}) async-start(f32[8,32,128]{2,1,0:T(8,128)} %get-tuple-element.31), calls=%async_computation.1 | async-start | bytes 262144 | tf_op jit(solution)/shard_map/all_to_all | solution.py:552
  46.7 5.8 %collective-permute-done.4.below.above = f32[8,32,128]{2,1,0:T(8,128)S(1)} collective-permute-done((f32[8,32,128]{2,1,0:T(8,128)S(1)}, f32[8,32,128]{2,1,0:T(8,128)S(1)}, u32[]{:S(2)}, u32[]{:S(2)}) %collective-permute-start.4) | collective-permute-done | bytes 131104 | tf_op jit(solution)/shard_map/ppermute | solution.py:570
  52.5 0.2 shard_map.63.part
  52.7 1.9 %all-to-all-done.1.planes = f32[8,32,128]{2,1,0:T(8,128)S(1)} async-done(((f32[8,32,128]{2,1,0:T(8,128)}), f32[8,32,128]{2,1,0:T(8,128)S(1)}, u32[]{:S(2)}, u32[]{:S(2)}) %all-to-all-start.1) | async-done | bytes 131104 | tf_op jit(solution)/shard_map/all_to_all | solution.py:552
  54.6 0.2 shard_map.64
  54.7 9.0 %all_to_all.28 = f32[16,1,128]{2,1,0:T(1,128)S(1)} all-to-all(f32[16,1,128]{2,1,0:T(1,128)S(1)} %bitcast.13), channel_id=1, replica_groups=mesh['grp'=2,'run'=8,'sub'=2] {'run','sub'}, dimensions={0} | all-to-all | bytes 16384 | tf_op jit(solution)/shard_map/all_to_all | solution.py:511
  63.7 0.8 %shard_map.65 = f32[8,32,128]{2,1,0:T(8,128)} custom-call(f32[16,128]{1,0:T(8,128)S(1)} %bitcast.11, f32[8,32,128]{2,1,0:T(8,128)S(1)} %get-tuple-element.33.stimulus, s32[8,32,128]{2,1,0:T(8,128)S(1)} %copy-done, f32[8,32,128]{2,1,0:T(8,128)S(1)} %copy-done.1), custom_call_target="tpu_custom_call" | custom-call | tf_op jit(solution)/shard_map/pallas_call | solution.py:37
  (1 shorter events, 0.0 us)
Async XLA Ops:
  1.5 2.8 %copy-start.2 = (f32[3,8,32,128]{3,2,1,0:T(8,128)S(1)}, f32[3,8,32,128]{3,2,1,0:T(8,128)}, u32[]{:S(2)}) copy-start(f32[3,8,32,128]{3,2,1,0:T(8,128)} %load.1) | copy-start | bytes 1179652
  1.5 2.8 %copy-start.3 = (f32[3,8,32,128]{3,2,1,0:T(8,128)S(1)}, f32[3,8,32,128]{3,2,1,0:T(8,128)}, u32[]{:S(2)}) copy-start(f32[3,8,32,128]{3,2,1,0:T(8,128)} %guess.1) | copy-start | bytes 1179652
  2.6 1.7 %copy-start = (s32[8,32,128]{2,1,0:T(8,128)S(1)}, s32[8,32,128]{2,1,0:T(8,128)}, u32[]{:S(2)}) copy-start(s32[8,32,128]{2,1,0:T(8,128)} %occupancy.5) | copy-start | bytes 393220
  2.6 1.7 %copy-start.1 = (f32[8,32,128]{2,1,0:T(8,128)S(1)}, f32[8,32,128]{2,1,0:T(8,128)}, u32[]{:S(2)}) copy-start(f32[8,32,128]{2,1,0:T(8,128)} %density.5) | copy-start | bytes 393220
  2.7 1.6 %collective-permute-start = (f32[56,8,128]{2,1,0:T(8,128)S(1)}, f32[56,8,128]{2,1,0:T(8,128)S(1)}, u32[]{:S(2)}, u32[]{:S(2)}) collective-permute-start(f32[56,8,128]{2,1,0:T(8,128)S(1)} %pad_maximum_fusion), channel_id=1, source_target_pairs={{0,1},{1,0},{2,3},{3,2},{4,5},{5,4},{6,7},{7,6},{8,9},{9,8},{10,11... | collective-permute-start | bytes 688136 | tf_op jit(solution)/shard_map/ppermute | solution.py:519
  6.7 13.0 %collective-permute-start.1 = (f32[10,40,128]{2,1,0:T(8,128)S(1)}, f32[10,40,128]{2,1,0:T(8,128)S(1)}, u32[]{:S(2)}, u32[]{:S(2)}) collective-permute-start(f32[10,40,128]{2,1,0:T(8,128)S(1)} %get-tuple-element.18.up), channel_id=1, source_target_pairs={{0,2},{2,4},{4,6},{6,8},{8,10},{10,12},{12,14},{1,3},{3,5},{5,7},{... | collective-permute-start | bytes 614408 | tf_op jit(solution)/shard_map/ppermute | solution.py:531
  11.5 7.8 %collective-permute-start.2 = (f32[8,40,128]{2,1,0:T(8,128)S(1)}, f32[8,40,128]{2,1,0:T(8,128)S(1)}, u32[]{:S(2)}, u32[]{:S(2)}) collective-permute-start(f32[8,40,128]{2,1,0:T(8,128)S(1)} %get-tuple-element.19.down), channel_id=1, source_target_pairs={{2,0},{4,2},{6,4},{8,6},{10,8},{12,10},{14,12},{3,1},{5,3},{7,5},{... | collective-permute-start | bytes 491528 | tf_op jit(solution)/shard_map/ppermute | solution.py:532
  40.0 1.3 %collective-permute-start.3 = (f32[8,32,128]{2,1,0:T(8,128)S(1)}, f32[8,32,128]{2,1,0:T(8,128)S(1)}, u32[]{:S(2)}, u32[]{:S(2)}) collective-permute-start(f32[8,32,128]{2,1,0:T(8,128)S(1)} %get-tuple-element.29.mine), channel_id=1, source_target_pairs={{0,1},{1,0},{2,3},{3,2},{4,5},{5,4},{6,7},{7,6},{8,9},{9,8},{10,11... | collective-permute-start | bytes 393224 | tf_op jit(solution)/shard_map/ppermute | solution.py:549
  42.5 10.0 %collective-permute-start.4 = (f32[8,32,128]{2,1,0:T(8,128)S(1)}, f32[8,32,128]{2,1,0:T(8,128)S(1)}, u32[]{:S(2)}, u32[]{:S(2)}) collective-permute-start(f32[8,32,128]{2,1,0:T(8,128)S(1)} %get-tuple-element.30.mine), channel_id=1, source_target_pairs={{0,8},{2,10},{4,12},{6,14},{8,0},{10,2},{12,4},{14,6},{1,9},{3,11}... | collective-permute-start | bytes 393224 | tf_op jit(solution)/shard_map/ppermute | solution.py:570
  43.0 11.5 %all-to-all-start.1 = ((f32[8,32,128]{2,1,0:T(8,128)}), f32[8,32,128]{2,1,0:T(8,128)S(1)}, u32[]{:S(2)}, u32[]{:S(2)}) async-start(f32[8,32,128]{2,1,0:T(8,128)} %get-tuple-element.31), calls=%async_computation.1 | async-start | bytes 262144 | tf_op jit(solution)/shard_map/all_to_all | solution.py:552

commit v3 on v2

--- a/solution.py
+++ b/solution.py
@@ -289,7 +289,7 @@
 
 
 def krylov(
-    up, down, guess_w, first_w, mod_w, inverse, square, low, high, row_out, first, second,
+    up, down, guess_w, first_w, mod_w, inverse, square, low, high, planes_in, planes, first, second,
     pair, near, far, mods, inverses, sums,
 ):
     sub = lax.axis_index("sub")
@@ -370,7 +370,10 @@
     line = jnp.zeros((1, 128), jnp.float32)
     for k in range(4):
         line = jnp.where(lane == k, whole(sums[k, own]), line)
-    row_out[...] = jnp.broadcast_to(line, row_out.shape)
+    tile = planes_in[0, 32:40] + jnp.broadcast_to(line, (8, 128))
+    for k in range(planes.shape[0]):
+        planes[k, 0:32] = planes_in[k, 0:32]
+        planes[k, 32:40] = tile
 
 
 def pick(line, k):
@@ -379,11 +382,12 @@
 
 
 def energies(
-    lines, guess_w, low, first, second, occupancy, density, out, smooth, pair, field, specific
+    lines, lines_b, guess_w, low, first, second, occupancy, density, spread,
+    out, smooth, pair, field, specific,
 ):
     sub = lax.axis_index("sub")
     own = pl.ds(pl.multiple_of(8 * sub, 8), 32)
-    line = jnp.sum(lines[...], axis=0, keepdims=True)
+    line = (jnp.sum(lines[...], axis=0) + jnp.sum(lines_b[...], axis=0))[0:1]
     a, b, c, e = (pick(line, k) for k in range(4))
     alpha = a / b
     fresh = alpha * alpha * c - a
@@ -420,15 +424,32 @@
     col = lax.broadcasted_iota(jnp.int32, (128, 128), 1)
     gap = jnp.abs(row - col).astype(jnp.float32)
     band = jnp.where(gap <= REACH, NORM * jnp.exp(gap * (-1.0 / DECAY)), 0.0)
-    smooth[...] = jnp.dot(
+    value = jnp.dot(
         jnp.concatenate(parts, axis=0), band,
         precision=lax.Precision.HIGHEST, preferred_element_type=jnp.float32,
-    ).reshape(smooth.shape)
-
-
-def along_y(mine, other, out, planes):
+    )
+    smooth[0:256] = value
+    total = whole(value * spread[...].reshape(256, 128))
+    smooth[256:264] = jnp.broadcast_to(total, (8, 128))
+
+
+def decayed(block):
+    upward, downward = 0.0, 0.0
+    for k in range(8):
+        upward = upward + math.exp(-(7 - k) / DECAY) * block[k]
+        downward = downward + math.exp(-k / DECAY) * block[k]
+    return upward, downward
+
+
+def ladder(upward, downward, tile, out):
+    run = lax.axis_index("run")
+    for k in range(out.shape[0]):
+        out[k, 0:32] = jnp.where(k > run, upward, downward)
+        out[k, 32:40] = tile
+
+
+def smooth_y(mine, other, planes=8):
     sub = lax.axis_index("sub")
-    run = lax.axis_index("run")
     row = lax.broadcasted_iota(jnp.int32, (32, 32), 0)
     col = lax.broadcasted_iota(jnp.int32, (32, 32), 1)
 
@@ -438,18 +459,38 @@
 
     near = band(0)
     far = band(32 - 64 * sub)
-    upward, downward = 0.0, 0.0
+    for k in range(planes):
+        yield jnp.dot(
+            near, mine(k), precision=lax.Precision.HIGHEST, preferred_element_type=jnp.float32
+        ) + jnp.dot(
+            far, other(k), precision=lax.Precision.HIGHEST, preferred_element_type=jnp.float32
+        )
+
+
+def bone_z(count, bone, below, above, out):
+    blocks = [lambda j, ref=ref: ref[j].astype(jnp.float32) for ref in (bone, below, above)]
+    for i, value in enumerate(far_z(count, *blocks)):
+        out[i] = value
+    out[8], out[9] = decayed([blocks[0](k) for k in range(8)])
+
+
+def bone_y(mine, other, bone, out, planes):
+    block = list(smooth_y(lambda k: mine[k], lambda k: other[k], 10))
     for k in range(8):
-        value = jnp.dot(
-            near, mine[k], precision=lax.Precision.HIGHEST, preferred_element_type=jnp.float32
-        ) + jnp.dot(
-            far, other[k], precision=lax.Precision.HIGHEST, preferred_element_type=jnp.float32
-        )
-        out[k] = value
-        upward = upward + math.exp(-(7 - k) / DECAY) * value
-        downward = downward + math.exp(-k / DECAY) * value
-    for k in range(planes.shape[0]):
-        planes[k] = jnp.where(k > run, upward, downward)
+        out[k] = block[k]
+    lane = lax.broadcasted_iota(jnp.int32, (8, 128), 1)
+    total = whole(jnp.sum(bone[...].astype(jnp.float32), axis=0))
+    ladder(block[8], block[9], jnp.where(lane == 4, total, 0.0), planes)
+
+
+def along_y(mine, other, out, planes):
+    def at(ref):
+        return lambda k: ref[32 * k : 32 * k + 32]
+
+    block = list(smooth_y(at(mine), at(other)))
+    for k in range(8):
+        out[k] = block[k]
+    ladder(*decayed(block), mine[256:264] + other[256:264], planes)
 
 
 def near_z(count, planes, i):
@@ -485,35 +526,24 @@
         out[i] = value
 
 
-def along_z(count, part, planes, occupancy, stimulus, row_out):
-    total, bone = 0.0, 0.0
+def spread_z(count, part, planes, out):
+    for i in range(8):
+        out[i] = part[i] + near_z(count, planes, i)
+
+
+def remodel(count, part, planes, lines, lines_b, bone, density, out):
+    bones = (jnp.sum(lines[...], axis=0) + jnp.sum(lines_b[...], axis=0))[0:1]
+    line = jnp.sum(planes[:, 32:40], axis=0)[0:1]
+    scale = jnp.broadcast_to(pick(bones, 4) / line, density.shape[1:])
     for i in range(8):
         value = part[i] + near_z(count, planes, i)
-        stimulus[i] = value
-        share = occupancy[i].astype(jnp.float32)
-        total = total + share * value
-        bone = bone + share
-    lane = lax.broadcasted_iota(jnp.int32, (1, 128), 1)
-    line = jnp.where(lane == 0, whole(total), jnp.where(lane == 1, whole(bone), 0.0))
-    row_out[...] = jnp.broadcast_to(line, row_out.shape)
-
-
-def remodel(lines, stimulus, occupancy, density, out):
-    line = jnp.sum(lines[...], axis=0, keepdims=True)
-    mean = jnp.broadcast_to(pick(line, 0) / pick(line, 1), stimulus.shape[1:])
-    for k in range(8):
-        rho = density[k]
-        updated = jnp.minimum(rho * (1.0 + RATE * jnp.tanh(SLOPE * (stimulus[k] / mean - 1.0))), 1.0)
-        out[k] = jnp.where(occupancy[k] == 1, updated, rho)
-
-
-def everyone(lines):
-    return lax.all_to_all(lines, PAIR, 0, 0, tiled=True)
+        rho = density[i]
+        updated = jnp.minimum(rho * (1.0 + RATE * jnp.tanh(SLOPE * (value * scale - 1.0))), 1.0)
+        out[i] = jnp.where(bone[i] == 1, updated, rho)
 
 
 def local(load, guess, occupancy, density):
     count = lax.axis_size("run")
-    members = count * lax.axis_size("sub")
     block = density.shape
     swap = [(0, 1), (1, 0)]
     side = lax.ppermute(side_rows(load, guess, occupancy, density), "sub", swap)
@@ -530,34 +560,45 @@
     up, down, guess_w = kept[:3]
     low = lax.ppermute(up, "run", [(i, i + 1) for i in range(count - 1)])
     high = lax.ppermute(down, "run", [(i + 1, i) for i in range(count - 1)])
-    lines, first, second = call(
+    (smooth,) = call(
+        functools.partial(bone_z, count), [(10, 32, 128)], [occupancy, *far_slabs(occupancy)]
+    )
+    spread, planes = call(
+        bone_y,
+        [block, (count, 40, 128)],
+        [smooth, lax.ppermute(smooth, "sub", swap), occupancy],
+    )
+    planes, first, second = call(
         krylov,
-        [(members, 128), (3, 11, ROWS, 128), (3, 9, ROWS, 128)],
-        [*kept, low, high],
+        [(count, 40, 128), (3, 11, ROWS, 128), (3, 9, ROWS, 128)],
+        [*kept, low, high, planes],
         [
             (6, 11, 48, 128), (6, 11, 48, 128), (6, 11, 48, 128),
             (10, ROWS, 128), (9, ROWS, 128), (4, ROWS, 128),
         ],
     )
-    lines = everyone(lines)
+    planes = lax.all_to_all(planes, "run", 0, 0, tiled=True)
+    lines = planes[:, 32:40]
+    lines_b = lax.ppermute(lines, "sub", swap)
+    (spread,) = call(functools.partial(spread_z, count), [block], [spread, planes])
     displacement, smooth = call(
         energies,
-        [guess.shape, block],
-        [lines, guess_w, low, first, second, occupancy, density],
+        [guess.shape, (264, 128)],
+        [lines, lines_b, guess_w, low, first, second, occupancy, density, spread],
         [(6, 9, 48, 128), (3, ROWS, 128), (8, ROWS, 128)],
     )
     other = lax.ppermute(smooth, "sub", swap)
-    smooth, planes = call(along_y, [block, (count, 32, 128)], [smooth, other])
+    smooth, planes = call(along_y, [block, (count, 40, 128)], [smooth, other])
     below, above = far_slabs(smooth)
     planes = lax.all_to_all(planes, "run", 0, 0, tiled=True)
     (part,) = call(
         functools.partial(partial_z, count), [block], [smooth, below, above], flops=10**10
     )
-    stimulus, lines = call(
-        functools.partial(along_z, count), [block, (members, 128)], [part, planes, occupancy]
-    )
-    lines = everyone(lines)
-    (new_density,) = call(remodel, [block], [lines, stimulus, occupancy, density])
+    (new_density,) = call(
+        functools.partial(remodel, count),
+        [block],
+        [part, planes, lines, lines_b, occupancy, density],
+    )
     return displacement, new_density
 
 

time: 64.9 us -> 59.7 us (0.920)
  blocking collectives: 22 us -> 12.2 us
  starting transfers between devices: 10.8 us -> 14 us
  Pallas kernels: 12 us -> 12.8 us
    all_to_all x2 -> x1, blocking collectives: 22 us -> 12.2 us  [local(): planes = lax.all_to_all(planes, 'run', 0, 0, tiled=True)]
    ppermute x1 -> x2, starting transfers between devices: 0.52 us -> 4.6 us  [far_slabs(): both = lax.ppermute(block, 'run', rise + fall)]
    all_to_all x1, waiting for transfers between devices: 1.85 us -> 3.26 us  [local(): planes = lax.all_to_all(planes, 'run', 0, 0, tiled=True)]
    ppermute x1, starting transfers between devices: 4.81 us -> 3.44 us  [local(): low = lax.ppermute(up, 'run', [(i, i + 1) for i in range(count - 1)])]
    ppermute x0 -> x2, waiting for transfers between devices: none -> 1.23 us  [the longest x1 1.15 us: local(): lines_b = lax.ppermute(lines, 'sub', swap)]
    ppermute x1, waiting for transfers between devices: 1.12 us -> 0.01 us  [local(): side = lax.ppermute(side_rows(load, guess, occupancy, density), 'sub', swap)]
    ppermute x1 -> x2, waiting for transfers between devices: 5.83 us -> 4.99 us  [far_slabs(): both = lax.ppermute(block, 'run', rise + fall)]
    pallas_call x7 -> x9, Pallas kernels: 12 us -> 12.8 us  [call(): pl.pallas_call(kernel, out_shape=[jax.ShapeDtypeStruct(s, jnp.float32) fo...]
  transfers between devices with their start and end apart: 6 -> 9, of which waited for: 6 -> 7; matrix products, arithmetic and copies ran while one was open for 0% -> 0% of each run, Pallas kernels for 0% -> 6%
where the time goes in v3:
time: 59.7 us; the launch traced here: 59.3 us
  waiting for transfers between devices  17.2 us (29%)
  starting transfers between devices  14 us (23%)
  Pallas kernels  12.8 us (21%)
  blocking collectives  12.2 us (20%)
  other arithmetic  1.97 us (3%)
  between operations  0.75 us (1%)
    pallas_call x9, Pallas kernels, call(): pl.pallas_call(kernel, out_shape=[jax.ShapeDtypeStruct(s, jnp.float32) fo...  12.8 us
    all_to_all x1, blocking collectives, local(): planes = lax.all_to_all(planes, 'run', 0, 0, tiled=True)  12.2 us
    ppermute x1, waiting for transfers between devices, local(): high = lax.ppermute(down, 'run', [(i + 1, i) for i in range(count - 1)])  6.57 us
    ppermute x2, waiting for transfers between devices, far_slabs(): both = lax.ppermute(block, 'run', rise + fall)  4.99 us
    ppermute x2, starting transfers between devices, far_slabs(): both = lax.ppermute(block, 'run', rise + fall)  4.6 us
    all_to_all x1, starting transfers between devices, local(): planes = lax.all_to_all(planes, 'run', 0, 0, tiled=True)  3.9 us
    ppermute x1, starting transfers between devices, local(): low = lax.ppermute(up, 'run', [(i, i + 1) for i in range(count - 1)])  3.44 us
    all_to_all x1, waiting for transfers between devices, local(): planes = lax.all_to_all(planes, 'run', 0, 0, tiled=True)  3.26 us
  transfers between devices with their start and end apart: 9, of which 7 were waited for; matrix products, arithmetic and copies ran while one was open for 0% of the time, Pallas kernels for 6%

profile of v3, /device:TPU:0, one launch (start us, length us, event | category | flops | bytes accessed | tf_op | source)
XLA Modules:
  0.0 59.3 jit_solution(9438878127946867603)
XLA Ops:
  0.6 0.8 %multiply_select_fusion = f32[8,8,128]{2,1,0:T(8,128)S(1)} fusion(f32[8,32,128]{2,1,0:T(8,128)} %density.5, s32[8,32,128]{2,1,0:T(8,128)} %bone.7, pred[]{:T(512)S(6)} %eq.12), kind=kLoop, calls=%fused_computation.3 | loop fusion | flops 40960 | bytes 163841 | tf_op jit(solution)/shard_map/jit(_where)/select_n | solution.py:64
  1.5 0.0 copy-start.2
  1.5 0.0 copy-start.3
  1.5 1.1 %slice_select_fusion = (f32[3,8,8,128]{3,2,1,0:T(8,128)S(1)}, f32[3,8,8,128]{3,2,1,0:T(8,128)S(1)}) fusion(f32[3,8,32,128]{3,2,1,0:T(8,128)} %load.1, pred[]{:T(512)S(6)} %eq.12, f32[3,8,32,128]{3,2,1,0:T(8,128)} %guess.1), kind=kLoop, calls=%fused_computation.1 | loop fusion | flops 49152 | bytes 589825 | tf_op jit(solution)/shard_map/jit(_where)/select_n | solution.py:235
  2.6 0.0 copy-start
  2.6 0.0 copy-start.1
  2.7 0.5 collective-permute-start
  3.2 0.3 copy-done
  3.5 4.0 %collective-permute-start.3 = (s32[8,32,128]{2,1,0:T(8,128)S(1)}, s32[8,32,128]{2,1,0:T(8,128)S(1)}, u32[]{:S(2)}, u32[]{:S(2)}) collective-permute-start(s32[8,32,128]{2,1,0:T(8,128)S(1)} %copy-done), channel_id=1, source_target_pairs={{0,8},{2,10},{4,12},{6,14},{8,0},{10,2},{12,4},{14,6},{1,9},{3,11}... | collective-permute-start | bytes 393224 | tf_op jit(solution)/shard_map/ppermute | solution.py:611
  7.6 0.0 collective-permute-done.side
  7.6 0.0 copy-done.2
  7.6 0.0 copy-done.3
  7.6 0.0 copy-done.1
  7.6 2.4 %shard_map.59 = (f32[10,40,128]{2,1,0:T(8,128)S(1)}, f32[8,40,128]{2,1,0:T(8,128)S(1)}, f32[3,8,40,128]{3,2,1,0:T(8,128)S(1)}, f32[3,8,40,128]{3,2,1,0:T(8,128)S...) custom-call(f32[3,8,32,128]{3,2,1,0:T(8,128)S(1)} %copy-done.2, ...), custom_call_target="tpu_custom_call" | custom-call | tf_op jit(solution)/shard_map/pallas_call | solution.py:37
  10.0 3.4 %collective-permute-start.1 = (f32[10,40,128]{2,1,0:T(8,128)S(1)}, f32[10,40,128]{2,1,0:T(8,128)S(1)}, u32[]{:S(2)}, u32[]{:S(2)}) collective-permute-start(f32[10,40,128]{2,1,0:T(8,128)S(1)} %get-tuple-element.18.up), channel_id=1, source_target_pairs={{0,2},{2,4},{4,6},{6,8},{8,10},{10,12},{12,14},{1,3},{3,5},{5,7},{... | collective-permute-start | bytes 614408 | tf_op jit(solution)/shard_map/ppermute | solution.py:561
  13.4 0.5 collective-permute-done.3.below.above
  13.9 0.2 shard_map.60.mine
  14.1 0.1 collective-permute-start.4
  14.2 1.3 %collective-permute-start.2 = (f32[8,40,128]{2,1,0:T(8,128)S(1)}, f32[8,40,128]{2,1,0:T(8,128)S(1)}, u32[]{:S(2)}, u32[]{:S(2)}) collective-permute-start(f32[8,40,128]{2,1,0:T(8,128)S(1)} %get-tuple-element.19.down), channel_id=1, source_target_pairs={{2,0},{4,2},{6,4},{8,6},{10,8},{12,10},{14,12},{3,1},{5,3},{7,5},{... | collective-permute-start | bytes 491528 | tf_op jit(solution)/shard_map/ppermute | solution.py:562
  15.5 0.1 collective-permute-done.4.other
  15.6 0.5 shard_map.61
  16.1 6.6 %collective-permute-done.2.high = f32[8,40,128]{2,1,0:T(8,128)S(1)} collective-permute-done((f32[8,40,128]{2,1,0:T(8,128)S(1)}, f32[8,40,128]{2,1,0:T(8,128)S(1)}, u32[]{:S(2)}, u32[]{:S(2)}) %collective-permute-start.2) | collective-permute-done | bytes 163872 | tf_op jit(solution)/shard_map/ppermute | solution.py:562
  22.7 0.0 collective-permute-done.1.low
  22.7 4.9 %shard_map.62 = (f32[8,40,128]{2,1,0:T(8,128)S(1)}, f32[3,11,40,128]{3,2,1,0:T(8,128)S(1)}, f32[3,9,40,128]{3,2,1,0:T(8,128)S(1)}) custom-call(f32[10,40,128]{2,1,0:T(8,128)S(1)} %get-tuple-element.18.up, f32[8,40,128]{2,1,0:T(8,128)S(1)} %get-tuple-element.19.down, f32[3,8,40,128]{3,2,1,0:T(8,128)S(1)} %get-tuple-element.20.guess_w, ...), custom_call_target="tpu_custom_call" | custom-call | tf_op jit(solution)/shard_map/pallas_call | solution.py:37
  27.6 12.2 %all_to_all.10.planes = f32[8,40,128]{2,1,0:T(8,128)S(1)} all-to-all(f32[8,40,128]{2,1,0:T(8,128)S(1)} %get-tuple-element.26), channel_id=1, replica_groups=mesh['grp'=2,'run'=8,'sub'=2] {'run'}, dimensions={0} | all-to-all | bytes 327680 | tf_op jit(solution)/shard_map/all_to_all | solution.py:580
  39.8 0.0 collective-permute-start.5
  39.8 1.1 %collective-permute-done.5.lines_b = f32[8,8,128]{2,1,0:T(8,128)S(1)} collective-permute-done((f32[8,8,128]{2,1,0:T(8,128)S(1)}, f32[8,8,128]{2,1,0:T(8,128)S(1)}, u32[]{:S(2)}, u32[]{:S(2)}) %collective-permute-start.5) | collective-permute-done | bytes 32800 | tf_op jit(solution)/shard_map/ppermute | solution.py:582
  41.0 2.6 %shard_map.64 = (f32[3,8,32,128]{3,2,1,0:T(8,128)}, f32[264,128]{1,0:T(8,128)S(1)}) custom-call(f32[8,8,128]{2,1,0:T(8,128)S(1)} %slice.36.lines, f32[8,8,128]{2,1,0:T(8,128)S(1)} %collective-permute-done.5.lines_b, f32[3,8,40,128]{3,2,1,0:T(8,128)S(1)} %get-tuple-element.20.guess_w, f32[10,40,128]{2,1,0:T(8,128)S(1)} %collective-permute-done.1.low, ...), custom_call_target="tpu_custom_call" | custom-call | tf_op jit(solution)/shard_map/pallas_call | solution.py:37
  43.6 0.2 collective-permute-start.6
  43.8 1.2 %collective-permute-done.6.other = f32[264,128]{1,0:T(8,128)S(1)} collective-permute-done((f32[264,128]{1,0:T(8,128)S(1)}, f32[264,128]{1,0:T(8,128)S(1)}, u32[]{:S(2)}, u32[]{:S(2)}) %collective-permute-start.6) | collective-permute-done | bytes 135200 | tf_op jit(solution)/shard_map/ppermute | solution.py:590
  45.0 1.1 %shard_map.65 = (f32[8,32,128]{2,1,0:T(8,128)S(1)}, f32[8,40,128]{2,1,0:T(8,128)}) custom-call(f32[264,128]{1,0:T(8,128)S(1)} %get-tuple-element.31.mine, f32[264,128]{1,0:T(8,128)S(1)} %collective-permute-done.6.other), custom_call_target="tpu_custom_call" | custom-call | tf_op jit(solution)/shard_map/pallas_call | solution.py:37
  46.1 0.6 collective-permute-start.7
  46.7 3.9 %all-to-all-start.1 = ((f32[8,40,128]{2,1,0:T(8,128)}), f32[8,40,128]{2,1,0:T(8,128)S(1)}, u32[]{:S(2)}, u32[]{:S(2)}) async-start(f32[8,40,128]{2,1,0:T(8,128)} %get-tuple-element.33), calls=%async_computation.1 | async-start | bytes 327680 | tf_op jit(solution)/shard_map/all_to_all | solution.py:593
  50.6 4.5 %collective-permute-done.7.below.above = f32[8,32,128]{2,1,0:T(8,128)S(1)} collective-permute-done((f32[8,32,128]{2,1,0:T(8,128)S(1)}, f32[8,32,128]{2,1,0:T(8,128)S(1)}, u32[]{:S(2)}, u32[]{:S(2)}) %collective-permute-start.7) | collective-permute-done | bytes 131104 | tf_op jit(solution)/shard_map/ppermute | solution.py:611
  55.1 0.2 shard_map.66.part
  55.3 3.3 %all-to-all-done.1.planes = f32[8,40,128]{2,1,0:T(8,128)S(1)} async-done(((f32[8,40,128]{2,1,0:T(8,128)}), f32[8,40,128]{2,1,0:T(8,128)S(1)}, u32[]{:S(2)}, u32[]{:S(2)}) %all-to-all-start.1) | async-done | bytes 163872 | tf_op jit(solution)/shard_map/all_to_all | solution.py:593
  58.5 0.8 %shard_map.67 = f32[8,32,128]{2,1,0:T(8,128)} custom-call(f32[8,32,128]{2,1,0:T(8,128)S(1)} %shard_map.66.part, f32[8,40,128]{2,1,0:T(8,128)S(1)} %all-to-all-done.1.planes, f32[8,8,128]{2,1,0:T(8,128)S(1)} %slice.36.lines, f32[8,8,128]{2,1,0:T(8,128)S(1)} %collective-permute-done.5.lines_b, s32[8,32,128]{2,1,0:T(8,128)S(1)} %copy-done, ...), custom_call_target="tpu_custom_call" | custom-call | tf_op jit(solution)/shard_map/pallas_call | solution.py:37
  (3 shorter events, 0.1 us)
Async XLA Ops:
  1.5 6.1 %copy-start.2 = (f32[3,8,32,128]{3,2,1,0:T(8,128)S(1)}, f32[3,8,32,128]{3,2,1,0:T(8,128)}, u32[]{:S(2)}) copy-start(f32[3,8,32,128]{3,2,1,0:T(8,128)} %load.1) | copy-start | bytes 1179652
  1.5 6.1 %copy-start.3 = (f32[3,8,32,128]{3,2,1,0:T(8,128)S(1)}, f32[3,8,32,128]{3,2,1,0:T(8,128)}, u32[]{:S(2)}) copy-start(f32[3,8,32,128]{3,2,1,0:T(8,128)} %guess.1) | copy-start | bytes 1179652
  2.6 0.9 %copy-start = (s32[8,32,128]{2,1,0:T(8,128)S(1)}, s32[8,32,128]{2,1,0:T(8,128)}, u32[]{:S(2)}) copy-start(s32[8,32,128]{2,1,0:T(8,128)} %bone.7) | copy-start | bytes 393220
  2.6 4.9 %copy-start.1 = (f32[8,32,128]{2,1,0:T(8,128)S(1)}, f32[8,32,128]{2,1,0:T(8,128)}, u32[]{:S(2)}) copy-start(f32[8,32,128]{2,1,0:T(8,128)} %density.5) | copy-start | bytes 393220
  2.7 4.9 %collective-permute-start = (f32[56,8,128]{2,1,0:T(8,128)S(1)}, f32[56,8,128]{2,1,0:T(8,128)S(1)}, u32[]{:S(2)}, u32[]{:S(2)}) collective-permute-start(f32[56,8,128]{2,1,0:T(8,128)S(1)} %pad_maximum_fusion), channel_id=1, source_target_pairs={{0,1},{1,0},{2,3},{3,2},{4,5},{5,4},{6,7},{7,6},{8,9},{9,8},{10,11... | collective-permute-start | bytes 688136 | tf_op jit(solution)/shard_map/ppermute | solution.py:549
  3.5 10.3 %collective-permute-start.3 = (s32[8,32,128]{2,1,0:T(8,128)S(1)}, s32[8,32,128]{2,1,0:T(8,128)S(1)}, u32[]{:S(2)}, u32[]{:S(2)}) collective-permute-start(s32[8,32,128]{2,1,0:T(8,128)S(1)} %copy-done), channel_id=1, source_target_pairs={{0,8},{2,10},{4,12},{6,14},{8,0},{10,2},{12,4},{14,6},{1,9},{3,11}... | collective-permute-start | bytes 393224 | tf_op jit(solution)/shard_map/ppermute | solution.py:611
  10.0 12.7 %collective-permute-start.1 = (f32[10,40,128]{2,1,0:T(8,128)S(1)}, f32[10,40,128]{2,1,0:T(8,128)S(1)}, u32[]{:S(2)}, u32[]{:S(2)}) collective-permute-start(f32[10,40,128]{2,1,0:T(8,128)S(1)} %get-tuple-element.18.up), channel_id=1, source_target_pairs={{0,2},{2,4},{4,6},{6,8},{8,10},{10,12},{12,14},{1,3},{3,5},{5,7},{... | collective-permute-start | bytes 614408 | tf_op jit(solution)/shard_map/ppermute | solution.py:561
  14.1 1.5 %collective-permute-start.4 = (f32[10,32,128]{2,1,0:T(8,128)S(1)}, f32[10,32,128]{2,1,0:T(8,128)S(1)}, u32[]{:S(2)}, u32[]{:S(2)}) collective-permute-start(f32[10,32,128]{2,1,0:T(8,128)S(1)} %shard_map.60.mine), channel_id=1, source_target_pairs={{0,1},{1,0},{2,3},{3,2},{4,5},{5,4},{6,7},{7,6},{8,9},{9,8},{10,11... | collective-permute-start | bytes 491528 | tf_op jit(solution)/shard_map/ppermute | solution.py:569
  14.2 8.5 %collective-permute-start.2 = (f32[8,40,128]{2,1,0:T(8,128)S(1)}, f32[8,40,128]{2,1,0:T(8,128)S(1)}, u32[]{:S(2)}, u32[]{:S(2)}) collective-permute-start(f32[8,40,128]{2,1,0:T(8,128)S(1)} %get-tuple-element.19.down), channel_id=1, source_target_pairs={{2,0},{4,2},{6,4},{8,6},{10,8},{12,10},{14,12},{3,1},{5,3},{7,5},{... | collective-permute-start | bytes 491528 | tf_op jit(solution)/shard_map/ppermute | solution.py:562
  39.8 1.2 %collective-permute-start.5 = (f32[8,8,128]{2,1,0:T(8,128)S(1)}, f32[8,8,128]{2,1,0:T(8,128)S(1)}, u32[]{:S(2)}, u32[]{:S(2)}) collective-permute-start(f32[8,8,128]{2,1,0:T(8,128)S(1)} %slice.36.lines), channel_id=1, source_target_pairs={{0,1},{1,0},{2,3},{3,2},{4,5},{5,4},{6,7},{7,6},{8,9},{9,8},{10,11... | collective-permute-start | bytes 98312 | tf_op jit(solution)/shard_map/ppermute | solution.py:582
  43.6 1.4 %collective-permute-start.6 = (f32[264,128]{1,0:T(8,128)S(1)}, f32[264,128]{1,0:T(8,128)S(1)}, u32[]{:S(2)}, u32[]{:S(2)}) collective-permute-start(f32[264,128]{1,0:T(8,128)S(1)} %get-tuple-element.31.mine), channel_id=1, source_target_pairs={{0,1},{1,0},{2,3},{3,2},{4,5},{5,4},{6,7},{7,6},{8,9},{9,8},{10,11... | collective-permute-start | bytes 405512 | tf_op jit(solution)/shard_map/ppermute | solution.py:590
  46.1 9.0 %collective-permute-start.7 = (f32[8,32,128]{2,1,0:T(8,128)S(1)}, f32[8,32,128]{2,1,0:T(8,128)S(1)}, u32[]{:S(2)}, u32[]{:S(2)}) collective-permute-start(f32[8,32,128]{2,1,0:T(8,128)S(1)} %get-tuple-element.32.mine), channel_id=1, source_target_pairs={{0,8},{2,10},{4,12},{6,14},{8,0},{10,2},{12,4},{14,6},{1,9},{3,11}... | collective-permute-start | bytes 393224 | tf_op jit(solution)/shard_map/ppermute | solution.py:611
  46.7 11.9 %all-to-all-start.1 = ((f32[8,40,128]{2,1,0:T(8,128)}), f32[8,40,128]{2,1,0:T(8,128)S(1)}, u32[]{:S(2)}, u32[]{:S(2)}) async-start(f32[8,40,128]{2,1,0:T(8,128)} %get-tuple-element.33), calls=%async_computation.1 | async-start | bytes 327680 | tf_op jit(solution)/shard_map/all_to_all | solution.py:593

commit v4 on v3

--- a/solution.py
+++ b/solution.py
@@ -88,6 +88,11 @@
 
 
 def steps(count, body, carry):
+    if count <= 3:
+        for k in range(count):
+            carry = body(k, carry)
+        return carry
+
     def turn(k, carry):
         return body(2 * k + 1, body(2 * k, carry))
 
@@ -137,15 +142,15 @@
     return columns[0] + columns[1] + lane_left(columns[0] - columns[1])
 
 
-def energy_march(pair, count, use):
+def energy_march(pair, start, count, use):
     for tile in range(ROWS // 8):
 
         def body(k, low):
-            high = plane_modes(pair, k + 1, tile)
+            high = plane_modes(pair, start + k + 1, tile)
             use(k, tile, quadratic(modes_of(low, high)))
             return high
 
-        steps(count, body, plane_modes(pair, 0, tile))
+        steps(count, body, plane_modes(pair, start, tile))
 
 
 def inverted(low, high):
@@ -238,23 +243,80 @@
     )
 
 
-def inner(
-    load, guess, bone, density, side, up, down, guess_w, first_w, mod_w, inverse, square,
-    pair, near, far,
-):
-    sub = lax.axis_index("sub")
+def windows(sub, load, guess, bone, density, side):
     own = pl.ds(pl.multiple_of(8 * sub, 8), 32)
     rest = pl.ds(pl.multiple_of(32 * (1 - sub), 8), 8)
+
+    def put_guess(out, at, c, k):
+        out[c, at, own] = guess[c, k]
+        out[c, at, rest] = side[8 * c + k]
+
+    def put_load(out, at, c, k):
+        out[c, at, own] = load[c, k]
+        out[c, at, rest] = side[24 + 8 * c + k]
+
+    def put_mod(out, at, k):
+        out[at, own] = stiff(bone[k], density[k])
+        out[at, rest] = side[48 + k]
+
+    return put_guess, put_load, put_mod
+
+
+def blank(pair, far):
     clear(pair)
-    far[:, :, ROWS : ROWS + 8] = jnp.zeros((6, 8, 8, 128), jnp.float32)
+    for m in range(6):
+        for k in range(far.shape[1]):
+            far[m, k, ROWS : ROWS + 8] = jnp.zeros((8, 128), jnp.float32)
+
+
+def edge(
+    load, guess, bone, density, side, up, down, guess_w, load_w, mods, pair, near, far
+):
+    put_guess, put_load, put_mod = windows(
+        lax.axis_index("sub"), load, guess, bone, density, side
+    )
+    blank(pair, far)
+    for at, k in enumerate((0, 1, 6, 7)):
+        put_mod(mods, at, k)
+    for c in range(3):
+        for at, k in enumerate((0, 6, 7)):
+            put_load(load_w, at, c, k)
+        for at, k in enumerate((0, 1, 5, 6, 7)):
+            put_guess(guess_w, at, c, k)
+            enter(pair, at, c, guess_w[c, at])
+    march(pair, 0, 1, lambda k, rows: mods[1, rows], near, far, 0)
+    march(pair, 2, 2, lambda k, rows: mods[2 + k, rows], near, far, 2)
+    inverse = inverted(mods[2], mods[3])
+    for c in range(3):
+        down[c] = guess_w[c, 0]
+        down[3 + c] = load_w[c, 0] - image(near, far, 0, c)
+        up[c] = guess_w[c, 4]
+        up[3 + c] = load_w[c, 2] - image(near, far, 4, c)
+        up[6 + c] = (load_w[c, 1] - image(near, far, 3, c)) * inverse
+    up[9] = mods[3]
+    down[6] = mods[0]
+    down[7] = inverted(mods[0], mods[1])
+
+
+def middle(
+    count, load, guess, bone, density, side, bone_below, bone_above,
+    smooth, guess_w, mod_w, inverse, inner_z, inner_s, near_m, far_m, sums,
+    load_w, pair, near, far, pair_z, pair_s,
+):
+    put_guess, put_load, put_mod = windows(
+        lax.axis_index("sub"), load, guess, bone, density, side
+    )
+    bone_z(count, bone, bone_below, bone_above, smooth)
+    blank(pair, far)
+    blank(pair_z, far_m)
+    clear(pair_s)
     for k in range(8):
-        mod_w[k, own] = stiff(bone[k], density[k])
-        mod_w[k, rest] = side[48 + k]
+        put_mod(mod_w, k, k)
         for c in range(3):
-            guess_w[c, k, own] = guess[c, k]
-            guess_w[c, k, rest] = side[8 * c + k]
-            first_w[c, k, own] = load[c, k]
-            first_w[c, k, rest] = side[24 + 8 * c + k]
+            put_guess(guess_w, k, c, k)
+            put_load(load_w, k, c, k)
+    for k in range(7):
+        inverse[k] = inverted(mod_w[k], mod_w[k + 1])
 
     def prepare(k, _):
         for c in range(3):
@@ -262,49 +324,62 @@
         return 0
 
     lax.fori_loop(0, 8, prepare, 0)
-    for k in range(7):
-        inverse[k] = inverted(mod_w[k], mod_w[k + 1])
     march(pair, 0, 7, lambda k, rows: mod_w[k + 1, rows], near, far, 0)
-    square[...] = jnp.zeros_like(square)
-
-    def settle(k, _):
+    sums[...] = jnp.zeros_like(sums)
+
+    def settle_z(k, _):
+        dot = 0.0
         for c in range(3):
-            residual = first_w[c, k] - image(near, far, k, c)
+            residual = load_w[c, k] - image(near, far, k, c)
             z = residual * inverse[k]
-            first_w[c, k] = z
-            square[...] += residual * z
+            inner_z[c, k - 1] = z
+            enter(pair_z, k - 1, c, z)
+            dot = dot + residual * z
+        sums[0] += dot
         return 0
 
-    for c in range(3):
-        down[3 + c] = first_w[c, 0] - image(near, far, 0, c)
-        up[3 + c] = first_w[c, 7] - image(near, far, 7, c)
-    lax.fori_loop(1, 7, settle, 0)
-    for c in range(3):
-        down[c] = guess_w[c, 0]
-        up[c] = guess_w[c, 7]
-        up[6 + c] = first_w[c, 6]
-    up[9] = mod_w[7]
-    down[6] = mod_w[0]
-    down[7] = inverse[0]
+    lax.fori_loop(1, 7, settle_z, 0)
+    march(pair_z, 0, 5, lambda k, rows: mod_w[k + 2, rows], near_m, far_m, 0)
+
+    def settle_s(k, _):
+        dot, cross = 0.0, 0.0
+        for c in range(3):
+            w = image(near_m, far_m, k - 1, c)
+            s = w * inverse[k]
+            inner_s[c, k - 2] = s
+            enter(pair_s, k - 2, c, s)
+            dot = dot + w * inner_z[c, k - 1]
+            cross = cross + w * s
+        sums[1] += dot
+        sums[2] += cross
+        return 0
+
+    lax.fori_loop(2, 6, settle_s, 0)
+
+    def use(k, tile, value):
+        rows = slice(8 * tile, 8 * tile + 8)
+        sums[3, rows] += value * mod_w[k + 3, rows]
+
+    energy_march(pair_s, 0, 3, use)
 
 
 def krylov(
-    up, down, guess_w, first_w, mod_w, inverse, square, low, high, planes_in, planes, first, second,
-    pair, near, far, mods, inverses, sums,
+    up, down, guess_w, mod_w, inverse, inner_z, inner_s, near_m, far_m, sums_in, low, high,
+    row_out, first, second, pair, near, far, mods, sums,
 ):
     sub = lax.axis_index("sub")
     run = lax.axis_index("run")
     own = pl.ds(pl.multiple_of(8 * sub, 8), 32)
-    clear(pair)
-    far[:, :, ROWS : ROWS + 8] = jnp.zeros((6, 11, 8, 128), jnp.float32)
+    blank(pair, far)
+    sums[...] = sums_in[...]
     mods[0] = low[9]
-    mods[9] = high[6]
-    for k in range(8):
+    for k in range(3):
         mods[1 + k] = mod_w[k]
-    inverses[0] = jnp.where(run > 0, inverted(low[9], mod_w[0]), 0.0)
-    for k in range(7):
-        inverses[1 + k] = inverse[k]
-    inverses[8] = inverted(mod_w[7], high[6])
+    for k in range(2):
+        mods[4 + k] = mod_w[6 + k]
+    mods[6] = high[6]
+    bottom = jnp.where(run > 0, inverted(low[9], mod_w[0]), 0.0)
+    top = inverted(mod_w[7], high[6])
 
     for c in range(3):
         enter(pair, 0, c, low[c])
@@ -312,11 +387,11 @@
         enter(pair, 2, c, guess_w[c, 7])
         enter(pair, 3, c, high[c])
     march(pair, 0, 1, lambda k, rows: mods[1, rows], near, far, 0)
-    march(pair, 2, 1, lambda k, rows: mods[9, rows], near, far, 2)
+    march(pair, 2, 1, lambda k, rows: mods[6, rows], near, far, 2)
     begun = (low, down, up, high)
-    invert = (inverses[0], inverses[1], inverses[8], high[7])
-    sums[...] = jnp.zeros_like(sums)
-    dot = square[...]
+    invert = (bottom, inverse[0], top, high[7])
+    dot = 0.0
+    ends = []
     for c in range(3):
         values = []
         for k in range(4):
@@ -325,55 +400,61 @@
             values.append(z)
             if k in (1, 2):
                 dot = dot + residual * z
-        first[c, 0] = low[6 + c]
-        first[c, 1] = values[0]
-        first[c, 2] = values[1]
-        for k in range(1, 7):
-            first[c, 2 + k] = first_w[c, k]
-        first[c, 9] = values[2]
-        first[c, 10] = values[3]
-    sums[0] = dot
-
-    def prepare(k, _):
-        for c in range(3):
-            enter(pair, k, c, first[c, k])
-        return 0
-
-    lax.fori_loop(0, 11, prepare, 0)
-    march(pair, 0, 10, lambda k, rows: mods[k, rows], near, far, 0)
-
-    def settle(k, _):
-        dot, cross = 0.0, 0.0
-        for c in range(3):
-            w = image(near, far, k + 1, c)
-            s = w * inverses[k]
-            second[c, k] = s
-            enter(pair, k, c, s)
-            dot = dot + w * first[c, k + 1]
-            cross = cross + w * s
-
-        @pl.when(k >= 1)
-        def _():
-            sums[1] += dot
-            sums[2] += cross
-
-        return 0
-
-    lax.fori_loop(0, 9, settle, 0)
-
-    def use(k, tile, value):
-        rows = slice(8 * tile, 8 * tile + 8)
-        sums[3, rows] += value * mods[k + 1, rows]
-
-    energy_march(pair, 8, use)
+        first[c, 0] = values[0]
+        first[c, 1] = values[1]
+        for k in range(6):
+            first[c, 2 + k] = inner_z[c, k]
+        first[c, 8] = values[2]
+        ends.append(values[3])
+    sums[0] += dot
+
+    for c in range(3):
+        enter(pair, 0, c, low[6 + c])
+        for k in range(3):
+            enter(pair, 1 + k, c, first[c, k])
+        enter(pair, 4, c, first[c, 7])
+        enter(pair, 5, c, first[c, 8])
+        enter(pair, 6, c, ends[c])
+    march(pair, 0, 3, lambda k, rows: mods[k, rows], near, far, 0)
+    march(pair, 4, 2, lambda k, rows: mods[5 + k, rows], near, far, 4)
+    dot, cross = 0.0, 0.0
+    for c in range(3):
+        images = {
+            -1: image(near, far, 1, c),
+            0: image(near, far, 2, c),
+            1: image(near, far, 3, c) + image(near_m, far_m, 0, c),
+            6: image(near, far, 4, c) + image(near_m, far_m, 5, c),
+            7: image(near, far, 5, c),
+        }
+        for k, w in images.items():
+            s = w * (bottom if k < 0 else top if k == 7 else inverse[k])
+            second[c, k + 1] = s
+            if k >= 0:
+                dot = dot + w * first[c, k + 1]
+                cross = cross + w * s
+        for k in range(2, 6):
+            second[c, k + 1] = inner_s[c, k - 2]
+    sums[1] += dot
+    sums[2] += cross
+
+    for c in range(3):
+        for at, k in enumerate((-1, 0, 1, 2, 5, 6, 7)):
+            enter(pair, at, c, second[c, k + 1])
+
+    def use(first_mod):
+        def add(k, tile, value):
+            rows = slice(8 * tile, 8 * tile + 8)
+            sums[3, rows] += value * mods[first_mod + k, rows]
+
+        return add
+
+    energy_march(pair, 0, 3, use(1))
+    energy_march(pair, 4, 2, use(4))
     lane = lax.broadcasted_iota(jnp.int32, (1, 128), 1)
     line = jnp.zeros((1, 128), jnp.float32)
     for k in range(4):
         line = jnp.where(lane == k, whole(sums[k, own]), line)
-    tile = planes_in[0, 32:40] + jnp.broadcast_to(line, (8, 128))
-    for k in range(planes.shape[0]):
-        planes[k, 0:32] = planes_in[k, 0:32]
-        planes[k, 32:40] = tile
+    row_out[...] = jnp.broadcast_to(line, row_out.shape)
 
 
 def pick(line, k):
@@ -398,11 +479,11 @@
     q = jnp.broadcast_to(-after * alpha, (ROWS, 128))
     clear(pair)
     for c in range(3):
-        enter(pair, 0, c, low[c] + p * first[c, 1] + q * second[c, 0])
+        enter(pair, 0, c, low[c] + p * first[c, 0] + q * second[c, 0])
 
     def advance(k, _):
         for c in range(3):
-            value = guess_w[c, k] + p * first[c, k + 2] + q * second[c, k + 1]
+            value = guess_w[c, k] + p * first[c, k + 1] + q * second[c, k + 1]
             field[c] = value
             enter(pair, k + 1, c, value)
         for c in range(3):
@@ -414,7 +495,7 @@
     def use(k, tile, value):
         specific[k, 8 * tile : 8 * tile + 8] = value
 
-    energy_march(pair, 8, use)
+    energy_march(pair, 0, 8, use)
     parts = []
     for k in range(8):
         rho = density[k]
@@ -474,13 +555,13 @@
     out[8], out[9] = decayed([blocks[0](k) for k in range(8)])
 
 
-def bone_y(mine, other, bone, out, planes):
+def bone_y(mine, other, bone, line, out, planes):
     block = list(smooth_y(lambda k: mine[k], lambda k: other[k], 10))
     for k in range(8):
         out[k] = block[k]
     lane = lax.broadcasted_iota(jnp.int32, (8, 128), 1)
     total = whole(jnp.sum(bone[...].astype(jnp.float32), axis=0))
-    ladder(block[8], block[9], jnp.where(lane == 4, total, 0.0), planes)
+    ladder(block[8], block[9], jnp.where(lane == 4, total, line[...]), planes)
 
 
 def along_y(mine, other, out, planes):
@@ -547,35 +628,46 @@
     block = density.shape
     swap = [(0, 1), (1, 0)]
     side = lax.ppermute(side_rows(load, guess, occupancy, density), "sub", swap)
-    wide = (3, 8, ROWS, 128)
-    kept = call(
-        inner,
+    inputs = [load, guess, occupancy, density, side]
+    up, down = call(
+        edge,
+        [(10, ROWS, 128), (8, ROWS, 128)],
+        inputs,
         [
-            (10, ROWS, 128), (8, ROWS, 128), wide, wide,
-            (8, ROWS, 128), (7, ROWS, 128), (ROWS, 128),
+            (3, 5, ROWS, 128), (3, 3, ROWS, 128), (4, ROWS, 128),
+            (6, 5, 48, 128), (6, 5, ROWS, 128), (6, 5, 48, 128),
         ],
-        [load, guess, occupancy, density, side],
-        [(6, 8, 48, 128), (6, 8, 48, 128), (6, 8, 48, 128)],
-    )
-    up, down, guess_w = kept[:3]
+    )
     low = lax.ppermute(up, "run", [(i, i + 1) for i in range(count - 1)])
     high = lax.ppermute(down, "run", [(i + 1, i) for i in range(count - 1)])
-    (smooth,) = call(
-        functools.partial(bone_z, count), [(10, 32, 128)], [occupancy, *far_slabs(occupancy)]
+    smooth, *kept = call(
+        functools.partial(middle, count),
+        [
+            (10, 32, 128),
+            (3, 8, ROWS, 128), (8, ROWS, 128), (7, ROWS, 128),
+            (3, 6, ROWS, 128), (3, 4, ROWS, 128),
+            (6, 6, ROWS, 128), (6, 6, 48, 128), (4, ROWS, 128),
+        ],
+        [*inputs, *far_slabs(occupancy)],
+        [
+            (3, 8, ROWS, 128), (6, 8, 48, 128), (6, 8, ROWS, 128), (6, 8, 48, 128),
+            (6, 6, 48, 128), (6, 4, 48, 128),
+        ],
+    )
+    guess_w = kept[0]
+    line, first, second = call(
+        krylov,
+        [(8, 128), (3, 9, ROWS, 128), (3, 9, ROWS, 128)],
+        [up, down, *kept, low, high],
+        [
+            (6, 7, 48, 128), (6, 7, ROWS, 128), (6, 7, 48, 128),
+            (7, ROWS, 128), (4, ROWS, 128),
+        ],
     )
     spread, planes = call(
         bone_y,
         [block, (count, 40, 128)],
-        [smooth, lax.ppermute(smooth, "sub", swap), occupancy],
-    )
-    planes, first, second = call(
-        krylov,
-        [(count, 40, 128), (3, 11, ROWS, 128), (3, 9, ROWS, 128)],
-        [*kept, low, high, planes],
-        [
-            (6, 11, 48, 128), (6, 11, 48, 128), (6, 11, 48, 128),
-            (10, ROWS, 128), (9, ROWS, 128), (4, ROWS, 128),
-        ],
+        [smooth, lax.ppermute(smooth, "sub", swap), occupancy, line],
     )
     planes = lax.all_to_all(planes, "run", 0, 0, tiled=True)
     lines = planes[:, 32:40]

time: 59.7 us -> 56.1 us (0.940)
  waiting for transfers between devices: 17.2 us -> 11.8 us
  blocking collectives: 12.2 us -> 14.7 us
  Pallas kernels: 12.8 us -> 12.2 us
    ppermute x1, waiting for transfers between devices: 6.57 us -> 0.7 us  [local(): high = lax.ppermute(down, 'run', [(i + 1, i) for i in range(count - 1)])]
    all_to_all x1, blocking collectives: 12.2 us -> 14.7 us  [local(): planes = lax.all_to_all(planes, 'run', 0, 0, tiled=True)]
  transfers between devices with their start and end apart: 9 -> 9, of which waited for: 7 -> 7; matrix products, arithmetic and copies ran while one was open for 0% -> 0% of each run, Pallas kernels for 6% -> 13%
where the time goes in v4:
time: 56.1 us; the launch traced here: 55.7 us
  blocking collectives  14.7 us (26%)
  starting transfers between devices  13.9 us (25%)
  Pallas kernels  12.2 us (22%)
  waiting for transfers between devices  11.8 us (21%)
  other arithmetic  1.97 us (4%)
  between operations  0.75 us (1%)
    all_to_all x1, blocking collectives, local(): planes = lax.all_to_all(planes, 'run', 0, 0, tiled=True)  14.7 us
    pallas_call x9, Pallas kernels, call(): pl.pallas_call(kernel, out_shape=[jax.ShapeDtypeStruct(s, jnp.float32) fo...  12.2 us
    ppermute x2, waiting for transfers between devices, far_slabs(): both = lax.ppermute(block, 'run', rise + fall)  5.17 us
    ppermute x2, starting transfers between devices, far_slabs(): both = lax.ppermute(block, 'run', rise + fall)  4.34 us
    all_to_all x1, starting transfers between devices, local(): planes = lax.all_to_all(planes, 'run', 0, 0, tiled=True)  4.08 us
    ppermute x1, starting transfers between devices, local(): low = lax.ppermute(up, 'run', [(i, i + 1) for i in range(count - 1)])  3.44 us
    all_to_all x1, waiting for transfers between devices, local(): planes = lax.all_to_all(planes, 'run', 0, 0, tiled=True)  3.26 us
    ppermute x1, starting transfers between devices, local(): high = lax.ppermute(down, 'run', [(i + 1, i) for i in range(count - 1)])  1.29 us
  transfers between devices with their start and end apart: 9, of which 7 were waited for; matrix products, arithmetic and copies ran while one was open for 0% of the time, Pallas kernels for 13%

profile of v4, /device:TPU:0, one launch (start us, length us, event | category | flops | bytes accessed | tf_op | source)
XLA Modules:
  0.0 55.7 jit_solution(8206261661777045193)
XLA Ops:
  0.6 0.8 %multiply_select_fusion = f32[8,8,128]{2,1,0:T(8,128)S(1)} fusion(f32[8,32,128]{2,1,0:T(8,128)} %density.7, s32[8,32,128]{2,1,0:T(8,128)} %bone.7, pred[]{:T(512)S(6)} %eq.12), kind=kLoop, calls=%fused_computation.3 | loop fusion | flops 40960 | bytes 163841 | tf_op jit(solution)/shard_map/jit(_where)/select_n | solution.py:64
  1.5 0.0 copy-start.2
  1.5 0.0 copy-start.3
  1.5 1.1 %slice_select_fusion = (f32[3,8,8,128]{3,2,1,0:T(8,128)S(1)}, f32[3,8,8,128]{3,2,1,0:T(8,128)S(1)}) fusion(f32[3,8,32,128]{3,2,1,0:T(8,128)} %load.3, pred[]{:T(512)S(6)} %eq.12, f32[3,8,32,128]{3,2,1,0:T(8,128)} %guess.3), kind=kLoop, calls=%fused_computation.1 | loop fusion | flops 49152 | bytes 589825 | tf_op jit(solution)/shard_map/jit(_where)/select_n | solution.py:240
  2.6 0.0 copy-start
  2.6 0.0 copy-start.1
  2.7 0.5 collective-permute-start
  3.2 0.3 copy-done
  3.5 4.0 %collective-permute-start.1 = (s32[8,32,128]{2,1,0:T(8,128)S(1)}, s32[8,32,128]{2,1,0:T(8,128)S(1)}, u32[]{:S(2)}, u32[]{:S(2)}) collective-permute-start(s32[8,32,128]{2,1,0:T(8,128)S(1)} %copy-done), channel_id=1, source_target_pairs={{0,8},{2,10},{4,12},{6,14},{8,0},{10,2},{12,4},{14,6},{1,9},{3,11}... | collective-permute-start | bytes 393224 | tf_op jit(solution)/shard_map/ppermute | solution.py:703
  7.6 0.0 collective-permute-done.side
  7.6 0.0 copy-done.2
  7.6 0.0 copy-done.3
  7.6 0.0 copy-done.1
  7.6 0.6 %shard_map.60 = (f32[10,40,128]{2,1,0:T(8,128)S(1)}, f32[8,40,128]{2,1,0:T(8,128)S(1)}) custom-call(f32[3,8,32,128]{3,2,1,0:T(8,128)S(1)} %copy-done.2, f32[3,8,32,128]{3,2,1,0:T(8,128)S(1)} %copy-done.3, s32[8,32,128]{2,1,0:T(8,128)S(1)} %copy-done, f32[8,32,128]{2,1,0:T(8,128)S(1)} %copy-done.1, f32[56,8,128]{2,1,0:T(8,128)S(1)} %collective-permute-done.side), custom_call_target="tpu_custom_call" | custom-call | tf_op jit(solution)/shard_map/pallas_call | solution.py:37
  8.2 3.4 %collective-permute-start.3 = (f32[10,40,128]{2,1,0:T(8,128)S(1)}, f32[10,40,128]{2,1,0:T(8,128)S(1)}, u32[]{:S(2)}, u32[]{:S(2)}) collective-permute-start(f32[10,40,128]{2,1,0:T(8,128)S(1)} %get-tuple-element.23.up), channel_id=1, source_target_pairs={{0,2},{2,4},{4,6},{6,8},{8,10},{10,12},{12,14},{1,3},{3,5},{5,7},{... | collective-permute-start | bytes 614408 | tf_op jit(solution)/shard_map/ppermute | solution.py:641
  11.7 1.3 %collective-permute-start.4 = (f32[8,40,128]{2,1,0:T(8,128)S(1)}, f32[8,40,128]{2,1,0:T(8,128)S(1)}, u32[]{:S(2)}, u32[]{:S(2)}) collective-permute-start(f32[8,40,128]{2,1,0:T(8,128)S(1)} %get-tuple-element.24.down), channel_id=1, source_target_pairs={{2,0},{4,2},{6,4},{8,6},{10,8},{12,10},{14,12},{3,1},{5,3},{7,5},{... | collective-permute-start | bytes 491528 | tf_op jit(solution)/shard_map/ppermute | solution.py:642
  13.0 0.9 %collective-permute-done.1.bone_below.bone_above = s32[8,32,128]{2,1,0:T(8,128)S(1)} collective-permute-done((s32[8,32,128]{2,1,0:T(8,128)S(1)}, s32[8,32,128]{2,1,0:T(8,128)S(1)}, u32[]{:S(2)}, u32[]{:S(2)}) %collective-permute-start.1) | collective-permute-done | bytes 131104 | tf_op jit(solution)/shard_map/ppermute | solution.py:703
  13.9 4.3 %shard_map.59 = (f32[10,32,128]{2,1,0:T(8,128)S(1)}, f32[3,8,40,128]{3,2,1,0:T(8,128)S(1)}, f32[8,40,128]{2,1,0:T(8,128)S(1)}, f32[7,40,128]{2,1,0:T(8,128)S(1)}...) custom-call(f32[3,8,32,128]{3,2,1,0:T(8,128)S(1)} %copy-done.2, ...), custom_call_target="tpu_custom_call" | custom-call | tf_op jit(solution)/shard_map/pallas_call | solution.py:37
  18.2 0.1 collective-permute-start.2
  18.2 0.7 %collective-permute-done.4.high = f32[8,40,128]{2,1,0:T(8,128)S(1)} collective-permute-done((f32[8,40,128]{2,1,0:T(8,128)S(1)}, f32[8,40,128]{2,1,0:T(8,128)S(1)}, u32[]{:S(2)}, u32[]{:S(2)}) %collective-permute-start.4) | collective-permute-done | bytes 163872 | tf_op jit(solution)/shard_map/ppermute | solution.py:642
  18.9 0.3 collective-permute-done.3.low
  19.2 2.0 %shard_map.61 = (f32[8,128]{1,0:T(8,128)S(1)}, f32[3,9,40,128]{3,2,1,0:T(8,128)S(1)}, f32[3,9,40,128]{3,2,1,0:T(8,128)S(1)}) custom-call(f32[10,40,128]{2,1,0:T(8,128)S(1)} %get-tuple-element.23.up, f32[8,40,128]{2,1,0:T(8,128)S(1)} %get-tuple-element.24.down, f32[3,8,40,128]{3,2,1,0:T(8,128)S(1)} %get-tuple-element.25.guess_w, ...), custom_call_target="tpu_custom_call" | custom-call | tf_op jit(solution)/shard_map/pallas_call | solution.py:37
  21.2 0.0 collective-permute-done.2.other
  21.2 0.5 shard_map.62
  21.8 14.7 %all_to_all.10.planes = f32[8,40,128]{2,1,0:T(8,128)S(1)} all-to-all(f32[8,40,128]{2,1,0:T(8,128)S(1)} %get-tuple-element.34), channel_id=1, replica_groups=mesh['grp'=2,'run'=8,'sub'=2] {'run'}, dimensions={0} | all-to-all | bytes 327680 | tf_op jit(solution)/shard_map/all_to_all | solution.py:672
  36.4 0.0 collective-permute-start.5
  36.5 1.1 %collective-permute-done.5.lines_b = f32[8,8,128]{2,1,0:T(8,128)S(1)} collective-permute-done((f32[8,8,128]{2,1,0:T(8,128)S(1)}, f32[8,8,128]{2,1,0:T(8,128)S(1)}, u32[]{:S(2)}, u32[]{:S(2)}) %collective-permute-start.5) | collective-permute-done | bytes 32800 | tf_op jit(solution)/shard_map/ppermute | solution.py:674
  37.6 2.6 %shard_map.64 = (f32[3,8,32,128]{3,2,1,0:T(8,128)}, f32[264,128]{1,0:T(8,128)S(1)}) custom-call(f32[8,8,128]{2,1,0:T(8,128)S(1)} %slice.36.lines, f32[8,8,128]{2,1,0:T(8,128)S(1)} %collective-permute-done.5.lines_b, f32[3,8,40,128]{3,2,1,0:T(8,128)S(1)} %get-tuple-element.25.guess_w, f32[10,40,128]{2,1,0:T(8,128)S(1)} %collective-permute-done.3.low, ...), custom_call_target="tpu_custom_call" | custom-call | tf_op jit(solution)/shard_map/pallas_call | solution.py:37
  40.3 0.2 collective-permute-start.6
  40.4 1.2 %collective-permute-done.6.other = f32[264,128]{1,0:T(8,128)S(1)} collective-permute-done((f32[264,128]{1,0:T(8,128)S(1)}, f32[264,128]{1,0:T(8,128)S(1)}, u32[]{:S(2)}, u32[]{:S(2)}) %collective-permute-start.6) | collective-permute-done | bytes 135200 | tf_op jit(solution)/shard_map/ppermute | solution.py:682
  41.6 1.2 %shard_map.65 = (f32[8,32,128]{2,1,0:T(8,128)S(1)}, f32[8,40,128]{2,1,0:T(8,128)}) custom-call(f32[264,128]{1,0:T(8,128)S(1)} %get-tuple-element.39.mine, f32[264,128]{1,0:T(8,128)S(1)} %collective-permute-done.6.other), custom_call_target="tpu_custom_call" | custom-call | tf_op jit(solution)/shard_map/pallas_call | solution.py:37
  42.8 0.3 collective-permute-start.7
  43.1 4.1 %all-to-all-start.1 = ((f32[8,40,128]{2,1,0:T(8,128)}), f32[8,40,128]{2,1,0:T(8,128)S(1)}, u32[]{:S(2)}, u32[]{:S(2)}) async-start(f32[8,40,128]{2,1,0:T(8,128)} %get-tuple-element.41), calls=%async_computation.1 | async-start | bytes 327680 | tf_op jit(solution)/shard_map/all_to_all | solution.py:685
  47.2 4.3 %collective-permute-done.7.below.above = f32[8,32,128]{2,1,0:T(8,128)S(1)} collective-permute-done((f32[8,32,128]{2,1,0:T(8,128)S(1)}, f32[8,32,128]{2,1,0:T(8,128)S(1)}, u32[]{:S(2)}, u32[]{:S(2)}) %collective-permute-start.7) | collective-permute-done | bytes 131104 | tf_op jit(solution)/shard_map/ppermute | solution.py:703
  51.4 0.2 shard_map.66.part
  51.6 3.3 %all-to-all-done.1.planes = f32[8,40,128]{2,1,0:T(8,128)S(1)} async-done(((f32[8,40,128]{2,1,0:T(8,128)}), f32[8,40,128]{2,1,0:T(8,128)S(1)}, u32[]{:S(2)}, u32[]{:S(2)}) %all-to-all-start.1) | async-done | bytes 163872 | tf_op jit(solution)/shard_map/all_to_all | solution.py:685
  54.9 0.8 %shard_map.67 = f32[8,32,128]{2,1,0:T(8,128)} custom-call(f32[8,32,128]{2,1,0:T(8,128)S(1)} %shard_map.66.part, f32[8,40,128]{2,1,0:T(8,128)S(1)} %all-to-all-done.1.planes, f32[8,8,128]{2,1,0:T(8,128)S(1)} %slice.36.lines, f32[8,8,128]{2,1,0:T(8,128)S(1)} %collective-permute-done.5.lines_b, s32[8,32,128]{2,1,0:T(8,128)S(1)} %copy-done, ...), custom_call_target="tpu_custom_call" | custom-call | tf_op jit(solution)/shard_map/pallas_call | solution.py:37
  (3 shorter events, 0.1 us)
Async XLA Ops:
  1.5 6.1 %copy-start.2 = (f32[3,8,32,128]{3,2,1,0:T(8,128)S(1)}, f32[3,8,32,128]{3,2,1,0:T(8,128)}, u32[]{:S(2)}) copy-start(f32[3,8,32,128]{3,2,1,0:T(8,128)} %load.3) | copy-start | bytes 1179652
  1.5 6.1 %copy-start.3 = (f32[3,8,32,128]{3,2,1,0:T(8,128)S(1)}, f32[3,8,32,128]{3,2,1,0:T(8,128)}, u32[]{:S(2)}) copy-start(f32[3,8,32,128]{3,2,1,0:T(8,128)} %guess.3) | copy-start | bytes 1179652
  2.6 0.9 %copy-start = (s32[8,32,128]{2,1,0:T(8,128)S(1)}, s32[8,32,128]{2,1,0:T(8,128)}, u32[]{:S(2)}) copy-start(s32[8,32,128]{2,1,0:T(8,128)} %bone.7) | copy-start | bytes 393220
  2.6 4.9 %copy-start.1 = (f32[8,32,128]{2,1,0:T(8,128)S(1)}, f32[8,32,128]{2,1,0:T(8,128)}, u32[]{:S(2)}) copy-start(f32[8,32,128]{2,1,0:T(8,128)} %density.7) | copy-start | bytes 393220
  2.7 4.9 %collective-permute-start = (f32[56,8,128]{2,1,0:T(8,128)S(1)}, f32[56,8,128]{2,1,0:T(8,128)S(1)}, u32[]{:S(2)}, u32[]{:S(2)}) collective-permute-start(f32[56,8,128]{2,1,0:T(8,128)S(1)} %pad_maximum_fusion), channel_id=1, source_target_pairs={{0,1},{1,0},{2,3},{3,2},{4,5},{5,4},{6,7},{7,6},{8,9},{9,8},{10,11... | collective-permute-start | bytes 688136 | tf_op jit(solution)/shard_map/ppermute | solution.py:630
  3.5 10.3 %collective-permute-start.1 = (s32[8,32,128]{2,1,0:T(8,128)S(1)}, s32[8,32,128]{2,1,0:T(8,128)S(1)}, u32[]{:S(2)}, u32[]{:S(2)}) collective-permute-start(s32[8,32,128]{2,1,0:T(8,128)S(1)} %copy-done), channel_id=1, source_target_pairs={{0,8},{2,10},{4,12},{6,14},{8,0},{10,2},{12,4},{14,6},{1,9},{3,11}... | collective-permute-start | bytes 393224 | tf_op jit(solution)/shard_map/ppermute | solution.py:703
  8.2 11.0 %collective-permute-start.3 = (f32[10,40,128]{2,1,0:T(8,128)S(1)}, f32[10,40,128]{2,1,0:T(8,128)S(1)}, u32[]{:S(2)}, u32[]{:S(2)}) collective-permute-start(f32[10,40,128]{2,1,0:T(8,128)S(1)} %get-tuple-element.23.up), channel_id=1, source_target_pairs={{0,2},{2,4},{4,6},{6,8},{8,10},{10,12},{12,14},{1,3},{3,5},{5,7},{... | collective-permute-start | bytes 614408 | tf_op jit(solution)/shard_map/ppermute | solution.py:641
  11.7 7.3 %collective-permute-start.4 = (f32[8,40,128]{2,1,0:T(8,128)S(1)}, f32[8,40,128]{2,1,0:T(8,128)S(1)}, u32[]{:S(2)}, u32[]{:S(2)}) collective-permute-start(f32[8,40,128]{2,1,0:T(8,128)S(1)} %get-tuple-element.24.down), channel_id=1, source_target_pairs={{2,0},{4,2},{6,4},{8,6},{10,8},{12,10},{14,12},{3,1},{5,3},{7,5},{... | collective-permute-start | bytes 491528 | tf_op jit(solution)/shard_map/ppermute | solution.py:642
  18.2 3.0 %collective-permute-start.2 = (f32[10,32,128]{2,1,0:T(8,128)S(1)}, f32[10,32,128]{2,1,0:T(8,128)S(1)}, u32[]{:S(2)}, u32[]{:S(2)}) collective-permute-start(f32[10,32,128]{2,1,0:T(8,128)S(1)} %get-tuple-element.22.mine), channel_id=1, source_target_pairs={{0,1},{1,0},{2,3},{3,2},{4,5},{5,4},{6,7},{7,6},{8,9},{9,8},{10,11... | collective-permute-start | bytes 491528 | tf_op jit(solution)/shard_map/ppermute | solution.py:670
  36.4 1.2 %collective-permute-start.5 = (f32[8,8,128]{2,1,0:T(8,128)S(1)}, f32[8,8,128]{2,1,0:T(8,128)S(1)}, u32[]{:S(2)}, u32[]{:S(2)}) collective-permute-start(f32[8,8,128]{2,1,0:T(8,128)S(1)} %slice.36.lines), channel_id=1, source_target_pairs={{0,1},{1,0},{2,3},{3,2},{4,5},{5,4},{6,7},{7,6},{8,9},{9,8},{10,11... | collective-permute-start | bytes 98312 | tf_op jit(solution)/shard_map/ppermute | solution.py:674
  40.3 1.4 %collective-permute-start.6 = (f32[264,128]{1,0:T(8,128)S(1)}, f32[264,128]{1,0:T(8,128)S(1)}, u32[]{:S(2)}, u32[]{:S(2)}) collective-permute-start(f32[264,128]{1,0:T(8,128)S(1)} %get-tuple-element.39.mine), channel_id=1, source_target_pairs={{0,1},{1,0},{2,3},{3,2},{4,5},{5,4},{6,7},{7,6},{8,9},{9,8},{10,11... | collective-permute-start | bytes 405512 | tf_op jit(solution)/shard_map/ppermute | solution.py:682
  42.8 8.7 %collective-permute-start.7 = (f32[8,32,128]{2,1,0:T(8,128)S(1)}, f32[8,32,128]{2,1,0:T(8,128)S(1)}, u32[]{:S(2)}, u32[]{:S(2)}) collective-permute-start(f32[8,32,128]{2,1,0:T(8,128)S(1)} %get-tuple-element.40.mine), channel_id=1, source_target_pairs={{0,8},{2,10},{4,12},{6,14},{8,0},{10,2},{12,4},{14,6},{1,9},{3,11}... | collective-permute-start | bytes 393224 | tf_op jit(solution)/shard_map/ppermute | solution.py:703
  43.1 11.8 %all-to-all-start.1 = ((f32[8,40,128]{2,1,0:T(8,128)}), f32[8,40,128]{2,1,0:T(8,128)S(1)}, u32[]{:S(2)}, u32[]{:S(2)}) async-start(f32[8,40,128]{2,1,0:T(8,128)} %get-tuple-element.41), calls=%async_computation.1 | async-start | bytes 327680 | tf_op jit(solution)/shard_map/all_to_all | solution.py:685

commit v5 on v4

--- a/solution.py
+++ b/solution.py
@@ -238,9 +238,9 @@
     sub = lax.axis_index("sub")
     flat = lambda part: part.reshape((-1,) + part.shape[-2:])
     near = lambda part: jnp.where(sub == 0, part[..., 24:32, :], part[..., 0:8, :])
-    return jnp.concatenate(
-        [flat(near(guess)), flat(near(load)), stiff(near(occupancy), near(density))], axis=0
-    )
+    fields = [flat(near(guess)), flat(near(load))]
+    fields, occupancy, density = lax.optimization_barrier((fields, occupancy, density))
+    return jnp.concatenate(fields + [stiff(near(occupancy), near(density))], axis=0)
 
 
 def windows(sub, load, guess, bone, density, side):
@@ -365,7 +365,7 @@
 
 def krylov(
     up, down, guess_w, mod_w, inverse, inner_z, inner_s, near_m, far_m, sums_in, low, high,
-    row_out, first, second, pair, near, far, mods, sums,
+    bone, row_out, first, second, pair, near, far, mods, sums,
 ):
     sub = lax.axis_index("sub")
     run = lax.axis_index("run")
@@ -454,6 +454,8 @@
     line = jnp.zeros((1, 128), jnp.float32)
     for k in range(4):
         line = jnp.where(lane == k, whole(sums[k, own]), line)
+    total = whole(jnp.sum(bone[...].astype(jnp.float32), axis=0))
+    line = jnp.where(lane == 4, total, line)
     row_out[...] = jnp.broadcast_to(line, row_out.shape)
 
 
@@ -462,35 +464,29 @@
     return jnp.sum(jnp.where(lane == k, line, 0.0), axis=1, keepdims=True)
 
 
-def energies(
-    lines, lines_b, guess_w, low, first, second, occupancy, density, spread,
-    out, smooth, pair, field, specific,
-):
-    sub = lax.axis_index("sub")
-    own = pl.ds(pl.multiple_of(8 * sub, 8), 32)
-    line = (jnp.sum(lines[...], axis=0) + jnp.sum(lines_b[...], axis=0))[0:1]
+def steplengths(lines):
+    line = jnp.sum(lines[:, 32:40], axis=0)[0:1]
     a, b, c, e = (pick(line, k) for k in range(4))
     alpha = a / b
     fresh = alpha * alpha * c - a
     beta = fresh / a
     square = alpha * alpha * e - (1.0 + beta) * (1.0 + beta) * b
     after = fresh / square
-    p = jnp.broadcast_to(alpha + after * (1.0 + beta), (ROWS, 128))
-    q = jnp.broadcast_to(-after * alpha, (ROWS, 128))
+    return alpha + after * (1.0 + beta), -after * alpha
+
+
+def energies(
+    lines, guess_w, low, first, second, occupancy, density, spread,
+    smooth, pair, specific,
+):
+    sub = lax.axis_index("sub")
+    own = pl.ds(pl.multiple_of(8 * sub, 8), 32)
+    p, q = (jnp.broadcast_to(step, (ROWS, 128)) for step in steplengths(lines))
     clear(pair)
-    for c in range(3):
-        enter(pair, 0, c, low[c] + p * first[c, 0] + q * second[c, 0])
-
-    def advance(k, _):
+    for k in range(9):
         for c in range(3):
-            value = guess_w[c, k] + p * first[c, k + 1] + q * second[c, k + 1]
-            field[c] = value
-            enter(pair, k + 1, c, value)
-        for c in range(3):
-            out[c, k] = field[c, own]
-        return 0
-
-    lax.fori_loop(0, 8, advance, 0)
+            start = guess_w[c, k - 1] if k else low[c]
+            enter(pair, k, c, start + p * first[c, k] + q * second[c, k])
 
     def use(k, tile, value):
         specific[k, 8 * tile : 8 * tile + 8] = value
@@ -555,13 +551,15 @@
     out[8], out[9] = decayed([blocks[0](k) for k in range(8)])
 
 
-def bone_y(mine, other, bone, line, out, planes):
+def bone_y(mine, other, spread, rails):
     block = list(smooth_y(lambda k: mine[k], lambda k: other[k], 10))
     for k in range(8):
-        out[k] = block[k]
-    lane = lax.broadcasted_iota(jnp.int32, (8, 128), 1)
-    total = whole(jnp.sum(bone[...].astype(jnp.float32), axis=0))
-    ladder(block[8], block[9], jnp.where(lane == 4, total, line[...]), planes)
+        spread[k] = block[k]
+    rails[0], rails[1] = block[8], block[9]
+
+
+def rungs(rails, mine, other, out):
+    ladder(rails[0], rails[1], mine[...] + other[...], out)
 
 
 def along_y(mine, other, out, planes):
@@ -601,10 +599,19 @@
         yield value + jnp.where(has_below, far_below, 0.0) + jnp.where(has_above, far_above, 0.0)
 
 
-def partial_z(count, mine, below, above, out):
+def partial_z(
+    count, mine, below, above, lines, guess, first, second, out, displacement
+):
     blocks = [lambda j, ref=ref: ref[j] for ref in (mine, below, above)]
     for i, value in enumerate(far_z(count, *blocks)):
         out[i] = value
+    own = pl.ds(pl.multiple_of(8 * lax.axis_index("sub"), 8), 32)
+    p, q = (jnp.broadcast_to(step, (32, 128)) for step in steplengths(lines))
+    for c in range(3):
+        for k in range(8):
+            displacement[c, k] = (
+                guess[c, k] + p * first[c, k + 1, own] + q * second[c, k + 1, own]
+            )
 
 
 def spread_z(count, part, planes, out):
@@ -612,8 +619,8 @@
         out[i] = part[i] + near_z(count, planes, i)
 
 
-def remodel(count, part, planes, lines, lines_b, bone, density, out):
-    bones = (jnp.sum(lines[...], axis=0) + jnp.sum(lines_b[...], axis=0))[0:1]
+def remodel(count, part, planes, lines, bone, density, out):
+    bones = jnp.sum(lines[:, 32:40], axis=0)[0:1]
     line = jnp.sum(planes[:, 32:40], axis=0)[0:1]
     scale = jnp.broadcast_to(pick(bones, 4) / line, density.shape[1:])
     for i in range(8):
@@ -658,38 +665,41 @@
     line, first, second = call(
         krylov,
         [(8, 128), (3, 9, ROWS, 128), (3, 9, ROWS, 128)],
-        [up, down, *kept, low, high],
+        [up, down, *kept, low, high, occupancy],
         [
             (6, 7, 48, 128), (6, 7, ROWS, 128), (6, 7, 48, 128),
             (7, ROWS, 128), (4, ROWS, 128),
         ],
     )
-    spread, planes = call(
-        bone_y,
-        [block, (count, 40, 128)],
-        [smooth, lax.ppermute(smooth, "sub", swap), occupancy, line],
+    spread, rails = call(
+        bone_y, [block, (2, 32, 128)], [smooth, lax.ppermute(smooth, "sub", swap)]
+    )
+    (planes,) = call(
+        rungs, [(count, 40, 128)], [rails, line, lax.ppermute(line, "sub", swap)]
     )
     planes = lax.all_to_all(planes, "run", 0, 0, tiled=True)
-    lines = planes[:, 32:40]
-    lines_b = lax.ppermute(lines, "sub", swap)
+    lines = planes
     (spread,) = call(functools.partial(spread_z, count), [block], [spread, planes])
-    displacement, smooth = call(
+    (smooth,) = call(
         energies,
-        [guess.shape, (264, 128)],
-        [lines, lines_b, guess_w, low, first, second, occupancy, density, spread],
-        [(6, 9, 48, 128), (3, ROWS, 128), (8, ROWS, 128)],
+        [(264, 128)],
+        [lines, guess_w, low, first, second, occupancy, density, spread],
+        [(6, 9, 48, 128), (8, ROWS, 128)],
     )
     other = lax.ppermute(smooth, "sub", swap)
     smooth, planes = call(along_y, [block, (count, 40, 128)], [smooth, other])
     below, above = far_slabs(smooth)
     planes = lax.all_to_all(planes, "run", 0, 0, tiled=True)
-    (part,) = call(
-        functools.partial(partial_z, count), [block], [smooth, below, above], flops=10**10
+    part, displacement = call(
+        functools.partial(partial_z, count),
+        [block, guess.shape],
+        [smooth, below, above, lines, guess, first, second],
+        flops=10**10,
     )
     (new_density,) = call(
         functools.partial(remodel, count),
         [block],
-        [part, planes, lines, lines_b, occupancy, density],
+        [part, planes, lines, occupancy, density],
     )
     return displacement, new_density
 

time: 56.1 us -> 53.8 us (0.959)
  other arithmetic: 1.97 us -> 1.16 us
  waiting for transfers between devices: 11.8 us -> 11.2 us
    all_to_all x1, waiting for transfers between devices: 3.26 us -> 2.44 us  [local(): planes = lax.all_to_all(planes, 'run', 0, 0, tiled=True)]
    select_n x1, other arithmetic: 0.82 us -> 0.01 us  [stiff(): return jnp.where(occupancy == 1, density * density, MARROW)]
    ppermute x2, waiting for transfers between devices: 5.17 us -> 5.79 us  [far_slabs(): both = lax.ppermute(block, 'run', rise + fall)]
    pallas_call x9 -> x10, Pallas kernels: 12.2 us -> 11.7 us  [call(): pl.pallas_call(kernel, out_shape=[jax.ShapeDtypeStruct(s, jnp.float32) fo...]
  transfers between devices with their start and end apart: 9 -> 9, of which waited for: 7 -> 7; matrix products, arithmetic and copies ran while one was open for 0% -> 0% of each run, Pallas kernels for 13% -> 16%
where the time goes in v5:
time: 53.8 us; the launch traced here: 53.5 us
  blocking collectives  15.1 us (28%)
  starting transfers between devices  13.4 us (25%)
  Pallas kernels  11.7 us (22%)
  waiting for transfers between devices  11.2 us (21%)
  other arithmetic  1.16 us (2%)
  between operations  0.78 us (1%)
    all_to_all x1, blocking collectives, local(): planes = lax.all_to_all(planes, 'run', 0, 0, tiled=True)  15.1 us
    pallas_call x10, Pallas kernels, call(): pl.pallas_call(kernel, out_shape=[jax.ShapeDtypeStruct(s, jnp.float32) fo...  11.7 us
    ppermute x2, waiting for transfers between devices, far_slabs(): both = lax.ppermute(block, 'run', rise + fall)  5.79 us
    ppermute x2, starting transfers between devices, far_slabs(): both = lax.ppermute(block, 'run', rise + fall)  4.23 us
    all_to_all x1, starting transfers between devices, local(): planes = lax.all_to_all(planes, 'run', 0, 0, tiled=True)  3.89 us
    ppermute x1, starting transfers between devices, local(): low = lax.ppermute(up, 'run', [(i, i + 1) for i in range(count - 1)])  3.44 us
    all_to_all x1, waiting for transfers between devices, local(): planes = lax.all_to_all(planes, 'run', 0, 0, tiled=True)  2.44 us
    ppermute x1, waiting for transfers between devices, local(): other = lax.ppermute(smooth, 'sub', swap)  1.35 us
  transfers between devices with their start and end apart: 9, of which 7 were waited for; matrix products, arithmetic and copies ran while one was open for 0% of the time, Pallas kernels for 16%

profile of v5, /device:TPU:0, one launch (start us, length us, event | category | flops | bytes accessed | tf_op | source)
XLA Modules:
  0.0 53.5 jit_solution(5309330229421029011)
XLA Ops:
  0.6 0.0 copy-start
  0.6 0.0 copy-start.1
  0.7 0.0 copy-start.3
  0.7 1.1 %slice_select_fusion = (f32[3,8,8,128]{3,2,1,0:T(8,128)S(1)}, f32[3,8,8,128]{3,2,1,0:T(8,128)S(1)}) fusion(f32[3,8,32,128]{3,2,1,0:T(8,128)} %load.3, pred[]{:T(512)S(6)} %eq.12, f32[3,8,32,128]{3,2,1,0:T(8,128)} %guess.5), kind=kLoop, calls=%fused_computation.1 | loop fusion | flops 49152 | bytes 589825 | tf_op jit(solution)/shard_map/jit(_where)/select_n | solution.py:240
  1.8 0.0 copy-start.2
  1.8 0.0 copy-done
  1.8 0.0 copy-done.1
  1.9 0.5 collective-permute-start
  2.4 3.7 %collective-permute-start.1 = (s32[8,32,128]{2,1,0:T(8,128)S(1)}, s32[8,32,128]{2,1,0:T(8,128)S(1)}, u32[]{:S(2)}, u32[]{:S(2)}) collective-permute-start(s32[8,32,128]{2,1,0:T(8,128)S(1)} %copy-done), channel_id=1, source_target_pairs={{0,8},{2,10},{4,12},{6,14},{8,0},{10,2},{12,4},{14,6},{1,9},{3,11}... | collective-permute-start | bytes 393224 | tf_op jit(solution)/shard_map/ppermute | solution.py:713
  6.1 0.0 collective-permute-done.side
  6.1 0.0 copy-done.3
  6.1 0.0 copy-done.2
  6.1 0.6 %shard_map.61 = (f32[10,40,128]{2,1,0:T(8,128)S(1)}, f32[8,40,128]{2,1,0:T(8,128)S(1)}) custom-call(f32[3,8,32,128]{3,2,1,0:T(8,128)S(1)} %copy-done.2, f32[3,8,32,128]{3,2,1,0:T(8,128)S(1)} %copy-done.3, s32[8,32,128]{2,1,0:T(8,128)S(1)} %copy-done, f32[8,32,128]{2,1,0:T(8,128)S(1)} %copy-done.1, f32[56,8,128]{2,1,0:T(8,128)S(1)} %collective-permute-done.side), custom_call_target="tpu_custom_call" | custom-call | tf_op jit(solution)/shard_map/pallas_call | solution.py:37
  6.7 3.4 %collective-permute-start.3 = (f32[10,40,128]{2,1,0:T(8,128)S(1)}, f32[10,40,128]{2,1,0:T(8,128)S(1)}, u32[]{:S(2)}, u32[]{:S(2)}) collective-permute-start(f32[10,40,128]{2,1,0:T(8,128)S(1)} %get-tuple-element.32.up), channel_id=1, source_target_pairs={{0,2},{2,4},{4,6},{6,8},{8,10},{10,12},{12,14},{1,3},{3,5},{5,7},{... | collective-permute-start | bytes 614408 | tf_op jit(solution)/shard_map/ppermute | solution.py:648
  10.1 1.3 %collective-permute-start.4 = (f32[8,40,128]{2,1,0:T(8,128)S(1)}, f32[8,40,128]{2,1,0:T(8,128)S(1)}, u32[]{:S(2)}, u32[]{:S(2)}) collective-permute-start(f32[8,40,128]{2,1,0:T(8,128)S(1)} %get-tuple-element.33.down), channel_id=1, source_target_pairs={{2,0},{4,2},{6,4},{8,6},{10,8},{12,10},{14,12},{3,1},{5,3},{7,5},{... | collective-permute-start | bytes 491528 | tf_op jit(solution)/shard_map/ppermute | solution.py:649
  11.4 1.5 %collective-permute-done.1.bone_below.bone_above = s32[8,32,128]{2,1,0:T(8,128)S(1)} collective-permute-done((s32[8,32,128]{2,1,0:T(8,128)S(1)}, s32[8,32,128]{2,1,0:T(8,128)S(1)}, u32[]{:S(2)}, u32[]{:S(2)}) %collective-permute-start.1) | collective-permute-done | bytes 131104 | tf_op jit(solution)/shard_map/ppermute | solution.py:713
  13.0 4.3 %shard_map.59 = (f32[10,32,128]{2,1,0:T(8,128)S(1)}, f32[3,8,40,128]{3,2,1,0:T(8,128)S(1)}, f32[8,40,128]{2,1,0:T(8,128)S(1)}, f32[7,40,128]{2,1,0:T(8,128)S(1)}...) custom-call(f32[3,8,32,128]{3,2,1,0:T(8,128)S(1)} %copy-done.2, ...), custom_call_target="tpu_custom_call" | custom-call | tf_op jit(solution)/shard_map/pallas_call | solution.py:37
  17.2 0.1 collective-permute-start.2
  17.3 0.7 %collective-permute-done.4.high = f32[8,40,128]{2,1,0:T(8,128)S(1)} collective-permute-done((f32[8,40,128]{2,1,0:T(8,128)S(1)}, f32[8,40,128]{2,1,0:T(8,128)S(1)}, u32[]{:S(2)}, u32[]{:S(2)}) %collective-permute-start.4) | collective-permute-done | bytes 163872 | tf_op jit(solution)/shard_map/ppermute | solution.py:649
  18.0 0.3 collective-permute-done.3.low
  18.3 2.0 %shard_map.62 = (f32[8,128]{1,0:T(8,128)S(1)}, f32[3,9,40,128]{3,2,1,0:T(8,128)S(1)}, f32[3,9,40,128]{3,2,1,0:T(8,128)S(1)}) custom-call(f32[10,40,128]{2,1,0:T(8,128)S(1)} %get-tuple-element.32.up, f32[8,40,128]{2,1,0:T(8,128)S(1)} %get-tuple-element.33.down, f32[3,8,40,128]{3,2,1,0:T(8,128)S(1)} %get-tuple-element.34.guess_w, ...), custom_call_target="tpu_custom_call" | custom-call | tf_op jit(solution)/shard_map/pallas_call | solution.py:37
  20.3 0.0 collective-permute-start.5
  20.3 0.0 collective-permute-done.2.other
  20.3 0.5 shard_map.60
  20.8 0.6 %collective-permute-done.5.other = f32[8,128]{1,0:T(8,128)S(1)} collective-permute-done((f32[8,128]{1,0:T(8,128)S(1)}, f32[8,128]{1,0:T(8,128)S(1)}, u32[]{:S(2)}, u32[]{:S(2)}) %collective-permute-start.5) | collective-permute-done | bytes 4128 | tf_op jit(solution)/shard_map/ppermute | solution.py:678
  21.5 15.1 %all_to_all.10.planes.lines = f32[8,40,128]{2,1,0:T(8,128)S(1)} all-to-all(f32[8,40,128]{2,1,0:T(8,128)S(1)} %shard_map.63), channel_id=1, replica_groups=mesh['grp'=2,'run'=8,'sub'=2] {'run'}, dimensions={0} | all-to-all | bytes 327680 | tf_op jit(solution)/shard_map/all_to_all | solution.py:680
  36.6 1.4 %shard_map.65.mine = f32[264,128]{1,0:T(8,128)S(1)} custom-call(f32[8,40,128]{2,1,0:T(8,128)S(1)} %all_to_all.10.planes.lines, f32[3,8,40,128]{3,2,1,0:T(8,128)S(1)} %get-tuple-element.34.guess_w, f32[10,40,128]{2,1,0:T(8,128)S(1)} %collective-permute-done.3.low, f32[3,9,40,128]{3,2,1,0:T(8,128)S(1)} %get-tuple-element.43.first, ...), custom_call_target="tpu_custom_call" | custom-call | tf_op jit(solution)/shard_map/pallas_call | solution.py:37
  38.0 0.0 collective-permute-start.6
  38.0 1.4 %collective-permute-done.6.other = f32[264,128]{1,0:T(8,128)S(1)} collective-permute-done((f32[264,128]{1,0:T(8,128)S(1)}, f32[264,128]{1,0:T(8,128)S(1)}, u32[]{:S(2)}, u32[]{:S(2)}) %collective-permute-start.6) | collective-permute-done | bytes 135200 | tf_op jit(solution)/shard_map/ppermute | solution.py:689
  39.4 1.1 %shard_map.66 = (f32[8,32,128]{2,1,0:T(8,128)S(1)}, f32[8,40,128]{2,1,0:T(8,128)}) custom-call(f32[264,128]{1,0:T(8,128)S(1)} %shard_map.65.mine, f32[264,128]{1,0:T(8,128)S(1)} %collective-permute-done.6.other), custom_call_target="tpu_custom_call" | custom-call | tf_op jit(solution)/shard_map/pallas_call | solution.py:37
  40.5 0.6 %collective-permute-start.7 = (f32[8,32,128]{2,1,0:T(8,128)S(1)}, f32[8,32,128]{2,1,0:T(8,128)S(1)}, u32[]{:S(2)}, u32[]{:S(2)}) collective-permute-start(f32[8,32,128]{2,1,0:T(8,128)S(1)} %get-tuple-element.46.mine), channel_id=1, source_target_pairs={{0,8},{2,10},{4,12},{6,14},{8,0},{10,2},{12,4},{14,6},{1,9},{3,11}... | collective-permute-start | bytes 393224 | tf_op jit(solution)/shard_map/ppermute | solution.py:713
  41.1 3.9 %all-to-all-start.1 = ((f32[8,40,128]{2,1,0:T(8,128)}), f32[8,40,128]{2,1,0:T(8,128)S(1)}, u32[]{:S(2)}, u32[]{:S(2)}) async-start(f32[8,40,128]{2,1,0:T(8,128)} %get-tuple-element.49), calls=%async_computation.1 | async-start | bytes 327680 | tf_op jit(solution)/shard_map/all_to_all | solution.py:692
  45.0 4.3 %collective-permute-done.7.below.above = f32[8,32,128]{2,1,0:T(8,128)S(1)} collective-permute-done((f32[8,32,128]{2,1,0:T(8,128)S(1)}, f32[8,32,128]{2,1,0:T(8,128)S(1)}, u32[]{:S(2)}, u32[]{:S(2)}) %collective-permute-start.7) | collective-permute-done | bytes 131104 | tf_op jit(solution)/shard_map/ppermute | solution.py:713
  49.3 1.0 %shard_map.67 = (f32[8,32,128]{2,1,0:T(8,128)S(1)}, f32[3,8,32,128]{3,2,1,0:T(8,128)}) custom-call(f32[8,32,128]{2,1,0:T(8,128)S(1)} %get-tuple-element.46.mine, f32[8,32,128]{2,1,0:T(8,128)S(1)} %collective-permute-done.7.below.above, f32[8,32,128]{2,1,0:T(8,128)S(1)} %collective-permute-done.7.below.above, f32[8,40,128]{2,1,0:T(8,128)S(1)} %all_to_all.10.planes.lines, ...), custom_call_target="tpu_custom_call" | custom-call | flops 10000000000 | bytes 1048576 | tf_op jit(solution)/shard_map/pallas_call | solution.py:37
  50.3 2.4 %all-to-all-done.1.planes = f32[8,40,128]{2,1,0:T(8,128)S(1)} async-done(((f32[8,40,128]{2,1,0:T(8,128)}), f32[8,40,128]{2,1,0:T(8,128)S(1)}, u32[]{:S(2)}, u32[]{:S(2)}) %all-to-all-start.1) | async-done | bytes 163872 | tf_op jit(solution)/shard_map/all_to_all | solution.py:692
  52.7 0.8 %shard_map.68 = f32[8,32,128]{2,1,0:T(8,128)} custom-call(f32[8,32,128]{2,1,0:T(8,128)S(1)} %get-tuple-element.48.part, f32[8,40,128]{2,1,0:T(8,128)S(1)} %all-to-all-done.1.planes, f32[8,40,128]{2,1,0:T(8,128)S(1)} %all_to_all.10.planes.lines, s32[8,32,128]{2,1,0:T(8,128)S(1)} %copy-done, f32[8,32,128]{2,1,0:T(8,128)S(1)} %copy-done.1), custom_call_target="tpu_custom_call" | custom-call | tf_op jit(solution)/shard_map/pallas_call | solution.py:37
  (4 shorter events, 0.1 us)
Async XLA Ops:
  0.6 1.2 %copy-start = (s32[8,32,128]{2,1,0:T(8,128)S(1)}, s32[8,32,128]{2,1,0:T(8,128)}, u32[]{:S(2)}) copy-start(s32[8,32,128]{2,1,0:T(8,128)} %bone.7) | copy-start | bytes 393220
  0.6 1.2 %copy-start.1 = (f32[8,32,128]{2,1,0:T(8,128)S(1)}, f32[8,32,128]{2,1,0:T(8,128)}, u32[]{:S(2)}) copy-start(f32[8,32,128]{2,1,0:T(8,128)} %density.7) | copy-start | bytes 393220
  0.7 5.4 %copy-start.3 = (f32[3,8,32,128]{3,2,1,0:T(8,128)S(1)}, f32[3,8,32,128]{3,2,1,0:T(8,128)}, u32[]{:S(2)}) copy-start(f32[3,8,32,128]{3,2,1,0:T(8,128)} %guess.5) | copy-start | bytes 1179652
  1.8 4.3 %copy-start.2 = (f32[3,8,32,128]{3,2,1,0:T(8,128)S(1)}, f32[3,8,32,128]{3,2,1,0:T(8,128)}, u32[]{:S(2)}) copy-start(f32[3,8,32,128]{3,2,1,0:T(8,128)} %load.3) | copy-start | bytes 1179652
  1.9 4.2 %collective-permute-start = (f32[56,8,128]{2,1,0:T(8,128)S(1)}, f32[56,8,128]{2,1,0:T(8,128)S(1)}, u32[]{:S(2)}, u32[]{:S(2)}) collective-permute-start(f32[56,8,128]{2,1,0:T(8,128)S(1)} %pad_maximum_fusion), channel_id=1, source_target_pairs={{0,1},{1,0},{2,3},{3,2},{4,5},{5,4},{6,7},{7,6},{8,9},{9,8},{10,11... | collective-permute-start | bytes 688136 | tf_op jit(solution)/shard_map/ppermute | solution.py:637
  2.4 10.6 %collective-permute-start.1 = (s32[8,32,128]{2,1,0:T(8,128)S(1)}, s32[8,32,128]{2,1,0:T(8,128)S(1)}, u32[]{:S(2)}, u32[]{:S(2)}) collective-permute-start(s32[8,32,128]{2,1,0:T(8,128)S(1)} %copy-done), channel_id=1, source_target_pairs={{0,8},{2,10},{4,12},{6,14},{8,0},{10,2},{12,4},{14,6},{1,9},{3,11}... | collective-permute-start | bytes 393224 | tf_op jit(solution)/shard_map/ppermute | solution.py:713
  6.7 11.6 %collective-permute-start.3 = (f32[10,40,128]{2,1,0:T(8,128)S(1)}, f32[10,40,128]{2,1,0:T(8,128)S(1)}, u32[]{:S(2)}, u32[]{:S(2)}) collective-permute-start(f32[10,40,128]{2,1,0:T(8,128)S(1)} %get-tuple-element.32.up), channel_id=1, source_target_pairs={{0,2},{2,4},{4,6},{6,8},{8,10},{10,12},{12,14},{1,3},{3,5},{5,7},{... | collective-permute-start | bytes 614408 | tf_op jit(solution)/shard_map/ppermute | solution.py:648
  10.1 7.9 %collective-permute-start.4 = (f32[8,40,128]{2,1,0:T(8,128)S(1)}, f32[8,40,128]{2,1,0:T(8,128)S(1)}, u32[]{:S(2)}, u32[]{:S(2)}) collective-permute-start(f32[8,40,128]{2,1,0:T(8,128)S(1)} %get-tuple-element.33.down), channel_id=1, source_target_pairs={{2,0},{4,2},{6,4},{8,6},{10,8},{12,10},{14,12},{3,1},{5,3},{7,5},{... | collective-permute-start | bytes 491528 | tf_op jit(solution)/shard_map/ppermute | solution.py:649
  17.2 3.1 %collective-permute-start.2 = (f32[10,32,128]{2,1,0:T(8,128)S(1)}, f32[10,32,128]{2,1,0:T(8,128)S(1)}, u32[]{:S(2)}, u32[]{:S(2)}) collective-permute-start(f32[10,32,128]{2,1,0:T(8,128)S(1)} %get-tuple-element.30.mine), channel_id=1, source_target_pairs={{0,1},{1,0},{2,3},{3,2},{4,5},{5,4},{6,7},{7,6},{8,9},{9,8},{10,11... | collective-permute-start | bytes 491528 | tf_op jit(solution)/shard_map/ppermute | solution.py:675
  20.3 1.2 %collective-permute-start.5 = (f32[8,128]{1,0:T(8,128)S(1)}, f32[8,128]{1,0:T(8,128)S(1)}, u32[]{:S(2)}, u32[]{:S(2)}) collective-permute-start(f32[8,128]{1,0:T(8,128)S(1)} %get-tuple-element.42.mine), channel_id=1, source_target_pairs={{0,1},{1,0},{2,3},{3,2},{4,5},{5,4},{6,7},{7,6},{8,9},{9,8},{10,11... | collective-permute-start | bytes 12296 | tf_op jit(solution)/shard_map/ppermute | solution.py:678
  38.0 1.4 %collective-permute-start.6 = (f32[264,128]{1,0:T(8,128)S(1)}, f32[264,128]{1,0:T(8,128)S(1)}, u32[]{:S(2)}, u32[]{:S(2)}) collective-permute-start(f32[264,128]{1,0:T(8,128)S(1)} %shard_map.65.mine), channel_id=1, source_target_pairs={{0,1},{1,0},{2,3},{3,2},{4,5},{5,4},{6,7},{7,6},{8,9},{9,8},{10,11... | collective-permute-start | bytes 405512 | tf_op jit(solution)/shard_map/ppermute | solution.py:689
  40.5 8.7 %collective-permute-start.7 = (f32[8,32,128]{2,1,0:T(8,128)S(1)}, f32[8,32,128]{2,1,0:T(8,128)S(1)}, u32[]{:S(2)}, u32[]{:S(2)}) collective-permute-start(f32[8,32,128]{2,1,0:T(8,128)S(1)} %get-tuple-element.46.mine), channel_id=1, source_target_pairs={{0,8},{2,10},{4,12},{6,14},{8,0},{10,2},{12,4},{14,6},{1,9},{3,11}... | collective-permute-start | bytes 393224 | tf_op jit(solution)/shard_map/ppermute | solution.py:713
  41.1 11.6 %all-to-all-start.1 = ((f32[8,40,128]{2,1,0:T(8,128)}), f32[8,40,128]{2,1,0:T(8,128)S(1)}, u32[]{:S(2)}, u32[]{:S(2)}) async-start(f32[8,40,128]{2,1,0:T(8,128)} %get-tuple-element.49), calls=%async_computation.1 | async-start | bytes 327680 | tf_op jit(solution)/shard_map/all_to_all | solution.py:692

commit v6 on v5

--- a/solution.py
+++ b/solution.py
@@ -87,8 +87,8 @@
     return out
 
 
-def steps(count, body, carry):
-    if count <= 3:
+def steps(count, body, carry, straight=3):
+    if count <= straight:
         for k in range(count):
             carry = body(k, carry)
         return carry
@@ -142,7 +142,7 @@
     return columns[0] + columns[1] + lane_left(columns[0] - columns[1])
 
 
-def energy_march(pair, start, count, use):
+def energy_march(pair, start, count, use, straight=3):
     for tile in range(ROWS // 8):
 
         def body(k, low):
@@ -150,7 +150,7 @@
             use(k, tile, quadratic(modes_of(low, high)))
             return high
 
-        steps(count, body, plane_modes(pair, start, tile))
+        steps(count, body, plane_modes(pair, start, tile), straight)
 
 
 def inverted(low, high):
@@ -299,14 +299,13 @@
 
 
 def middle(
-    count, load, guess, bone, density, side, bone_below, bone_above,
-    smooth, guess_w, mod_w, inverse, inner_z, inner_s, near_m, far_m, sums,
+    load, guess, bone, density, side,
+    guess_w, mod_w, inverse, inner_z, inner_s, near_m, far_m, sums,
     load_w, pair, near, far, pair_z, pair_s,
 ):
     put_guess, put_load, put_mod = windows(
         lax.axis_index("sub"), load, guess, bone, density, side
     )
-    bone_z(count, bone, bone_below, bone_above, smooth)
     blank(pair, far)
     blank(pair_z, far_m)
     clear(pair_s)
@@ -491,7 +490,7 @@
     def use(k, tile, value):
         specific[k, 8 * tile : 8 * tile + 8] = value
 
-    energy_march(pair, 0, 8, use)
+    energy_march(pair, 0, 8, use, 8)
     parts = []
     for k in range(8):
         rho = density[k]
@@ -544,10 +543,10 @@
         )
 
 
-def bone_z(count, bone, below, above, out):
+def bone_z(count, bone, below, above, _, out):
     blocks = [lambda j, ref=ref: ref[j].astype(jnp.float32) for ref in (bone, below, above)]
-    for i, value in enumerate(far_z(count, *blocks)):
-        out[i] = value
+    for i, (own, far) in enumerate(zip(own_z(blocks[0]), far_z(count, *blocks[1:]))):
+        out[i] = own + far
     out[8], out[9] = decayed([blocks[0](k) for k in range(8)])
 
 
@@ -572,7 +571,7 @@
     ladder(*decayed(block), mine[256:264] + other[256:264], planes)
 
 
-def near_z(count, planes, i):
+def near_z(count, planes):
     run = lax.axis_index("run")
     lower, upper = 0.0, 0.0
     for o in range(1, REACH // 8):
@@ -581,28 +580,33 @@
         lower = lower + jnp.where(run - o >= 0, scale * planes[at, 0:32], 0.0)
         at = jnp.minimum(run + o, count - 1)
         upper = upper + jnp.where(run + o < count, scale * planes[at, 0:32], 0.0)
-    return weight(i + 1) * lower + weight(8 - i) * upper
-
-
-def far_z(count, mine, below, above):
+    return [weight(i + 1) * lower + weight(8 - i) * upper for i in range(8)]
+
+
+def own_z(mine):
+    for i in range(8):
+        value = 0.0
+        for j in range(8):
+            value = value + weight(abs(i - j)) * mine(j)
+        yield value
+
+
+def far_z(count, below, above):
     run = lax.axis_index("run")
     has_below = run - REACH // 8 >= 0
     has_above = run + REACH // 8 < count
     for i in range(8):
-        value, far_below, far_above = 0.0, 0.0, 0.0
+        far_below, far_above = 0.0, 0.0
         for j in range(8):
-            value = value + weight(abs(i - j)) * mine(j)
             if j >= i:
                 far_below = far_below + weight(i - j + REACH) * below(j)
             if j <= i:
                 far_above = far_above + weight(j - i + REACH) * above(j)
-        yield value + jnp.where(has_below, far_below, 0.0) + jnp.where(has_above, far_above, 0.0)
-
-
-def partial_z(
-    count, mine, below, above, lines, guess, first, second, out, displacement
-):
-    blocks = [lambda j, ref=ref: ref[j] for ref in (mine, below, above)]
+        yield jnp.where(has_below, far_below, 0.0) + jnp.where(has_above, far_above, 0.0)
+
+
+def distant_z(count, below, above, lines, guess, first, second, out, displacement):
+    blocks = [lambda j, ref=ref: ref[32 * j : 32 * j + 32] for ref in (below, above)]
     for i, value in enumerate(far_z(count, *blocks)):
         out[i] = value
     own = pl.ds(pl.multiple_of(8 * lax.axis_index("sub"), 8), 32)
@@ -614,17 +618,23 @@
             )
 
 
+def distant_y(smooth, mine, other, out):
+    far = smooth_y(lambda k: mine[k], lambda k: other[k])
+    for i, (near, value) in enumerate(zip(own_z(lambda j: smooth[j]), far)):
+        out[i] = near + value
+
+
 def spread_z(count, part, planes, out):
-    for i in range(8):
-        out[i] = part[i] + near_z(count, planes, i)
+    for i, share in enumerate(near_z(count, planes)):
+        out[i] = part[i] + share
 
 
 def remodel(count, part, planes, lines, bone, density, out):
     bones = jnp.sum(lines[:, 32:40], axis=0)[0:1]
     line = jnp.sum(planes[:, 32:40], axis=0)[0:1]
     scale = jnp.broadcast_to(pick(bones, 4) / line, density.shape[1:])
-    for i in range(8):
-        value = part[i] + near_z(count, planes, i)
+    for i, share in enumerate(near_z(count, planes)):
+        value = part[i] + share
         rho = density[i]
         updated = jnp.minimum(rho * (1.0 + RATE * jnp.tanh(SLOPE * (value * scale - 1.0))), 1.0)
         out[i] = jnp.where(bone[i] == 1, updated, rho)
@@ -633,6 +643,7 @@
 def local(load, guess, occupancy, density):
     count = lax.axis_size("run")
     block = density.shape
+    depth = block[0]
     swap = [(0, 1), (1, 0)]
     side = lax.ppermute(side_rows(load, guess, occupancy, density), "sub", swap)
     inputs = [load, guess, occupancy, density, side]
@@ -647,15 +658,14 @@
     )
     low = lax.ppermute(up, "run", [(i, i + 1) for i in range(count - 1)])
     high = lax.ppermute(down, "run", [(i + 1, i) for i in range(count - 1)])
-    smooth, *kept = call(
-        functools.partial(middle, count),
+    kept = call(
+        middle,
         [
-            (10, 32, 128),
             (3, 8, ROWS, 128), (8, ROWS, 128), (7, ROWS, 128),
             (3, 6, ROWS, 128), (3, 4, ROWS, 128),
             (6, 6, ROWS, 128), (6, 6, 48, 128), (4, ROWS, 128),
         ],
-        [*inputs, *far_slabs(occupancy)],
+        inputs,
         [
             (3, 8, ROWS, 128), (6, 8, 48, 128), (6, 8, ROWS, 128), (6, 8, 48, 128),
             (6, 6, 48, 128), (6, 4, 48, 128),
@@ -671,6 +681,9 @@
             (7, ROWS, 128), (4, ROWS, 128),
         ],
     )
+    (smooth,) = call(
+        functools.partial(bone_z, count), [(10, 32, 128)], [occupancy, *far_slabs(occupancy, depth), kept[-1]]
+    )
     spread, rails = call(
         bone_y, [block, (2, 32, 128)], [smooth, lax.ppermute(smooth, "sub", swap)]
     )
@@ -686,15 +699,18 @@
         [lines, guess_w, low, first, second, occupancy, density, spread],
         [(6, 9, 48, 128), (8, ROWS, 128)],
     )
+    below, above = far_slabs(smooth, depth)
     other = lax.ppermute(smooth, "sub", swap)
     smooth, planes = call(along_y, [block, (count, 40, 128)], [smooth, other])
-    below, above = far_slabs(smooth)
     planes = lax.all_to_all(planes, "run", 0, 0, tiled=True)
-    part, displacement = call(
-        functools.partial(partial_z, count),
+    distant, displacement = call(
+        functools.partial(distant_z, count),
         [block, guess.shape],
-        [smooth, below, above, lines, guess, first, second],
+        [below, above, lines, guess, first, second],
         flops=10**10,
+    )
+    (part,) = call(
+        distant_y, [block], [smooth, distant, lax.ppermute(distant, "sub", swap)]
     )
     (new_density,) = call(
         functools.partial(remodel, count),
@@ -704,9 +720,9 @@
     return displacement, new_density
 
 
-def far_slabs(block):
+def far_slabs(block, depth):
     count = lax.axis_size("run")
-    span = REACH // block.shape[0]
+    span = REACH // depth
     rise = [(i, i + span) for i in range(count - span)]
     fall = [(i + span, i) for i in range(count - span)]
     if count <= 2 * span:

time: 53.8 us -> 52.8 us (0.981)
  waiting for transfers between devices: 11.2 us -> 10.3 us
    ppermute x2, waiting for transfers between devices: 5.79 us -> 3.32 us  [far_slabs(): both = lax.ppermute(block, 'run', rise + fall)]
    ppermute x1, waiting for transfers between devices: 0.71 us -> 2.1 us  [local(): high = lax.ppermute(down, 'run', [(i + 1, i) for i in range(count - 1)])]
    ppermute x0 -> x1, waiting for transfers between devices: none -> 1.33 us  [local(): lax.ppermute(distant, 'sub', swap)]
    ppermute x1, waiting for transfers between devices: 1.35 us -> 0.72 us  [local(): other = lax.ppermute(smooth, 'sub', swap)]
    pallas_call x10 -> x12, Pallas kernels: 11.7 us -> 12.1 us  [call(): pl.pallas_call(kernel, out_shape=[jax.ShapeDtypeStruct(s, jnp.float32) fo...]
  transfers between devices with their start and end apart: 9 -> 10, of which waited for: 7 -> 7; matrix products, arithmetic and copies ran while one was open for 0% -> 0% of each run, Pallas kernels for 16% -> 19%
where the time goes in v6:
time: 52.8 us; the launch traced here: 52.5 us
  blocking collectives  15.1 us (29%)
  starting transfers between devices  13 us (25%)
  Pallas kernels  12.1 us (23%)
  waiting for transfers between devices  10.3 us (20%)
  other arithmetic  1.16 us (2%)
  between operations  0.8 us (2%)
    all_to_all x1, blocking collectives, local(): planes = lax.all_to_all(planes, 'run', 0, 0, tiled=True)  15.1 us
    pallas_call x12, Pallas kernels, call(): pl.pallas_call(kernel, out_shape=[jax.ShapeDtypeStruct(s, jnp.float32) fo...  12.1 us
    ppermute x2, starting transfers between devices, far_slabs(): both = lax.ppermute(block, 'run', rise + fall)  4.29 us
    ppermute x1, starting transfers between devices, local(): low = lax.ppermute(up, 'run', [(i, i + 1) for i in range(count - 1)])  3.44 us
    all_to_all x1, starting transfers between devices, local(): planes = lax.all_to_all(planes, 'run', 0, 0, tiled=True)  3.38 us
    ppermute x2, waiting for transfers between devices, far_slabs(): both = lax.ppermute(block, 'run', rise + fall)  3.32 us
    ppermute x1, waiting for transfers between devices, local(): high = lax.ppermute(down, 'run', [(i + 1, i) for i in range(count - 1)])  2.1 us
    all_to_all x1, waiting for transfers between devices, local(): planes = lax.all_to_all(planes, 'run', 0, 0, tiled=True)  1.92 us
  transfers between devices with their start and end apart: 10, of which 7 were waited for; matrix products, arithmetic and copies ran while one was open for 0% of the time, Pallas kernels for 19%

profile of v6, /device:TPU:0, one launch (start us, length us, event | category | flops | bytes accessed | tf_op | source)
XLA Modules:
  0.0 52.5 jit_solution(15942737756203173011)
XLA Ops:
  0.6 0.0 copy-start
  0.6 0.0 copy-start.1
  0.7 0.0 copy-start.3
  0.7 1.1 %slice_select_fusion = (f32[3,8,8,128]{3,2,1,0:T(8,128)S(1)}, f32[3,8,8,128]{3,2,1,0:T(8,128)S(1)}) fusion(f32[3,8,32,128]{3,2,1,0:T(8,128)} %load.3, pred[]{:T(512)S(6)} %eq.12, f32[3,8,32,128]{3,2,1,0:T(8,128)} %guess.5), kind=kLoop, calls=%fused_computation.1 | loop fusion | flops 49152 | bytes 589825 | tf_op jit(solution)/shard_map/jit(_where)/select_n | solution.py:240
  1.8 0.0 copy-start.2
  1.8 0.0 copy-done
  1.8 0.0 copy-done.1
  1.9 0.5 collective-permute-start.1
  2.4 3.7 %collective-permute-start = (s32[8,32,128]{2,1,0:T(8,128)S(1)}, s32[8,32,128]{2,1,0:T(8,128)S(1)}, u32[]{:S(2)}, u32[]{:S(2)}) collective-permute-start(s32[8,32,128]{2,1,0:T(8,128)S(1)} %copy-done), channel_id=1, source_target_pairs={{0,8},{2,10},{4,12},{6,14},{8,0},{10,2},{12,4},{14,6},{1,9},{3,11}... | collective-permute-start | bytes 393224 | tf_op jit(solution)/shard_map/ppermute | solution.py:729
  6.1 0.0 collective-permute-done.1.side
  6.1 0.0 copy-done.3
  6.1 0.0 copy-done.2
  6.1 0.6 %shard_map.62 = (f32[10,40,128]{2,1,0:T(8,128)S(1)}, f32[8,40,128]{2,1,0:T(8,128)S(1)}) custom-call(f32[3,8,32,128]{3,2,1,0:T(8,128)S(1)} %copy-done.2, f32[3,8,32,128]{3,2,1,0:T(8,128)S(1)} %copy-done.3, s32[8,32,128]{2,1,0:T(8,128)S(1)} %copy-done, f32[8,32,128]{2,1,0:T(8,128)S(1)} %copy-done.1, f32[56,8,128]{2,1,0:T(8,128)S(1)} %collective-permute-done.1.side), custom_call_target="tpu_custom_call" | custom-call | tf_op jit(solution)/shard_map/pallas_call | solution.py:37
  6.7 3.4 %collective-permute-start.3 = (f32[10,40,128]{2,1,0:T(8,128)S(1)}, f32[10,40,128]{2,1,0:T(8,128)S(1)}, u32[]{:S(2)}, u32[]{:S(2)}) collective-permute-start(f32[10,40,128]{2,1,0:T(8,128)S(1)} %get-tuple-element.31.up), channel_id=1, source_target_pairs={{0,2},{2,4},{4,6},{6,8},{8,10},{10,12},{12,14},{1,3},{3,5},{5,7},{... | collective-permute-start | bytes 614408 | tf_op jit(solution)/shard_map/ppermute | solution.py:659
  10.1 1.3 %collective-permute-start.4 = (f32[8,40,128]{2,1,0:T(8,128)S(1)}, f32[8,40,128]{2,1,0:T(8,128)S(1)}, u32[]{:S(2)}, u32[]{:S(2)}) collective-permute-start(f32[8,40,128]{2,1,0:T(8,128)S(1)} %get-tuple-element.32.down), channel_id=1, source_target_pairs={{2,0},{4,2},{6,4},{8,6},{10,8},{12,10},{14,12},{3,1},{5,3},{7,5},{... | collective-permute-start | bytes 491528 | tf_op jit(solution)/shard_map/ppermute | solution.py:660
  11.4 4.1 %shard_map.59 = (f32[3,8,40,128]{3,2,1,0:T(8,128)S(1)}, f32[8,40,128]{2,1,0:T(8,128)S(1)}, f32[7,40,128]{2,1,0:T(8,128)S(1)}, f32[3,6,40,128]{3,2,1,0:T(8,128)S(...) custom-call(f32[3,8,32,128]{3,2,1,0:T(8,128)S(1)} %copy-done.2, ...), custom_call_target="tpu_custom_call" | custom-call | tf_op jit(solution)/shard_map/pallas_call | solution.py:37
  15.6 0.0 collective-permute-done.below.above
  15.6 0.2 shard_map.60.mine
  15.9 0.1 collective-permute-start.2
  15.9 2.1 %collective-permute-done.4.high = f32[8,40,128]{2,1,0:T(8,128)S(1)} collective-permute-done((f32[8,40,128]{2,1,0:T(8,128)S(1)}, f32[8,40,128]{2,1,0:T(8,128)S(1)}, u32[]{:S(2)}, u32[]{:S(2)}) %collective-permute-start.4) | collective-permute-done | bytes 163872 | tf_op jit(solution)/shard_map/ppermute | solution.py:660
  18.0 0.3 collective-permute-done.3.low
  18.3 2.0 %shard_map.63 = (f32[8,128]{1,0:T(8,128)S(1)}, f32[3,9,40,128]{3,2,1,0:T(8,128)S(1)}, f32[3,9,40,128]{3,2,1,0:T(8,128)S(1)}) custom-call(f32[10,40,128]{2,1,0:T(8,128)S(1)} %get-tuple-element.31.up, f32[8,40,128]{2,1,0:T(8,128)S(1)} %get-tuple-element.32.down, f32[3,8,40,128]{3,2,1,0:T(8,128)S(1)} %get-tuple-element.33.guess_w, ...), custom_call_target="tpu_custom_call" | custom-call | tf_op jit(solution)/shard_map/pallas_call | solution.py:37
  20.3 0.0 collective-permute-start.5
  20.3 0.0 collective-permute-done.2.other
  20.3 0.6 %shard_map.61 = (f32[8,32,128]{2,1,0:T(8,128)S(1)}, f32[2,32,128]{2,1,0:T(8,128)S(1)}) custom-call(f32[10,32,128]{2,1,0:T(8,128)S(1)} %shard_map.60.mine, f32[10,32,128]{2,1,0:T(8,128)S(1)} %collective-permute-done.2.other), custom_call_target="tpu_custom_call" | custom-call | tf_op jit(solution)/shard_map/pallas_call | solution.py:37
  20.9 0.6 %collective-permute-done.5.other = f32[8,128]{1,0:T(8,128)S(1)} collective-permute-done((f32[8,128]{1,0:T(8,128)S(1)}, f32[8,128]{1,0:T(8,128)S(1)}, u32[]{:S(2)}, u32[]{:S(2)}) %collective-permute-start.5) | collective-permute-done | bytes 4128 | tf_op jit(solution)/shard_map/ppermute | solution.py:691
  21.5 15.1 %all_to_all.10.planes.lines = f32[8,40,128]{2,1,0:T(8,128)S(1)} all-to-all(f32[8,40,128]{2,1,0:T(8,128)S(1)} %shard_map.64), channel_id=1, replica_groups=mesh['grp'=2,'run'=8,'sub'=2] {'run'}, dimensions={0} | all-to-all | bytes 327680 | tf_op jit(solution)/shard_map/all_to_all | solution.py:693
  36.6 1.2 %shard_map.66.mine = f32[264,128]{1,0:T(8,128)S(1)} custom-call(f32[8,40,128]{2,1,0:T(8,128)S(1)} %all_to_all.10.planes.lines, f32[3,8,40,128]{3,2,1,0:T(8,128)S(1)} %get-tuple-element.33.guess_w, f32[10,40,128]{2,1,0:T(8,128)S(1)} %collective-permute-done.3.low, f32[3,9,40,128]{3,2,1,0:T(8,128)S(1)} %get-tuple-element.41.first, ...), custom_call_target="tpu_custom_call" | custom-call | tf_op jit(solution)/shard_map/pallas_call | solution.py:37
  37.8 0.0 collective-permute-start.7
  37.9 0.6 %collective-permute-start.6 = (f32[264,128]{1,0:T(8,128)S(1)}, f32[264,128]{1,0:T(8,128)S(1)}, u32[]{:S(2)}, u32[]{:S(2)}) collective-permute-start(f32[264,128]{1,0:T(8,128)S(1)} %shard_map.66.mine), channel_id=1, source_target_pairs={{0,8},{2,10},{4,12},{6,14},{8,0},{10,2},{12,4},{14,6},{1,9},{3,11}... | collective-permute-start | bytes 405512 | tf_op jit(solution)/shard_map/ppermute | solution.py:729
  38.5 0.7 %collective-permute-done.7.other = f32[264,128]{1,0:T(8,128)S(1)} collective-permute-done((f32[264,128]{1,0:T(8,128)S(1)}, f32[264,128]{1,0:T(8,128)S(1)}, u32[]{:S(2)}, u32[]{:S(2)}) %collective-permute-start.7) | collective-permute-done | bytes 135200 | tf_op jit(solution)/shard_map/ppermute | solution.py:703
  39.2 1.1 %shard_map.68 = (f32[8,32,128]{2,1,0:T(8,128)S(1)}, f32[8,40,128]{2,1,0:T(8,128)}) custom-call(f32[264,128]{1,0:T(8,128)S(1)} %shard_map.66.mine, f32[264,128]{1,0:T(8,128)S(1)} %collective-permute-done.7.other), custom_call_target="tpu_custom_call" | custom-call | tf_op jit(solution)/shard_map/pallas_call | solution.py:37
  40.3 3.4 %all-to-all-start.1 = ((f32[8,40,128]{2,1,0:T(8,128)}), f32[8,40,128]{2,1,0:T(8,128)S(1)}, u32[]{:S(2)}, u32[]{:S(2)}) async-start(f32[8,40,128]{2,1,0:T(8,128)} %get-tuple-element.47), calls=%async_computation.1 | async-start | bytes 327680 | tf_op jit(solution)/shard_map/all_to_all | solution.py:705
  43.7 3.3 %collective-permute-done.6.below.above = f32[264,128]{1,0:T(8,128)S(1)} collective-permute-done((f32[264,128]{1,0:T(8,128)S(1)}, f32[264,128]{1,0:T(8,128)S(1)}, u32[]{:S(2)}, u32[]{:S(2)}) %collective-permute-start.6) | collective-permute-done | bytes 135200 | tf_op jit(solution)/shard_map/ppermute | solution.py:729
  47.0 0.9 %shard_map.67 = (f32[8,32,128]{2,1,0:T(8,128)S(1)}, f32[3,8,32,128]{3,2,1,0:T(8,128)}) custom-call(f32[264,128]{1,0:T(8,128)S(1)} %collective-permute-done.6.below.above, f32[264,128]{1,0:T(8,128)S(1)} %collective-permute-done.6.below.above, f32[8,40,128]{2,1,0:T(8,128)S(1)} %all_to_all.10.planes.lines, f32[3,8,32,128]{3,2,1,0:T(8,128)S(1)} %copy-done.3, ...), custom_call_target="tpu_custom_call" | custom-call | flops 10000000000 | bytes 1048576 | tf_op jit(solution)/shard_map/pallas_call | solution.py:37
  48.0 0.0 collective-permute-start.8
  48.0 1.3 %collective-permute-done.8.other = f32[8,32,128]{2,1,0:T(8,128)S(1)} collective-permute-done((f32[8,32,128]{2,1,0:T(8,128)S(1)}, f32[8,32,128]{2,1,0:T(8,128)S(1)}, u32[]{:S(2)}, u32[]{:S(2)}) %collective-permute-start.8) | collective-permute-done | bytes 131104 | tf_op jit(solution)/shard_map/ppermute | solution.py:713
  49.3 0.5 shard_map.69.part
  49.8 1.9 %all-to-all-done.1.planes = f32[8,40,128]{2,1,0:T(8,128)S(1)} async-done(((f32[8,40,128]{2,1,0:T(8,128)}), f32[8,40,128]{2,1,0:T(8,128)S(1)}, u32[]{:S(2)}, u32[]{:S(2)}) %all-to-all-start.1) | async-done | bytes 163872 | tf_op jit(solution)/shard_map/all_to_all | solution.py:705
  51.7 0.8 %shard_map.70 = f32[8,32,128]{2,1,0:T(8,128)} custom-call(f32[8,32,128]{2,1,0:T(8,128)S(1)} %shard_map.69.part, f32[8,40,128]{2,1,0:T(8,128)S(1)} %all-to-all-done.1.planes, f32[8,40,128]{2,1,0:T(8,128)S(1)} %all_to_all.10.planes.lines, s32[8,32,128]{2,1,0:T(8,128)S(1)} %copy-done, f32[8,32,128]{2,1,0:T(8,128)S(1)} %copy-done.1), custom_call_target="tpu_custom_call" | custom-call | tf_op jit(solution)/shard_map/pallas_call | solution.py:37
  (4 shorter events, 0.1 us)
Async XLA Ops:
  0.6 1.2 %copy-start = (s32[8,32,128]{2,1,0:T(8,128)S(1)}, s32[8,32,128]{2,1,0:T(8,128)}, u32[]{:S(2)}) copy-start(s32[8,32,128]{2,1,0:T(8,128)} %bone.9) | copy-start | bytes 393220
  0.6 1.2 %copy-start.1 = (f32[8,32,128]{2,1,0:T(8,128)S(1)}, f32[8,32,128]{2,1,0:T(8,128)}, u32[]{:S(2)}) copy-start(f32[8,32,128]{2,1,0:T(8,128)} %density.7) | copy-start | bytes 393220
  0.7 5.4 %copy-start.3 = (f32[3,8,32,128]{3,2,1,0:T(8,128)S(1)}, f32[3,8,32,128]{3,2,1,0:T(8,128)}, u32[]{:S(2)}) copy-start(f32[3,8,32,128]{3,2,1,0:T(8,128)} %guess.5) | copy-start | bytes 1179652
  1.8 4.3 %copy-start.2 = (f32[3,8,32,128]{3,2,1,0:T(8,128)S(1)}, f32[3,8,32,128]{3,2,1,0:T(8,128)}, u32[]{:S(2)}) copy-start(f32[3,8,32,128]{3,2,1,0:T(8,128)} %load.3) | copy-start | bytes 1179652
  1.9 4.2 %collective-permute-start.1 = (f32[56,8,128]{2,1,0:T(8,128)S(1)}, f32[56,8,128]{2,1,0:T(8,128)S(1)}, u32[]{:S(2)}, u32[]{:S(2)}) collective-permute-start(f32[56,8,128]{2,1,0:T(8,128)S(1)} %pad_maximum_fusion), channel_id=1, source_target_pairs={{0,1},{1,0},{2,3},{3,2},{4,5},{5,4},{6,7},{7,6},{8,9},{9,8},{10,11... | collective-permute-start | bytes 688136 | tf_op jit(solution)/shard_map/ppermute | solution.py:648
  2.4 13.2 %collective-permute-start = (s32[8,32,128]{2,1,0:T(8,128)S(1)}, s32[8,32,128]{2,1,0:T(8,128)S(1)}, u32[]{:S(2)}, u32[]{:S(2)}) collective-permute-start(s32[8,32,128]{2,1,0:T(8,128)S(1)} %copy-done), channel_id=1, source_target_pairs={{0,8},{2,10},{4,12},{6,14},{8,0},{10,2},{12,4},{14,6},{1,9},{3,11}... | collective-permute-start | bytes 393224 | tf_op jit(solution)/shard_map/ppermute | solution.py:729
  6.7 11.6 %collective-permute-start.3 = (f32[10,40,128]{2,1,0:T(8,128)S(1)}, f32[10,40,128]{2,1,0:T(8,128)S(1)}, u32[]{:S(2)}, u32[]{:S(2)}) collective-permute-start(f32[10,40,128]{2,1,0:T(8,128)S(1)} %get-tuple-element.31.up), channel_id=1, source_target_pairs={{0,2},{2,4},{4,6},{6,8},{8,10},{10,12},{12,14},{1,3},{3,5},{5,7},{... | collective-permute-start | bytes 614408 | tf_op jit(solution)/shard_map/ppermute | solution.py:659
  10.1 7.9 %collective-permute-start.4 = (f32[8,40,128]{2,1,0:T(8,128)S(1)}, f32[8,40,128]{2,1,0:T(8,128)S(1)}, u32[]{:S(2)}, u32[]{:S(2)}) collective-permute-start(f32[8,40,128]{2,1,0:T(8,128)S(1)} %get-tuple-element.32.down), channel_id=1, source_target_pairs={{2,0},{4,2},{6,4},{8,6},{10,8},{12,10},{14,12},{3,1},{5,3},{7,5},{... | collective-permute-start | bytes 491528 | tf_op jit(solution)/shard_map/ppermute | solution.py:660
  15.9 4.4 %collective-permute-start.2 = (f32[10,32,128]{2,1,0:T(8,128)S(1)}, f32[10,32,128]{2,1,0:T(8,128)S(1)}, u32[]{:S(2)}, u32[]{:S(2)}) collective-permute-start(f32[10,32,128]{2,1,0:T(8,128)S(1)} %shard_map.60.mine), channel_id=1, source_target_pairs={{0,1},{1,0},{2,3},{3,2},{4,5},{5,4},{6,7},{7,6},{8,9},{9,8},{10,11... | collective-permute-start | bytes 491528 | tf_op jit(solution)/shard_map/ppermute | solution.py:688
  20.3 1.2 %collective-permute-start.5 = (f32[8,128]{1,0:T(8,128)S(1)}, f32[8,128]{1,0:T(8,128)S(1)}, u32[]{:S(2)}, u32[]{:S(2)}) collective-permute-start(f32[8,128]{1,0:T(8,128)S(1)} %get-tuple-element.40.mine), channel_id=1, source_target_pairs={{0,1},{1,0},{2,3},{3,2},{4,5},{5,4},{6,7},{7,6},{8,9},{9,8},{10,11... | collective-permute-start | bytes 12296 | tf_op jit(solution)/shard_map/ppermute | solution.py:691
  37.8 1.4 %collective-permute-start.7 = (f32[264,128]{1,0:T(8,128)S(1)}, f32[264,128]{1,0:T(8,128)S(1)}, u32[]{:S(2)}, u32[]{:S(2)}) collective-permute-start(f32[264,128]{1,0:T(8,128)S(1)} %shard_map.66.mine), channel_id=1, source_target_pairs={{0,1},{1,0},{2,3},{3,2},{4,5},{5,4},{6,7},{7,6},{8,9},{9,8},{10,11... | collective-permute-start | bytes 405512 | tf_op jit(solution)/shard_map/ppermute | solution.py:703
  37.9 9.2 %collective-permute-start.6 = (f32[264,128]{1,0:T(8,128)S(1)}, f32[264,128]{1,0:T(8,128)S(1)}, u32[]{:S(2)}, u32[]{:S(2)}) collective-permute-start(f32[264,128]{1,0:T(8,128)S(1)} %shard_map.66.mine), channel_id=1, source_target_pairs={{0,8},{2,10},{4,12},{6,14},{8,0},{10,2},{12,4},{14,6},{1,9},{3,11}... | collective-permute-start | bytes 405512 | tf_op jit(solution)/shard_map/ppermute | solution.py:729
  40.3 11.4 %all-to-all-start.1 = ((f32[8,40,128]{2,1,0:T(8,128)}), f32[8,40,128]{2,1,0:T(8,128)S(1)}, u32[]{:S(2)}, u32[]{:S(2)}) async-start(f32[8,40,128]{2,1,0:T(8,128)} %get-tuple-element.47), calls=%async_computation.1 | async-start | bytes 327680 | tf_op jit(solution)/shard_map/all_to_all | solution.py:705
  48.0 1.3 %collective-permute-start.8 = (f32[8,32,128]{2,1,0:T(8,128)S(1)}, f32[8,32,128]{2,1,0:T(8,128)S(1)}, u32[]{:S(2)}, u32[]{:S(2)}) collective-permute-start(f32[8,32,128]{2,1,0:T(8,128)S(1)} %get-tuple-element.46.mine), channel_id=1, source_target_pairs={{0,1},{1,0},{2,3},{3,2},{4,5},{5,4},{6,7},{7,6},{8,9},{9,8},{10,11... | collective-permute-start | bytes 393224 | tf_op jit(solution)/shard_map/ppermute | solution.py:713

commit v7 on v6

--- a/solution.py
+++ b/solution.py
@@ -269,8 +269,34 @@
             far[m, k, ROWS : ROWS + 8] = jnp.zeros((8, 128), jnp.float32)
 
 
+def narrow(wide, out):
+    sub = lax.axis_index("sub")
+    own = pl.ds(pl.multiple_of(8 * sub, 8), 32)
+    planes = wide.shape[0]
+    out[planes] = jnp.zeros((32, 128), jnp.float32)
+    for k in range(planes):
+        out[k] = wide[k, own]
+        out[planes, 3 * k : 3 * k + 3] = jnp.where(sub == 0, wide[k, 32:35], wide[k, 5:8])
+
+
+def widen(sent, out):
+    sub = lax.axis_index("sub")
+    own = pl.ds(pl.multiple_of(8 * sub, 8), 32)
+    rest = pl.ds(pl.multiple_of(32 * (1 - sub), 8), 8)
+    planes = out.shape[0]
+    gap = jnp.zeros((5, 128), jnp.float32)
+    for k in range(planes):
+        rows = sent[planes, 3 * k : 3 * k + 3]
+        out[k, own] = sent[k]
+        out[k, rest] = jnp.where(
+            sub == 0,
+            jnp.concatenate([rows, gap], axis=0),
+            jnp.concatenate([gap, rows], axis=0),
+        )
+
+
 def edge(
-    load, guess, bone, density, side, up, down, guess_w, load_w, mods, pair, near, far
+    load, guess, bone, density, side, up, down, up_sent, down_sent, guess_w, load_w, mods, pair, near, far
 ):
     put_guess, put_load, put_mod = windows(
         lax.axis_index("sub"), load, guess, bone, density, side
@@ -296,6 +322,8 @@
     up[9] = mods[3]
     down[6] = mods[0]
     down[7] = inverted(mods[0], mods[1])
+    narrow(up, up_sent)
+    narrow(down, down_sent)
 
 
 def middle(
@@ -363,12 +391,14 @@
 
 
 def krylov(
-    up, down, guess_w, mod_w, inverse, inner_z, inner_s, near_m, far_m, sums_in, low, high,
-    bone, row_out, first, second, pair, near, far, mods, sums,
+    up, down, guess_w, mod_w, inverse, inner_z, inner_s, near_m, far_m, sums_in, low_sent, high_sent,
+    bone, row_out, low, first, second, pair, near, far, mods, sums, high,
 ):
     sub = lax.axis_index("sub")
     run = lax.axis_index("run")
     own = pl.ds(pl.multiple_of(8 * sub, 8), 32)
+    widen(low_sent, low)
+    widen(high_sent, high)
     blank(pair, far)
     sums[...] = sums_in[...]
     mods[0] = low[9]
@@ -543,18 +573,18 @@
         )
 
 
-def bone_z(count, bone, below, above, _, out):
+def bone_z(count, bone, below, above, _, out, rails):
     blocks = [lambda j, ref=ref: ref[j].astype(jnp.float32) for ref in (bone, below, above)]
     for i, (own, far) in enumerate(zip(own_z(blocks[0]), far_z(count, *blocks[1:]))):
         out[i] = own + far
-    out[8], out[9] = decayed([blocks[0](k) for k in range(8)])
-
-
-def bone_y(mine, other, spread, rails):
-    block = list(smooth_y(lambda k: mine[k], lambda k: other[k], 10))
-    for k in range(8):
-        spread[k] = block[k]
-    rails[0], rails[1] = block[8], block[9]
+    rails[0], rails[1] = decayed([blocks[0](k) for k in range(8)])
+
+
+def bone_y(mine, other, rails_mine, rails_other, spread, rails):
+    for k, value in enumerate(smooth_y(lambda k: mine[k], lambda k: other[k])):
+        spread[k] = value
+    for k, value in enumerate(smooth_y(lambda k: rails_mine[k], lambda k: rails_other[k], 2)):
+        rails[k] = value
 
 
 def rungs(rails, mine, other, out):
@@ -647,17 +677,17 @@
     swap = [(0, 1), (1, 0)]
     side = lax.ppermute(side_rows(load, guess, occupancy, density), "sub", swap)
     inputs = [load, guess, occupancy, density, side]
-    up, down = call(
+    up, down, up_sent, down_sent = call(
         edge,
-        [(10, ROWS, 128), (8, ROWS, 128)],
+        [(10, ROWS, 128), (8, ROWS, 128), (11, 32, 128), (9, 32, 128)],
         inputs,
         [
             (3, 5, ROWS, 128), (3, 3, ROWS, 128), (4, ROWS, 128),
             (6, 5, 48, 128), (6, 5, ROWS, 128), (6, 5, 48, 128),
         ],
     )
-    low = lax.ppermute(up, "run", [(i, i + 1) for i in range(count - 1)])
-    high = lax.ppermute(down, "run", [(i + 1, i) for i in range(count - 1)])
+    low = lax.ppermute(up_sent, "run", [(i, i + 1) for i in range(count - 1)])
+    high = lax.ppermute(down_sent, "run", [(i + 1, i) for i in range(count - 1)])
     kept = call(
         middle,
         [
@@ -672,20 +702,24 @@
         ],
     )
     guess_w = kept[0]
-    line, first, second = call(
+    line, low, first, second = call(
         krylov,
-        [(8, 128), (3, 9, ROWS, 128), (3, 9, ROWS, 128)],
+        [(8, 128), (10, ROWS, 128), (3, 9, ROWS, 128), (3, 9, ROWS, 128)],
         [up, down, *kept, low, high, occupancy],
         [
             (6, 7, 48, 128), (6, 7, ROWS, 128), (6, 7, 48, 128),
-            (7, ROWS, 128), (4, ROWS, 128),
+            (7, ROWS, 128), (4, ROWS, 128), (8, ROWS, 128),
         ],
     )
-    (smooth,) = call(
-        functools.partial(bone_z, count), [(10, 32, 128)], [occupancy, *far_slabs(occupancy, depth), kept[-1]]
+    smooth, rails = call(
+        functools.partial(bone_z, count),
+        [block, (2, 32, 128)],
+        [occupancy, *far_slabs(occupancy, depth), kept[-1]]
     )
     spread, rails = call(
-        bone_y, [block, (2, 32, 128)], [smooth, lax.ppermute(smooth, "sub", swap)]
+        bone_y,
+        [block, (2, 32, 128)],
+        [smooth, lax.ppermute(smooth, "sub", swap), rails, lax.ppermute(rails, "sub", swap)],
     )
     (planes,) = call(
         rungs, [(count, 40, 128)], [rails, line, lax.ppermute(line, "sub", swap)]

time: 52.8 us -> 51.9 us (0.983)
  waiting for transfers between devices: 10.3 us -> 9.17 us
    ppermute x2 -> x3, waiting for transfers between devices: 2.39 us -> 1.25 us  [the longest x1 1.25 us: local(): lax.ppermute(down_sent, 'run', [(i + 1, i) for i in range(count - 1)])]
    ppermute x2 -> x3, starting transfers between devices: 4.73 us -> 5.22 us  [the longest x1 3.43 us: local(): low = lax.ppermute(up_sent, 'run', [(i, i + 1) for i in range(count - 1)])]
  transfers between devices with their start and end apart: 10 -> 11, of which waited for: 7 -> 6; matrix products, arithmetic and copies ran while one was open for 0% -> 0% of each run, Pallas kernels for 19% -> 19%
where the time goes in v7:
time: 51.9 us; the launch traced here: 51.6 us
  blocking collectives  14.9 us (29%)
  starting transfers between devices  13.5 us (26%)
  Pallas kernels  12 us (23%)
  waiting for transfers between devices  9.17 us (18%)
  other arithmetic  1.16 us (2%)
  between operations  0.81 us (2%)
    all_to_all x1, blocking collectives, local(): planes = lax.all_to_all(planes, 'run', 0, 0, tiled=True)  14.9 us
    pallas_call x12, Pallas kernels, call(): pl.pallas_call(kernel, out_shape=[jax.ShapeDtypeStruct(s, jnp.float32) fo...  12 us
    ppermute x2, starting transfers between devices, far_slabs(): both = lax.ppermute(block, 'run', rise + fall)  4.29 us
    ppermute x1, starting transfers between devices, local(): low = lax.ppermute(up_sent, 'run', [(i, i + 1) for i in range(count - 1)])  3.43 us
    all_to_all x1, starting transfers between devices, local(): planes = lax.all_to_all(planes, 'run', 0, 0, tiled=True)  3.38 us
    ppermute x2, waiting for transfers between devices, far_slabs(): both = lax.ppermute(block, 'run', rise + fall)  3.33 us
    all_to_all x1, waiting for transfers between devices, local(): planes = lax.all_to_all(planes, 'run', 0, 0, tiled=True)  1.91 us
    ppermute x1, waiting for transfers between devices, local(): lax.ppermute(distant, 'sub', swap)  1.33 us
  transfers between devices with their start and end apart: 11, of which 6 were waited for; matrix products, arithmetic and copies ran while one was open for 0% of the time, Pallas kernels for 19%

profile of v7, /device:TPU:0, one launch (start us, length us, event | category | flops | bytes accessed | tf_op | source)
XLA Modules:
  0.0 51.6 jit_solution(9934585163453157119)
XLA Ops:
  0.6 0.0 copy-start
  0.6 0.0 copy-start.1
  0.7 0.0 copy-start.3
  0.7 1.1 %slice_select_fusion = (f32[3,8,8,128]{3,2,1,0:T(8,128)S(1)}, f32[3,8,8,128]{3,2,1,0:T(8,128)S(1)}) fusion(f32[3,8,32,128]{3,2,1,0:T(8,128)} %load.3, pred[]{:T(512)S(6)} %eq.12, f32[3,8,32,128]{3,2,1,0:T(8,128)} %guess.5), kind=kLoop, calls=%fused_computation.1 | loop fusion | flops 49152 | bytes 589825 | tf_op jit(solution)/shard_map/jit(_where)/select_n | solution.py:240
  1.8 0.0 copy-start.2
  1.8 0.0 copy-done
  1.8 0.0 copy-done.1
  1.9 0.5 %collective-permute-start.1 = (f32[56,8,128]{2,1,0:T(8,128)S(1)}, f32[56,8,128]{2,1,0:T(8,128)S(1)}, u32[]{:S(2)}, u32[]{:S(2)}) collective-permute-start(f32[56,8,128]{2,1,0:T(8,128)S(1)} %pad_maximum_fusion), channel_id=1, source_target_pairs={{0,1},{1,0},{2,3},{3,2},{4,5},{5,4},{6,7},{7,6},{8,9},{9,8},{10,11... | collective-permute-start | bytes 688136 | tf_op jit(solution)/shard_map/ppermute | solution.py:678
  2.4 3.7 %collective-permute-start = (s32[8,32,128]{2,1,0:T(8,128)S(1)}, s32[8,32,128]{2,1,0:T(8,128)S(1)}, u32[]{:S(2)}, u32[]{:S(2)}) collective-permute-start(s32[8,32,128]{2,1,0:T(8,128)S(1)} %copy-done), channel_id=1, source_target_pairs={{0,8},{2,10},{4,12},{6,14},{8,0},{10,2},{12,4},{14,6},{1,9},{3,11}... | collective-permute-start | bytes 393224 | tf_op jit(solution)/shard_map/ppermute | solution.py:763
  6.1 0.0 collective-permute-done.1.side
  6.1 0.0 copy-done.3
  6.1 0.0 copy-done.2
  6.1 0.6 %shard_map.62 = (f32[10,40,128]{2,1,0:T(8,128)S(1)}, f32[8,40,128]{2,1,0:T(8,128)S(1)}, f32[11,32,128]{2,1,0:T(8,128)S(1)}, f32[9,32,128]{2,1,0:T(8,128)S(1)}) custom-call(f32[3,8,32,128]{3,2,1,0:T(8,128)S(1)} %copy-done.2, f32[3,8,32,128]{3,2,1,0:T(8,128)S(1)} %copy-done.3, s32[8,32,128]{2,1,0:T(8,128)S(1)} %copy-done, f32[8,32,128]{2,1,0:T(8,128)S(1)} %copy-done.1, ...), custom_call_target="tpu_custom_call" | custom-call | tf_op jit(solution)/shard_map/pallas_call | solution.py:37
  6.7 3.4 %collective-permute-start.4 = (f32[11,32,128]{2,1,0:T(8,128)S(1)}, f32[11,32,128]{2,1,0:T(8,128)S(1)}, u32[]{:S(2)}, u32[]{:S(2)}) collective-permute-start(f32[11,32,128]{2,1,0:T(8,128)S(1)} %get-tuple-element.47), channel_id=1, source_target_pairs={{0,2},{2,4},{4,6},{6,8},{8,10},{10,12},{12,14},{1,3},{3,5},{5,7},{... | collective-permute-start | bytes 540680 | tf_op jit(solution)/shard_map/ppermute | solution.py:689
  10.1 1.3 %collective-permute-start.5 = (f32[9,32,128]{2,1,0:T(8,128)S(1)}, f32[9,32,128]{2,1,0:T(8,128)S(1)}, u32[]{:S(2)}, u32[]{:S(2)}) collective-permute-start(f32[9,32,128]{2,1,0:T(8,128)S(1)} %get-tuple-element.48), channel_id=1, source_target_pairs={{2,0},{4,2},{6,4},{8,6},{10,8},{12,10},{14,12},{3,1},{5,3},{7,5},{... | collective-permute-start | bytes 442376 | tf_op jit(solution)/shard_map/ppermute | solution.py:690
  11.4 4.1 %shard_map.59 = (f32[3,8,40,128]{3,2,1,0:T(8,128)S(1)}, f32[8,40,128]{2,1,0:T(8,128)S(1)}, f32[7,40,128]{2,1,0:T(8,128)S(1)}, f32[3,6,40,128]{3,2,1,0:T(8,128)S(...) custom-call(f32[3,8,32,128]{3,2,1,0:T(8,128)S(1)} %copy-done.2, ...), custom_call_target="tpu_custom_call" | custom-call | tf_op jit(solution)/shard_map/pallas_call | solution.py:37
  15.6 0.0 collective-permute-done.below.above
  15.6 0.2 shard_map.60
  15.9 0.1 collective-permute-start.2
  15.9 0.5 collective-permute-start.3
  16.4 1.2 %collective-permute-done.5.high_sent = f32[9,32,128]{2,1,0:T(8,128)S(1)} collective-permute-done((f32[9,32,128]{2,1,0:T(8,128)S(1)}, f32[9,32,128]{2,1,0:T(8,128)S(1)}, u32[]{:S(2)}, u32[]{:S(2)}) %collective-permute-start.5) | collective-permute-done | bytes 147488 | tf_op jit(solution)/shard_map/ppermute | solution.py:690
  17.7 0.0 collective-permute-done.4.low_sent
  17.7 1.9 %shard_map.63 = (f32[8,128]{1,0:T(8,128)S(1)}, f32[10,40,128]{2,1,0:T(8,128)S(1)}, f32[3,9,40,128]{3,2,1,0:T(8,128)S(1)}, f32[3,9,40,128]{3,2,1,0:T(8,128)S(1)}) custom-call(f32[10,40,128]{2,1,0:T(8,128)S(1)} %get-tuple-element.38.up, f32[8,40,128]{2,1,0:T(8,128)S(1)} %get-tuple-element.39.down, f32[3,8,40,128]{3,2,1,0:T(8,128)S(1)} %get-tuple-element.40.guess_w, ...), custom_call_target="tpu_custom_call" | custom-call | tf_op jit(solution)/shard_map/pallas_call | solution.py:37
  19.6 0.0 collective-permute-start.6
  19.6 0.0 collective-permute-done.3.rails_other
  19.6 0.0 collective-permute-done.2.other
  19.7 0.5 shard_map.61
  20.2 0.6 %collective-permute-done.6.other = f32[8,128]{1,0:T(8,128)S(1)} collective-permute-done((f32[8,128]{1,0:T(8,128)S(1)}, f32[8,128]{1,0:T(8,128)S(1)}, u32[]{:S(2)}, u32[]{:S(2)}) %collective-permute-start.6) | collective-permute-done | bytes 4128 | tf_op jit(solution)/shard_map/ppermute | solution.py:725
  20.8 14.9 %all_to_all.10.planes.lines = f32[8,40,128]{2,1,0:T(8,128)S(1)} all-to-all(f32[8,40,128]{2,1,0:T(8,128)S(1)} %shard_map.64), channel_id=1, replica_groups=mesh['grp'=2,'run'=8,'sub'=2] {'run'}, dimensions={0} | all-to-all | bytes 327680 | tf_op jit(solution)/shard_map/all_to_all | solution.py:727
  35.7 1.2 %shard_map.66.mine = f32[264,128]{1,0:T(8,128)S(1)} custom-call(f32[8,40,128]{2,1,0:T(8,128)S(1)} %all_to_all.10.planes.lines, f32[3,8,40,128]{3,2,1,0:T(8,128)S(1)} %get-tuple-element.40.guess_w, f32[10,40,128]{2,1,0:T(8,128)S(1)} %get-tuple-element.50.low, f32[3,9,40,128]{3,2,1,0:T(8,128)S(1)} %get-tuple-element.51.first, ...), custom_call_target="tpu_custom_call" | custom-call | tf_op jit(solution)/shard_map/pallas_call | solution.py:37
  37.0 0.0 collective-permute-start.8
  37.0 0.6 %collective-permute-start.7 = (f32[264,128]{1,0:T(8,128)S(1)}, f32[264,128]{1,0:T(8,128)S(1)}, u32[]{:S(2)}, u32[]{:S(2)}) collective-permute-start(f32[264,128]{1,0:T(8,128)S(1)} %shard_map.66.mine), channel_id=1, source_target_pairs={{0,8},{2,10},{4,12},{6,14},{8,0},{10,2},{12,4},{14,6},{1,9},{3,11}... | collective-permute-start | bytes 405512 | tf_op jit(solution)/shard_map/ppermute | solution.py:763
  37.6 0.7 %collective-permute-done.8.other = f32[264,128]{1,0:T(8,128)S(1)} collective-permute-done((f32[264,128]{1,0:T(8,128)S(1)}, f32[264,128]{1,0:T(8,128)S(1)}, u32[]{:S(2)}, u32[]{:S(2)}) %collective-permute-start.8) | collective-permute-done | bytes 135200 | tf_op jit(solution)/shard_map/ppermute | solution.py:737
  38.3 1.1 %shard_map.68 = (f32[8,32,128]{2,1,0:T(8,128)S(1)}, f32[8,40,128]{2,1,0:T(8,128)}) custom-call(f32[264,128]{1,0:T(8,128)S(1)} %shard_map.66.mine, f32[264,128]{1,0:T(8,128)S(1)} %collective-permute-done.8.other), custom_call_target="tpu_custom_call" | custom-call | tf_op jit(solution)/shard_map/pallas_call | solution.py:37
  39.4 3.4 %all-to-all-start.1 = ((f32[8,40,128]{2,1,0:T(8,128)}), f32[8,40,128]{2,1,0:T(8,128)S(1)}, u32[]{:S(2)}, u32[]{:S(2)}) async-start(f32[8,40,128]{2,1,0:T(8,128)} %get-tuple-element.57), calls=%async_computation.1 | async-start | bytes 327680 | tf_op jit(solution)/shard_map/all_to_all | solution.py:739
  42.8 3.3 %collective-permute-done.7.below.above = f32[264,128]{1,0:T(8,128)S(1)} collective-permute-done((f32[264,128]{1,0:T(8,128)S(1)}, f32[264,128]{1,0:T(8,128)S(1)}, u32[]{:S(2)}, u32[]{:S(2)}) %collective-permute-start.7) | collective-permute-done | bytes 135200 | tf_op jit(solution)/shard_map/ppermute | solution.py:763
  46.1 0.9 %shard_map.67 = (f32[8,32,128]{2,1,0:T(8,128)S(1)}, f32[3,8,32,128]{3,2,1,0:T(8,128)}) custom-call(f32[264,128]{1,0:T(8,128)S(1)} %collective-permute-done.7.below.above, f32[264,128]{1,0:T(8,128)S(1)} %collective-permute-done.7.below.above, f32[8,40,128]{2,1,0:T(8,128)S(1)} %all_to_all.10.planes.lines, f32[3,8,32,128]{3,2,1,0:T(8,128)S(1)} %copy-done.3, ...), custom_call_target="tpu_custom_call" | custom-call | flops 10000000000 | bytes 1048576 | tf_op jit(solution)/shard_map/pallas_call | solution.py:37
  47.1 0.0 collective-permute-start.9
  47.1 1.3 %collective-permute-done.9.other = f32[8,32,128]{2,1,0:T(8,128)S(1)} collective-permute-done((f32[8,32,128]{2,1,0:T(8,128)S(1)}, f32[8,32,128]{2,1,0:T(8,128)S(1)}, u32[]{:S(2)}, u32[]{:S(2)}) %collective-permute-start.9) | collective-permute-done | bytes 131104 | tf_op jit(solution)/shard_map/ppermute | solution.py:747
  48.4 0.5 shard_map.69.part
  48.9 1.9 %all-to-all-done.1.planes = f32[8,40,128]{2,1,0:T(8,128)S(1)} async-done(((f32[8,40,128]{2,1,0:T(8,128)}), f32[8,40,128]{2,1,0:T(8,128)S(1)}, u32[]{:S(2)}, u32[]{:S(2)}) %all-to-all-start.1) | async-done | bytes 163872 | tf_op jit(solution)/shard_map/all_to_all | solution.py:739
  50.8 0.8 %shard_map.70 = f32[8,32,128]{2,1,0:T(8,128)} custom-call(f32[8,32,128]{2,1,0:T(8,128)S(1)} %shard_map.69.part, f32[8,40,128]{2,1,0:T(8,128)S(1)} %all-to-all-done.1.planes, f32[8,40,128]{2,1,0:T(8,128)S(1)} %all_to_all.10.planes.lines, s32[8,32,128]{2,1,0:T(8,128)S(1)} %copy-done, f32[8,32,128]{2,1,0:T(8,128)S(1)} %copy-done.1), custom_call_target="tpu_custom_call" | custom-call | tf_op jit(solution)/shard_map/pallas_call | solution.py:37
  (4 shorter events, 0.1 us)
Async XLA Ops:
  0.6 1.2 %copy-start = (s32[8,32,128]{2,1,0:T(8,128)S(1)}, s32[8,32,128]{2,1,0:T(8,128)}, u32[]{:S(2)}) copy-start(s32[8,32,128]{2,1,0:T(8,128)} %bone.9) | copy-start | bytes 393220
  0.6 1.2 %copy-start.1 = (f32[8,32,128]{2,1,0:T(8,128)S(1)}, f32[8,32,128]{2,1,0:T(8,128)}, u32[]{:S(2)}) copy-start(f32[8,32,128]{2,1,0:T(8,128)} %density.7) | copy-start | bytes 393220
  0.7 5.4 %copy-start.3 = (f32[3,8,32,128]{3,2,1,0:T(8,128)S(1)}, f32[3,8,32,128]{3,2,1,0:T(8,128)}, u32[]{:S(2)}) copy-start(f32[3,8,32,128]{3,2,1,0:T(8,128)} %guess.5) | copy-start | bytes 1179652
  1.8 4.3 %copy-start.2 = (f32[3,8,32,128]{3,2,1,0:T(8,128)S(1)}, f32[3,8,32,128]{3,2,1,0:T(8,128)}, u32[]{:S(2)}) copy-start(f32[3,8,32,128]{3,2,1,0:T(8,128)} %load.3) | copy-start | bytes 1179652
  1.9 4.2 %collective-permute-start.1 = (f32[56,8,128]{2,1,0:T(8,128)S(1)}, f32[56,8,128]{2,1,0:T(8,128)S(1)}, u32[]{:S(2)}, u32[]{:S(2)}) collective-permute-start(f32[56,8,128]{2,1,0:T(8,128)S(1)} %pad_maximum_fusion), channel_id=1, source_target_pairs={{0,1},{1,0},{2,3},{3,2},{4,5},{5,4},{6,7},{7,6},{8,9},{9,8},{10,11... | collective-permute-start | bytes 688136 | tf_op jit(solution)/shard_map/ppermute | solution.py:678
  2.4 13.2 %collective-permute-start = (s32[8,32,128]{2,1,0:T(8,128)S(1)}, s32[8,32,128]{2,1,0:T(8,128)S(1)}, u32[]{:S(2)}, u32[]{:S(2)}) collective-permute-start(s32[8,32,128]{2,1,0:T(8,128)S(1)} %copy-done), channel_id=1, source_target_pairs={{0,8},{2,10},{4,12},{6,14},{8,0},{10,2},{12,4},{14,6},{1,9},{3,11}... | collective-permute-start | bytes 393224 | tf_op jit(solution)/shard_map/ppermute | solution.py:763
  6.7 11.0 %collective-permute-start.4 = (f32[11,32,128]{2,1,0:T(8,128)S(1)}, f32[11,32,128]{2,1,0:T(8,128)S(1)}, u32[]{:S(2)}, u32[]{:S(2)}) collective-permute-start(f32[11,32,128]{2,1,0:T(8,128)S(1)} %get-tuple-element.47), channel_id=1, source_target_pairs={{0,2},{2,4},{4,6},{6,8},{8,10},{10,12},{12,14},{1,3},{3,5},{5,7},{... | collective-permute-start | bytes 540680 | tf_op jit(solution)/shard_map/ppermute | solution.py:689
  10.1 7.5 %collective-permute-start.5 = (f32[9,32,128]{2,1,0:T(8,128)S(1)}, f32[9,32,128]{2,1,0:T(8,128)S(1)}, u32[]{:S(2)}, u32[]{:S(2)}) collective-permute-start(f32[9,32,128]{2,1,0:T(8,128)S(1)} %get-tuple-element.48), channel_id=1, source_target_pairs={{2,0},{4,2},{6,4},{8,6},{10,8},{12,10},{14,12},{3,1},{5,3},{7,5},{... | collective-permute-start | bytes 442376 | tf_op jit(solution)/shard_map/ppermute | solution.py:690
  15.9 3.8 %collective-permute-start.2 = (f32[8,32,128]{2,1,0:T(8,128)S(1)}, f32[8,32,128]{2,1,0:T(8,128)S(1)}, u32[]{:S(2)}, u32[]{:S(2)}) collective-permute-start(f32[8,32,128]{2,1,0:T(8,128)S(1)} %get-tuple-element.35.mine), channel_id=1, source_target_pairs={{0,1},{1,0},{2,3},{3,2},{4,5},{5,4},{6,7},{7,6},{8,9},{9,8},{10,11... | collective-permute-start | bytes 393224 | tf_op jit(solution)/shard_map/ppermute | solution.py:722
  15.9 3.7 %collective-permute-start.3 = (f32[2,32,128]{2,1,0:T(8,128)S(1)}, f32[2,32,128]{2,1,0:T(8,128)S(1)}, u32[]{:S(2)}, u32[]{:S(2)}) collective-permute-start(f32[2,32,128]{2,1,0:T(8,128)S(1)} %get-tuple-element.36.rails_mine), channel_id=1, source_target_pairs={{0,1},{1,0},{2,3},{3,2},{4,5},{5,4},{6,7},{7,6},{8,9},{9,8},{10,11... | collective-permute-start | bytes 98312 | tf_op jit(solution)/shard_map/ppermute | solution.py:722
  19.6 1.2 %collective-permute-start.6 = (f32[8,128]{1,0:T(8,128)S(1)}, f32[8,128]{1,0:T(8,128)S(1)}, u32[]{:S(2)}, u32[]{:S(2)}) collective-permute-start(f32[8,128]{1,0:T(8,128)S(1)} %get-tuple-element.49.mine), channel_id=1, source_target_pairs={{0,1},{1,0},{2,3},{3,2},{4,5},{5,4},{6,7},{7,6},{8,9},{9,8},{10,11... | collective-permute-start | bytes 12296 | tf_op jit(solution)/shard_map/ppermute | solution.py:725
  37.0 1.4 %collective-permute-start.8 = (f32[264,128]{1,0:T(8,128)S(1)}, f32[264,128]{1,0:T(8,128)S(1)}, u32[]{:S(2)}, u32[]{:S(2)}) collective-permute-start(f32[264,128]{1,0:T(8,128)S(1)} %shard_map.66.mine), channel_id=1, source_target_pairs={{0,1},{1,0},{2,3},{3,2},{4,5},{5,4},{6,7},{7,6},{8,9},{9,8},{10,11... | collective-permute-start | bytes 405512 | tf_op jit(solution)/shard_map/ppermute | solution.py:737
  37.0 9.2 %collective-permute-start.7 = (f32[264,128]{1,0:T(8,128)S(1)}, f32[264,128]{1,0:T(8,128)S(1)}, u32[]{:S(2)}, u32[]{:S(2)}) collective-permute-start(f32[264,128]{1,0:T(8,128)S(1)} %shard_map.66.mine), channel_id=1, source_target_pairs={{0,8},{2,10},{4,12},{6,14},{8,0},{10,2},{12,4},{14,6},{1,9},{3,11}... | collective-permute-start | bytes 405512 | tf_op jit(solution)/shard_map/ppermute | solution.py:763
  39.4 11.4 %all-to-all-start.1 = ((f32[8,40,128]{2,1,0:T(8,128)}), f32[8,40,128]{2,1,0:T(8,128)S(1)}, u32[]{:S(2)}, u32[]{:S(2)}) async-start(f32[8,40,128]{2,1,0:T(8,128)} %get-tuple-element.57), calls=%async_computation.1 | async-start | bytes 327680 | tf_op jit(solution)/shard_map/all_to_all | solution.py:739
  47.1 1.3 %collective-permute-start.9 = (f32[8,32,128]{2,1,0:T(8,128)S(1)}, f32[8,32,128]{2,1,0:T(8,128)S(1)}, u32[]{:S(2)}, u32[]{:S(2)}) collective-permute-start(f32[8,32,128]{2,1,0:T(8,128)S(1)} %get-tuple-element.56.mine), channel_id=1, source_target_pairs={{0,1},{1,0},{2,3},{3,2},{4,5},{5,4},{6,7},{7,6},{8,9},{9,8},{10,11... | collective-permute-start | bytes 393224 | tf_op jit(solution)/shard_map/ppermute | solution.py:747

commit v8 on v7

--- a/solution.py
+++ b/solution.py
@@ -591,14 +591,10 @@
     ladder(rails[0], rails[1], mine[...] + other[...], out)
 
 
-def along_y(mine, other, out, planes):
-    def at(ref):
-        return lambda k: ref[32 * k : 32 * k + 32]
-
-    block = list(smooth_y(at(mine), at(other)))
-    for k in range(8):
-        out[k] = block[k]
-    ladder(*decayed(block), mine[256:264] + other[256:264], planes)
+def along_y(mine, other, planes):
+    sums = [decayed([ref[32 * k : 32 * k + 32] for k in range(8)]) for ref in (mine, other)]
+    upward, downward = smooth_y(lambda k: sums[0][k], lambda k: sums[1][k], 2)
+    ladder(upward, downward, mine[256:264] + other[256:264], planes)
 
 
 def near_z(count, planes):
@@ -635,10 +631,10 @@
         yield jnp.where(has_below, far_below, 0.0) + jnp.where(has_above, far_above, 0.0)
 
 
-def distant_z(count, below, above, lines, guess, first, second, out, displacement):
-    blocks = [lambda j, ref=ref: ref[32 * j : 32 * j + 32] for ref in (below, above)]
-    for i, value in enumerate(far_z(count, *blocks)):
-        out[i] = value
+def distant_z(count, mine, below, above, lines, guess, first, second, out, displacement):
+    blocks = [lambda j, ref=ref: ref[32 * j : 32 * j + 32] for ref in (mine, below, above)]
+    for i, (near, far) in enumerate(zip(own_z(blocks[0]), far_z(count, *blocks[1:]))):
+        out[i] = near + far
     own = pl.ds(pl.multiple_of(8 * lax.axis_index("sub"), 8), 32)
     p, q = (jnp.broadcast_to(step, (32, 128)) for step in steplengths(lines))
     for c in range(3):
@@ -648,10 +644,9 @@
             )
 
 
-def distant_y(smooth, mine, other, out):
-    far = smooth_y(lambda k: mine[k], lambda k: other[k])
-    for i, (near, value) in enumerate(zip(own_z(lambda j: smooth[j]), far)):
-        out[i] = near + value
+def distant_y(mine, other, out):
+    for k, value in enumerate(smooth_y(lambda k: mine[k], lambda k: other[k])):
+        out[k] = value
 
 
 def spread_z(count, part, planes, out):
@@ -735,16 +730,16 @@
     )
     below, above = far_slabs(smooth, depth)
     other = lax.ppermute(smooth, "sub", swap)
-    smooth, planes = call(along_y, [block, (count, 40, 128)], [smooth, other])
+    (planes,) = call(along_y, [(count, 40, 128)], [smooth, other])
     planes = lax.all_to_all(planes, "run", 0, 0, tiled=True)
     distant, displacement = call(
         functools.partial(distant_z, count),
         [block, guess.shape],
-        [below, above, lines, guess, first, second],
+        [smooth, below, above, lines, guess, first, second],
         flops=10**10,
     )
     (part,) = call(
-        distant_y, [block], [smooth, distant, lax.ppermute(distant, "sub", swap)]
+        distant_y, [block], [distant, lax.ppermute(distant, "sub", swap)]
     )
     (new_density,) = call(
         functools.partial(remodel, count),

time: 51.9 us -> 51.7 us (level)
  no operation moved by 1% of the time
where the time goes in v8:
time: 51.7 us; the launch traced here: 51.4 us
  blocking collectives  14.9 us (29%)
  starting transfers between devices  13.5 us (26%)
  Pallas kernels  11.9 us (23%)
  waiting for transfers between devices  9.15 us (18%)
  other arithmetic  1.16 us (2%)
  between operations  0.81 us (2%)
    all_to_all x1, blocking collectives, local(): planes = lax.all_to_all(planes, 'run', 0, 0, tiled=True)  14.9 us
    pallas_call x12, Pallas kernels, call(): pl.pallas_call(kernel, out_shape=[jax.ShapeDtypeStruct(s, jnp.float32) fo...  11.9 us
    ppermute x2, starting transfers between devices, far_slabs(): both = lax.ppermute(block, 'run', rise + fall)  4.29 us
    ppermute x2, waiting for transfers between devices, far_slabs(): both = lax.ppermute(block, 'run', rise + fall)  3.55 us
    ppermute x1, starting transfers between devices, local(): low = lax.ppermute(up_sent, 'run', [(i, i + 1) for i in range(count - 1)])  3.43 us
    all_to_all x1, starting transfers between devices, local(): planes = lax.all_to_all(planes, 'run', 0, 0, tiled=True)  3.38 us
    all_to_all x1, waiting for transfers between devices, local(): planes = lax.all_to_all(planes, 'run', 0, 0, tiled=True)  1.65 us
    ppermute x1, waiting for transfers between devices, local(): lax.ppermute(distant, 'sub', swap)  1.35 us
  transfers between devices with their start and end apart: 11, of which 6 were waited for; matrix products, arithmetic and copies ran while one was open for 0% of the time, Pallas kernels for 19%

profile of v8, /device:TPU:0, one launch (start us, length us, event | category | flops | bytes accessed | tf_op | source)
XLA Modules:
  0.0 51.4 jit_solution(3470184973566648477)
XLA Ops:
  0.6 0.0 copy-start
  0.6 0.0 copy-start.1
  0.7 0.0 copy-start.3
  0.7 1.1 %slice_select_fusion = (f32[3,8,8,128]{3,2,1,0:T(8,128)S(1)}, f32[3,8,8,128]{3,2,1,0:T(8,128)S(1)}) fusion(f32[3,8,32,128]{3,2,1,0:T(8,128)} %load.3, pred[]{:T(512)S(6)} %eq.12, f32[3,8,32,128]{3,2,1,0:T(8,128)} %guess.5), kind=kLoop, calls=%fused_computation.1 | loop fusion | flops 49152 | bytes 589825 | tf_op jit(solution)/shard_map/jit(_where)/select_n | solution.py:240
  1.8 0.0 copy-start.2
  1.8 0.0 copy-done
  1.8 0.0 copy-done.1
  1.9 0.5 %collective-permute-start.1 = (f32[56,8,128]{2,1,0:T(8,128)S(1)}, f32[56,8,128]{2,1,0:T(8,128)S(1)}, u32[]{:S(2)}, u32[]{:S(2)}) collective-permute-start(f32[56,8,128]{2,1,0:T(8,128)S(1)} %pad_maximum_fusion), channel_id=1, source_target_pairs={{0,1},{1,0},{2,3},{3,2},{4,5},{5,4},{6,7},{7,6},{8,9},{9,8},{10,11... | collective-permute-start | bytes 688136 | tf_op jit(solution)/shard_map/ppermute | solution.py:673
  2.4 3.7 %collective-permute-start = (s32[8,32,128]{2,1,0:T(8,128)S(1)}, s32[8,32,128]{2,1,0:T(8,128)S(1)}, u32[]{:S(2)}, u32[]{:S(2)}) collective-permute-start(s32[8,32,128]{2,1,0:T(8,128)S(1)} %copy-done), channel_id=1, source_target_pairs={{0,8},{2,10},{4,12},{6,14},{8,0},{10,2},{12,4},{14,6},{1,9},{3,11}... | collective-permute-start | bytes 393224 | tf_op jit(solution)/shard_map/ppermute | solution.py:758
  6.1 0.0 collective-permute-done.1.side
  6.1 0.0 copy-done.3
  6.1 0.0 copy-done.2
  6.1 0.6 %shard_map.62 = (f32[10,40,128]{2,1,0:T(8,128)S(1)}, f32[8,40,128]{2,1,0:T(8,128)S(1)}, f32[11,32,128]{2,1,0:T(8,128)S(1)}, f32[9,32,128]{2,1,0:T(8,128)S(1)}) custom-call(f32[3,8,32,128]{3,2,1,0:T(8,128)S(1)} %copy-done.2, f32[3,8,32,128]{3,2,1,0:T(8,128)S(1)} %copy-done.3, s32[8,32,128]{2,1,0:T(8,128)S(1)} %copy-done, f32[8,32,128]{2,1,0:T(8,128)S(1)} %copy-done.1, ...), custom_call_target="tpu_custom_call" | custom-call | tf_op jit(solution)/shard_map/pallas_call | solution.py:37
  6.7 3.4 %collective-permute-start.4 = (f32[11,32,128]{2,1,0:T(8,128)S(1)}, f32[11,32,128]{2,1,0:T(8,128)S(1)}, u32[]{:S(2)}, u32[]{:S(2)}) collective-permute-start(f32[11,32,128]{2,1,0:T(8,128)S(1)} %get-tuple-element.45), channel_id=1, source_target_pairs={{0,2},{2,4},{4,6},{6,8},{8,10},{10,12},{12,14},{1,3},{3,5},{5,7},{... | collective-permute-start | bytes 540680 | tf_op jit(solution)/shard_map/ppermute | solution.py:684
  10.1 1.3 %collective-permute-start.5 = (f32[9,32,128]{2,1,0:T(8,128)S(1)}, f32[9,32,128]{2,1,0:T(8,128)S(1)}, u32[]{:S(2)}, u32[]{:S(2)}) collective-permute-start(f32[9,32,128]{2,1,0:T(8,128)S(1)} %get-tuple-element.46), channel_id=1, source_target_pairs={{2,0},{4,2},{6,4},{8,6},{10,8},{12,10},{14,12},{3,1},{5,3},{7,5},{... | collective-permute-start | bytes 442376 | tf_op jit(solution)/shard_map/ppermute | solution.py:685
  11.4 4.1 %shard_map.59 = (f32[3,8,40,128]{3,2,1,0:T(8,128)S(1)}, f32[8,40,128]{2,1,0:T(8,128)S(1)}, f32[7,40,128]{2,1,0:T(8,128)S(1)}, f32[3,6,40,128]{3,2,1,0:T(8,128)S(...) custom-call(f32[3,8,32,128]{3,2,1,0:T(8,128)S(1)} %copy-done.2, ...), custom_call_target="tpu_custom_call" | custom-call | tf_op jit(solution)/shard_map/pallas_call | solution.py:37
  15.6 0.0 collective-permute-done.below.above
  15.6 0.2 shard_map.60
  15.9 0.1 collective-permute-start.2
  15.9 0.5 collective-permute-start.3
  16.4 1.2 %collective-permute-done.5.high_sent = f32[9,32,128]{2,1,0:T(8,128)S(1)} collective-permute-done((f32[9,32,128]{2,1,0:T(8,128)S(1)}, f32[9,32,128]{2,1,0:T(8,128)S(1)}, u32[]{:S(2)}, u32[]{:S(2)}) %collective-permute-start.5) | collective-permute-done | bytes 147488 | tf_op jit(solution)/shard_map/ppermute | solution.py:685
  17.7 0.0 collective-permute-done.4.low_sent
  17.7 1.9 %shard_map.63 = (f32[8,128]{1,0:T(8,128)S(1)}, f32[10,40,128]{2,1,0:T(8,128)S(1)}, f32[3,9,40,128]{3,2,1,0:T(8,128)S(1)}, f32[3,9,40,128]{3,2,1,0:T(8,128)S(1)}) custom-call(f32[10,40,128]{2,1,0:T(8,128)S(1)} %get-tuple-element.36.up, f32[8,40,128]{2,1,0:T(8,128)S(1)} %get-tuple-element.37.down, f32[3,8,40,128]{3,2,1,0:T(8,128)S(1)} %get-tuple-element.38.guess_w, ...), custom_call_target="tpu_custom_call" | custom-call | tf_op jit(solution)/shard_map/pallas_call | solution.py:37
  19.6 0.0 collective-permute-start.6
  19.6 0.0 collective-permute-done.3.rails_other
  19.6 0.0 collective-permute-done.2.other
  19.7 0.5 shard_map.61
  20.2 0.6 %collective-permute-done.6.other = f32[8,128]{1,0:T(8,128)S(1)} collective-permute-done((f32[8,128]{1,0:T(8,128)S(1)}, f32[8,128]{1,0:T(8,128)S(1)}, u32[]{:S(2)}, u32[]{:S(2)}) %collective-permute-start.6) | collective-permute-done | bytes 4128 | tf_op jit(solution)/shard_map/ppermute | solution.py:720
  20.8 14.9 %all_to_all.10.planes.lines = f32[8,40,128]{2,1,0:T(8,128)S(1)} all-to-all(f32[8,40,128]{2,1,0:T(8,128)S(1)} %shard_map.64), channel_id=1, replica_groups=mesh['grp'=2,'run'=8,'sub'=2] {'run'}, dimensions={0} | all-to-all | bytes 327680 | tf_op jit(solution)/shard_map/all_to_all | solution.py:722
  35.7 1.2 %shard_map.66.mine = f32[264,128]{1,0:T(8,128)S(1)} custom-call(f32[8,40,128]{2,1,0:T(8,128)S(1)} %all_to_all.10.planes.lines, f32[3,8,40,128]{3,2,1,0:T(8,128)S(1)} %get-tuple-element.38.guess_w, f32[10,40,128]{2,1,0:T(8,128)S(1)} %get-tuple-element.48.low, f32[3,9,40,128]{3,2,1,0:T(8,128)S(1)} %get-tuple-element.49.first, ...), custom_call_target="tpu_custom_call" | custom-call | tf_op jit(solution)/shard_map/pallas_call | solution.py:37
  37.0 0.0 collective-permute-start.9
  37.0 0.6 %collective-permute-start.7 = (f32[264,128]{1,0:T(8,128)S(1)}, f32[264,128]{1,0:T(8,128)S(1)}, u32[]{:S(2)}, u32[]{:S(2)}) collective-permute-start(f32[264,128]{1,0:T(8,128)S(1)} %shard_map.66.mine), channel_id=1, source_target_pairs={{0,8},{2,10},{4,12},{6,14},{8,0},{10,2},{12,4},{14,6},{1,9},{3,11}... | collective-permute-start | bytes 405512 | tf_op jit(solution)/shard_map/ppermute | solution.py:758
  37.6 0.7 %collective-permute-done.9.other = f32[264,128]{1,0:T(8,128)S(1)} collective-permute-done((f32[264,128]{1,0:T(8,128)S(1)}, f32[264,128]{1,0:T(8,128)S(1)}, u32[]{:S(2)}, u32[]{:S(2)}) %collective-permute-start.9) | collective-permute-done | bytes 135200 | tf_op jit(solution)/shard_map/ppermute | solution.py:732
  38.3 0.9 %shard_map.69 = f32[8,40,128]{2,1,0:T(8,128)} custom-call(f32[264,128]{1,0:T(8,128)S(1)} %shard_map.66.mine, f32[264,128]{1,0:T(8,128)S(1)} %collective-permute-done.9.other), custom_call_target="tpu_custom_call" | custom-call | tf_op jit(solution)/shard_map/pallas_call | solution.py:37
  39.2 3.4 %all-to-all-start.1 = ((f32[8,40,128]{2,1,0:T(8,128)}), f32[8,40,128]{2,1,0:T(8,128)S(1)}, u32[]{:S(2)}, u32[]{:S(2)}) async-start(f32[8,40,128]{2,1,0:T(8,128)} %shard_map.69), calls=%async_computation.1 | async-start | bytes 327680 | tf_op jit(solution)/shard_map/all_to_all | solution.py:734
  42.6 3.6 %collective-permute-done.7.below.above = f32[264,128]{1,0:T(8,128)S(1)} collective-permute-done((f32[264,128]{1,0:T(8,128)S(1)}, f32[264,128]{1,0:T(8,128)S(1)}, u32[]{:S(2)}, u32[]{:S(2)}) %collective-permute-start.7) | collective-permute-done | bytes 135200 | tf_op jit(solution)/shard_map/ppermute | solution.py:758
  46.2 1.0 %shard_map.67 = (f32[8,32,128]{2,1,0:T(8,128)S(1)}, f32[3,8,32,128]{3,2,1,0:T(8,128)}) custom-call(f32[264,128]{1,0:T(8,128)S(1)} %shard_map.66.mine, f32[264,128]{1,0:T(8,128)S(1)} %collective-permute-done.7.below.above, f32[264,128]{1,0:T(8,128)S(1)} %collective-permute-done.7.below.above, f32[8,40,128]{2,1,0:T(8,128)S(1)} %all_to_all.10.planes.lines, ...), custom_call_target="tpu_custom_call" | custom-call | flops 10000000000 | bytes 1048576 | tf_op jit(solution)/shard_map/pallas_call | solution.py:37
  47.2 0.0 collective-permute-start.8
  47.2 1.3 %collective-permute-done.8.other = f32[8,32,128]{2,1,0:T(8,128)S(1)} collective-permute-done((f32[8,32,128]{2,1,0:T(8,128)S(1)}, f32[8,32,128]{2,1,0:T(8,128)S(1)}, u32[]{:S(2)}, u32[]{:S(2)}) %collective-permute-start.8) | collective-permute-done | bytes 131104 | tf_op jit(solution)/shard_map/ppermute | solution.py:742
  48.5 0.4 shard_map.68.part
  49.0 1.6 %all-to-all-done.1.planes = f32[8,40,128]{2,1,0:T(8,128)S(1)} async-done(((f32[8,40,128]{2,1,0:T(8,128)}), f32[8,40,128]{2,1,0:T(8,128)S(1)}, u32[]{:S(2)}, u32[]{:S(2)}) %all-to-all-start.1) | async-done | bytes 163872 | tf_op jit(solution)/shard_map/all_to_all | solution.py:734
  50.6 0.8 %shard_map.70 = f32[8,32,128]{2,1,0:T(8,128)} custom-call(f32[8,32,128]{2,1,0:T(8,128)S(1)} %shard_map.68.part, f32[8,40,128]{2,1,0:T(8,128)S(1)} %all-to-all-done.1.planes, f32[8,40,128]{2,1,0:T(8,128)S(1)} %all_to_all.10.planes.lines, s32[8,32,128]{2,1,0:T(8,128)S(1)} %copy-done, f32[8,32,128]{2,1,0:T(8,128)S(1)} %copy-done.1), custom_call_target="tpu_custom_call" | custom-call | tf_op jit(solution)/shard_map/pallas_call | solution.py:37
  (4 shorter events, 0.1 us)
Async XLA Ops:
  0.6 1.2 %copy-start = (s32[8,32,128]{2,1,0:T(8,128)S(1)}, s32[8,32,128]{2,1,0:T(8,128)}, u32[]{:S(2)}) copy-start(s32[8,32,128]{2,1,0:T(8,128)} %bone.9) | copy-start | bytes 393220
  0.6 1.2 %copy-start.1 = (f32[8,32,128]{2,1,0:T(8,128)S(1)}, f32[8,32,128]{2,1,0:T(8,128)}, u32[]{:S(2)}) copy-start(f32[8,32,128]{2,1,0:T(8,128)} %density.7) | copy-start | bytes 393220
  0.7 5.4 %copy-start.3 = (f32[3,8,32,128]{3,2,1,0:T(8,128)S(1)}, f32[3,8,32,128]{3,2,1,0:T(8,128)}, u32[]{:S(2)}) copy-start(f32[3,8,32,128]{3,2,1,0:T(8,128)} %guess.5) | copy-start | bytes 1179652
  1.8 4.3 %copy-start.2 = (f32[3,8,32,128]{3,2,1,0:T(8,128)S(1)}, f32[3,8,32,128]{3,2,1,0:T(8,128)}, u32[]{:S(2)}) copy-start(f32[3,8,32,128]{3,2,1,0:T(8,128)} %load.3) | copy-start | bytes 1179652
  1.9 4.2 %collective-permute-start.1 = (f32[56,8,128]{2,1,0:T(8,128)S(1)}, f32[56,8,128]{2,1,0:T(8,128)S(1)}, u32[]{:S(2)}, u32[]{:S(2)}) collective-permute-start(f32[56,8,128]{2,1,0:T(8,128)S(1)} %pad_maximum_fusion), channel_id=1, source_target_pairs={{0,1},{1,0},{2,3},{3,2},{4,5},{5,4},{6,7},{7,6},{8,9},{9,8},{10,11... | collective-permute-start | bytes 688136 | tf_op jit(solution)/shard_map/ppermute | solution.py:673
  2.4 13.2 %collective-permute-start = (s32[8,32,128]{2,1,0:T(8,128)S(1)}, s32[8,32,128]{2,1,0:T(8,128)S(1)}, u32[]{:S(2)}, u32[]{:S(2)}) collective-permute-start(s32[8,32,128]{2,1,0:T(8,128)S(1)} %copy-done), channel_id=1, source_target_pairs={{0,8},{2,10},{4,12},{6,14},{8,0},{10,2},{12,4},{14,6},{1,9},{3,11}... | collective-permute-start | bytes 393224 | tf_op jit(solution)/shard_map/ppermute | solution.py:758
  6.7 11.0 %collective-permute-start.4 = (f32[11,32,128]{2,1,0:T(8,128)S(1)}, f32[11,32,128]{2,1,0:T(8,128)S(1)}, u32[]{:S(2)}, u32[]{:S(2)}) collective-permute-start(f32[11,32,128]{2,1,0:T(8,128)S(1)} %get-tuple-element.45), channel_id=1, source_target_pairs={{0,2},{2,4},{4,6},{6,8},{8,10},{10,12},{12,14},{1,3},{3,5},{5,7},{... | collective-permute-start | bytes 540680 | tf_op jit(solution)/shard_map/ppermute | solution.py:684
  10.1 7.5 %collective-permute-start.5 = (f32[9,32,128]{2,1,0:T(8,128)S(1)}, f32[9,32,128]{2,1,0:T(8,128)S(1)}, u32[]{:S(2)}, u32[]{:S(2)}) collective-permute-start(f32[9,32,128]{2,1,0:T(8,128)S(1)} %get-tuple-element.46), channel_id=1, source_target_pairs={{2,0},{4,2},{6,4},{8,6},{10,8},{12,10},{14,12},{3,1},{5,3},{7,5},{... | collective-permute-start | bytes 442376 | tf_op jit(solution)/shard_map/ppermute | solution.py:685
  15.9 3.8 %collective-permute-start.2 = (f32[8,32,128]{2,1,0:T(8,128)S(1)}, f32[8,32,128]{2,1,0:T(8,128)S(1)}, u32[]{:S(2)}, u32[]{:S(2)}) collective-permute-start(f32[8,32,128]{2,1,0:T(8,128)S(1)} %get-tuple-element.33.mine), channel_id=1, source_target_pairs={{0,1},{1,0},{2,3},{3,2},{4,5},{5,4},{6,7},{7,6},{8,9},{9,8},{10,11... | collective-permute-start | bytes 393224 | tf_op jit(solution)/shard_map/ppermute | solution.py:717
  15.9 3.7 %collective-permute-start.3 = (f32[2,32,128]{2,1,0:T(8,128)S(1)}, f32[2,32,128]{2,1,0:T(8,128)S(1)}, u32[]{:S(2)}, u32[]{:S(2)}) collective-permute-start(f32[2,32,128]{2,1,0:T(8,128)S(1)} %get-tuple-element.34.rails_mine), channel_id=1, source_target_pairs={{0,1},{1,0},{2,3},{3,2},{4,5},{5,4},{6,7},{7,6},{8,9},{9,8},{10,11... | collective-permute-start | bytes 98312 | tf_op jit(solution)/shard_map/ppermute | solution.py:717
  19.6 1.2 %collective-permute-start.6 = (f32[8,128]{1,0:T(8,128)S(1)}, f32[8,128]{1,0:T(8,128)S(1)}, u32[]{:S(2)}, u32[]{:S(2)}) collective-permute-start(f32[8,128]{1,0:T(8,128)S(1)} %get-tuple-element.47.mine), channel_id=1, source_target_pairs={{0,1},{1,0},{2,3},{3,2},{4,5},{5,4},{6,7},{7,6},{8,9},{9,8},{10,11... | collective-permute-start | bytes 12296 | tf_op jit(solution)/shard_map/ppermute | solution.py:720
  37.0 1.4 %collective-permute-start.9 = (f32[264,128]{1,0:T(8,128)S(1)}, f32[264,128]{1,0:T(8,128)S(1)}, u32[]{:S(2)}, u32[]{:S(2)}) collective-permute-start(f32[264,128]{1,0:T(8,128)S(1)} %shard_map.66.mine), channel_id=1, source_target_pairs={{0,1},{1,0},{2,3},{3,2},{4,5},{5,4},{6,7},{7,6},{8,9},{9,8},{10,11... | collective-permute-start | bytes 405512 | tf_op jit(solution)/shard_map/ppermute | solution.py:732
  37.0 9.2 %collective-permute-start.7 = (f32[264,128]{1,0:T(8,128)S(1)}, f32[264,128]{1,0:T(8,128)S(1)}, u32[]{:S(2)}, u32[]{:S(2)}) collective-permute-start(f32[264,128]{1,0:T(8,128)S(1)} %shard_map.66.mine), channel_id=1, source_target_pairs={{0,8},{2,10},{4,12},{6,14},{8,0},{10,2},{12,4},{14,6},{1,9},{3,11}... | collective-permute-start | bytes 405512 | tf_op jit(solution)/shard_map/ppermute | solution.py:758
  39.2 11.4 %all-to-all-start.1 = ((f32[8,40,128]{2,1,0:T(8,128)}), f32[8,40,128]{2,1,0:T(8,128)S(1)}, u32[]{:S(2)}, u32[]{:S(2)}) async-start(f32[8,40,128]{2,1,0:T(8,128)} %shard_map.69), calls=%async_computation.1 | async-start | bytes 327680 | tf_op jit(solution)/shard_map/all_to_all | solution.py:734
  47.2 1.3 %collective-permute-start.8 = (f32[8,32,128]{2,1,0:T(8,128)S(1)}, f32[8,32,128]{2,1,0:T(8,128)S(1)}, u32[]{:S(2)}, u32[]{:S(2)}) collective-permute-start(f32[8,32,128]{2,1,0:T(8,128)S(1)} %get-tuple-element.53.mine), channel_id=1, source_target_pairs={{0,1},{1,0},{2,3},{3,2},{4,5},{5,4},{6,7},{7,6},{8,9},{9,8},{10,11... | collective-permute-start | bytes 393224 | tf_op jit(solution)/shard_map/ppermute | solution.py:742
